TPU v7x, 256 devices: a whole 4x4x8 slice. The times are simulated.
256 devices in a mesh: row: 16 (over x, z_hi), col: 16 (over z_lo, y, core).
Axes of the slice: x: 4, y: 4, z: 8 (z_hi: 4, z_lo: 2; z = z_hi * 2 + z_lo), core: 2. Of those that a mesh axis runs over, the one named last changes fastest.
Arguments:
- inputs: bfloat16 [2048, 8192], P('col', 'row'), may hold values from -6 to 6
- preact: bfloat16 [2048, 32768], P('row', 'col'), may hold values from -8 to 8
- out_grad: bfloat16 [2048, 32768], P('row', 'col'), may hold values from -0.796875 to 0.796875
- weight: bfloat16 [8192, 32768], P('row', 'col'), may hold values from -0.0625 to 0.0625
Outputs:
- input_grad: bfloat16 [2048, 8192], P('col', 'row')
- weight_grad: bfloat16 [8192, 32768], P('row', 'col')
All inputs are finite; a program needn't handle non-finite values.
Results may differ from a plain program's by a relative error of at most 0.0049.
Values may be sent and summed in bfloat16 or wider, within the bound.
No kernel may reach another device: no remote copies, remote signals or barrier semaphores. Data moves between devices by JAX's collectives and lax.ppermute only.
A program may use at most 64 MiB of HBM per device.

v0:
```python
import math

import jax
import jax.numpy as jnp
from jax import lax
from jax.sharding import PartitionSpec as P


def gelu_slope(preact):
    h = preact.astype(jnp.float32)
    scale_c = math.sqrt(2.0 / math.pi)
    t = jnp.tanh(scale_c * (h + 0.044715 * h * h * h))
    return 0.5 * (1.0 + t) + 0.5 * h * (1.0 - t * t) * scale_c * (1.0 + 3.0 * 0.044715 * h * h)


def times_weight(panel, weight):
    return lax.dot_general(
        panel, weight, (((1,), (1,)), ((), ())), preferred_element_type=jnp.float32
    )


def inner_rows(left, right):
    return lax.dot_general(
        left, right, (((0,), (0,)), ((), ())), preferred_element_type=jnp.float32
    )


def local(inputs, preact, out_grad, weight):
    grad = (out_grad.astype(jnp.float32) * gelu_slope(preact)).astype(jnp.bfloat16)
    all_inputs = lax.all_gather(inputs, "col", axis=0, tiled=True)
    all_grad = lax.all_gather(grad, "row", axis=0, tiled=True)
    weight_grad = inner_rows(all_inputs, all_grad).astype(jnp.bfloat16)
    input_grad = lax.psum_scatter(
        times_weight(all_grad, weight), "col", scatter_dimension=0, tiled=True
    ).astype(jnp.bfloat16)
    return (input_grad, weight_grad)


def solution(mesh):
    in_specs = (P("col", "row"), P("row", "col"), P("row", "col"), P("row", "col"))
    out_specs = (P("col", "row"), P("row", "col"))
    return jax.shard_map(local, mesh=mesh, in_specs=in_specs, out_specs=out_specs, check_vma=False)
```

profile of v0, /device:TPU:8, one launch (start us, length us, event | category | flops | bytes accessed | tf_op | source)
XLA Modules:
  0.0 243.2 jit_solution(4278960300006951862)
XLA Ops:
  7.2 0.0 copy-start
  7.2 0.0 all-gather.3.cloned.1.call-start
  7.2 2.9 %fusion.8 = bf16[128,2048]{1,0:T(8,128)(2,1)} fusion(bf16[128,2048]{1,0:T(8,128)(2,1)} %param.5, bf16[128,2048]{1,0:T(8,128)(2,1)} %param.6), kind=kLoop, calls=%fused_computation.16 | loop fusion | flops 5505024 | bytes 1572864 | tf_op jit(solution)/shard_map/convert_element_type | solution.py:29
  10.1 0.0 all-gather.3.cloned.1.call-update
  10.1 0.0 all-gather.5.cloned.1.call-start
  10.2 0.7 all-gather.5.cloned.1.call-update
  10.9 0.0 reduce-scatter.2.cloned.1.call-start
  10.9 106.1 %all-gather.3.cloned.1.call-done = bf16[2048,2048]{1,0:T(8,128)(2,1)} async-done(((bf16[128,2048]{1,0:T(8,128)(2,1)}), bf16[2048,2048]{1,0:T(8,128)(2,1)}) %all-gather.3.cloned.1.call-update) | async-done | bytes 8388624 | tf_op jit(solution)/shard_map/all_gather | solution.py:31
  117.0 0.0 copy-done
  117.0 9.5 %fusion.10 = f32[2048,512]{1,0:T(8,128)} fusion(bf16[2048,2048]{1,0:T(8,128)(2,1)} %all-gather.3.cloned.1.call-done, bf16[512,2048]{1,0:T(8,128)(2,1)S(1)} %copy-done), kind=kOutput, calls=%fused_computation.18 | convolution fusion | flops 4294967296 | bytes 14680064 | tf_op jit(solution)/shard_map/dot_general | solution.py:17
  126.5 0.0 reduce-scatter.2.cloned.1.call-update
  126.6 40.5 %all-gather.5.cloned.1.call-done = bf16[2048,512]{1,0:T(8,128)(2,1)} async-done(((bf16[128,512]{1,0:T(8,128)(2,1)}), bf16[2048,512]{1,0:T(8,128)(2,1)}) %all-gather.5.cloned.1.call-update) | async-done | bytes 2097168 | tf_op jit(solution)/shard_map/all_gather | solution.py:30
  167.0 9.8 %fusion = bf16[512,2048]{0,1:T(8,128)(2,1)} fusion(bf16[2048,2048]{1,0:T(8,128)(2,1)} %all-gather.3.cloned.1.call-done, bf16[2048,512]{1,0:T(8,128)(2,1)} %all-gather.5.cloned.1.call-done), kind=kOutput, calls=%fused_computation.1 | convolution fusion | flops 4296015872 | bytes 12582912 | tf_op jit(solution)/shard_map/dot_general | solution.py:23
  176.9 3.9 %copy.6 = bf16[512,2048]{1,0:T(8,128)(2,1)} copy(bf16[512,2048]{0,1:T(8,128)(2,1)} %fusion) | data formatting | bytes 4194304
  180.8 54.3 %reduce-scatter.2.cloned.1.call-done = f32[128,512]{1,0:T(8,128)} async-done(((f32[2048,512]{1,0:T(8,128)}), f32[128,512]{1,0:T(8,128)}) %reduce-scatter.2.cloned.1.call-update) | async-done | bytes 262160 | tf_op jit(solution)/shard_map/reduce_scatter | solution.py:33
  235.1 1.6 convert_element_type.21
Async XLA Ops:
  7.2 109.8 %copy-start = (bf16[512,2048]{1,0:T(8,128)(2,1)S(1)}, bf16[512,2048]{1,0:T(8,128)(2,1)}, u32[]{:S(2)}) copy-start(bf16[512,2048]{1,0:T(8,128)(2,1)} %param.7) | copy-start | bytes 6291460
  7.2 109.8 %all-gather.3.cloned.1.call-start = ((), (), s32[]{:S(2)}) async-start(), calls=%async_computation.1 | async-start | bytes 8912896 | tf_op jit(solution)/shard_map/all_gather | solution.py:31
  10.1 156.9 %all-gather.5.cloned.1.call-start = ((), (), s32[]{:S(2)}) async-start(), calls=%async_computation.3 | async-start | bytes 2228224 | tf_op jit(solution)/shard_map/all_gather | solution.py:30
  10.9 224.2 %reduce-scatter.2.cloned.1.call-start = ((), (), s32[]{:S(2)}) async-start(), calls=%async_computation.2 | async-start | bytes 4456448 | tf_op jit(solution)/shard_map/reduce_scatter | solution.py:33
Sparse Core Ops, SparseCore 0:
  11.0 105.9 all-gather.2
  118.9 48.1 all-gather.4
  169.6 65.4 reduce-scatter.1
where the time goes:
time: 248 us; the launch traced here: 243 us
  waiting for transfers between devices  202 us (81%)
  matrix products  19.4 us (8%)
  between operations  13.8 us (6%)
  other arithmetic  4.49 us (2%)
  local copies, waits for them, and re-layouts  3.92 us (2%)
    all_gather x1, waiting for transfers between devices, local(): all_grad = lax.all_gather(grad, 'row', axis=0, tiled=True)  106 us
    reduce_scatter x1, waiting for transfers between devices, local(): lax.psum_scatter(times_weight(all_grad, weight), 'col', scatter_dimension...  54.3 us
    all_gather x1, waiting for transfers between devices, local(): all_inputs = lax.all_gather(inputs, 'col', axis=0, tiled=True)  40.5 us
    dot_general x1, matrix products, inner_rows(): lax.dot_general(left, right, (((0,), (0,)), ((), ())), preferred_element_...  9.85 us
    dot_general x1, matrix products, times_weight(): lax.dot_general(panel, weight, (((1,), (1,)), ((), ())), preferred_elemen...  9.52 us
  transfers between devices with their start and end apart: 3, of which 3 were waited for; matrix products, arithmetic and copies ran while one was open for 10% of the time, Pallas kernels for 0%

commit v1 on v0

v1 whole, which is shorter than its diff:
```python
import math

import jax
import jax.numpy as jnp
from jax import lax
from jax.experimental import pallas as pl
from jax.experimental.pallas import tpu as pltpu
from jax.sharding import PartitionSpec as P

ROWS = 128
NZ = 96
NX = ROWS - NZ
VMEM_LIMIT = 56 * 1024 * 1024

ORDER_Z = ((0, 0), (1, 0), (3, 0), (2, 0), (0, 1), (0, 3), (0, 2), (2, 2),
           (1, 1), (1, 3), (3, 1), (3, 3), (1, 2), (2, 1), (3, 2), (2, 3))
ORDER_X = tuple((dx, dz) for dz in (0, 1, 3, 2) for dx in (0, 1, 3, 2))


def gelu_slope(preact):
    h = preact.astype(jnp.float32)
    scale_c = math.sqrt(2.0 / math.pi)
    t = jnp.tanh(scale_c * (h + 0.044715 * h * h * h))
    return 0.5 * (1.0 + t) + 0.5 * h * (1.0 - t * t) * scale_c * (1.0 + 3.0 * 0.044715 * h * h)


def along_row(a, dx, dz):
    perm = [(x * 4 + z, (x + dx) % 4 * 4 + (z + dz) % 4) for x in range(4) for z in range(4)]
    return lax.ppermute(a, "row", perm)


def along_col(a, dl, dy, dc):
    perm = [
        (l * 8 + y * 2 + c, (l + dl) % 2 * 8 + (y + dy) % 4 * 2 + (c + dc) % 2)
        for l in range(2) for y in range(4) for c in range(2)
    ]
    return lax.ppermute(a, "col", perm)


def vmem():
    return pl.BlockSpec(memory_space=pltpu.VMEM)


def smem():
    return pl.BlockSpec(memory_space=pltpu.SMEM)


def block_ids(order, x, z):
    return jnp.stack([(x - dx + 4) % 4 * 4 + (z - dz + 4) % 4 for dx, dz in order]).astype(jnp.int32)


def order_inputs(place_z, place_x, own, other):
    def kernel(pz, px, own_ref, other_ref, z_ref, x_ref):
        for i in range(16):
            for places, out, low, size in ((pz, z_ref, 0, NZ), (px, x_ref, NZ, NX)):
                place = places[i]

                @pl.when(place < 8)
                def _():
                    out[pl.ds(i * size, size), :] = own_ref[place, pl.ds(low, size), :]

                @pl.when(place >= 8)
                def _():
                    out[pl.ds(i * size, size), :] = other_ref[place - 8, pl.ds(low, size), :]

    d = own.shape[-1]
    return pl.pallas_call(
        kernel,
        out_shape=(
            jax.ShapeDtypeStruct((16 * NZ, d), own.dtype),
            jax.ShapeDtypeStruct((16 * NX, d), own.dtype),
        ),
        in_specs=[smem(), smem(), vmem(), vmem()],
        out_specs=(vmem(), vmem()),
        compiler_params=pltpu.CompilerParams(vmem_limit_bytes=VMEM_LIMIT),
        cost_estimate=pl.CostEstimate(flops=0, bytes_accessed=4 * 1024 * 1024, transcendentals=0),
    )(place_z, place_x, own, other)


def input_grad_parts(slots, pieces, weight, rows):
    d, hidden = weight.shape
    n = len(pieces)

    def kernel(slot_ref, *refs):
        w_ref, send_ref, keep_ref = refs[n:]
        blocks = [(r, k) for r in refs[:n] for k in range(r.shape[0] // rows)]
        per = len(blocks) // 4
        for g in range(4):
            group = blocks[g * per:(g + 1) * per]
            panel = jnp.concatenate([r[k * rows:(k + 1) * rows, :] for r, k in group], axis=0)
            sums = lax.dot_general(
                panel, w_ref[...], (((1,), (1,)), ((), ())), preferred_element_type=jnp.float32
            )
            for k in range(per):
                part = sums[k * rows:(k + 1) * rows]
                slot = slot_ref[g * per + k]

                @pl.when(slot < 8)
                def _():
                    send_ref[slot] = part.astype(jnp.bfloat16)

                @pl.when(slot >= 8)
                def _():
                    keep_ref[slot - 8] = part

    return pl.pallas_call(
        kernel,
        out_shape=(
            jax.ShapeDtypeStruct((8, rows, d), jnp.bfloat16),
            jax.ShapeDtypeStruct((8, rows, d), jnp.float32),
        ),
        in_specs=[smem()] + [vmem()] * (n + 1),
        out_specs=(vmem(), vmem()),
        compiler_params=pltpu.CompilerParams(vmem_limit_bytes=VMEM_LIMIT),
        cost_estimate=pl.CostEstimate(
            flops=2 * 16 * rows * d * hidden, bytes_accessed=16 * rows * hidden * 2, transcendentals=0
        ),
    )(slots, *pieces, weight)


def weight_grad_of(inputs_z, inputs_x, pieces_z, pieces_x, tile=512):
    d = inputs_z.shape[1]
    hidden = pieces_z[0].shape[1]
    pieces = [*pieces_z, *pieces_x]
    n = len(pieces)

    def kernel(iz_ref, ix_ref, *refs):
        out_ref = refs[n]
        left = jnp.concatenate([iz_ref[...], ix_ref[...]], axis=0)
        right = jnp.concatenate([r[...] for r in refs[:n]], axis=0)
        out_ref[...] = lax.dot_general(
            left, right, (((0,), (0,)), ((), ())), preferred_element_type=jnp.float32
        ).astype(jnp.bfloat16)

    return pl.pallas_call(
        kernel,
        grid=(hidden // tile,),
        out_shape=jax.ShapeDtypeStruct((d, hidden), jnp.bfloat16),
        in_specs=[pl.BlockSpec(a.shape, lambda j: (0, 0)) for a in (inputs_z, inputs_x)]
        + [pl.BlockSpec((p.shape[0], tile), lambda j: (0, j)) for p in pieces],
        out_specs=pl.BlockSpec((d, tile), lambda j: (0, j)),
        compiler_params=pltpu.CompilerParams(vmem_limit_bytes=VMEM_LIMIT),
        cost_estimate=pl.CostEstimate(
            flops=2 * 2048 * d * hidden, bytes_accessed=12 * 1024 * 1024, transcendentals=0
        ),
    )(inputs_z, inputs_x, *pieces)


def reduce_rows(send, keep, l, y):
    got = along_col(send, 0, 0, 1)
    sums = (keep + got.astype(jnp.float32)).reshape(2, 4, *keep.shape[1:])

    def pick(a, axis, i):
        return lax.dynamic_index_in_dim(a, i, axis, keepdims=False)

    terms = [
        along_col(pick(sums, 1, (y + dy) % 4).astype(jnp.bfloat16), 0, dy, 0) for dy in (1, 3, 2)
    ]
    total = pick(sums, 1, y)
    for term in terms:
        total = total + term.astype(jnp.float32)
    last = along_col(pick(total, 0, 1 - l).astype(jnp.bfloat16), 1, 0, 0)
    return (pick(total, 0, l) + last.astype(jnp.float32)).astype(jnp.bfloat16)


def local(inputs, preact, out_grad, weight):
    row, col = lax.axis_index("row"), lax.axis_index("col")
    x, z = row // 4, row % 4
    l, y, c = col // 8, col // 2 % 4, col % 2

    pair = jnp.stack([inputs, along_col(inputs, 1, 0, 0)])
    own = jnp.concatenate(
        [pair, along_col(pair, 0, 1, 0), along_col(pair, 0, 2, 0), along_col(pair, 0, 3, 0)]
    )
    other = along_col(own, 0, 0, 1)

    grad = (out_grad.astype(jnp.float32) * gelu_slope(preact)).astype(jnp.bfloat16)
    gz, gx = grad[:NZ], grad[NZ:]
    half = NZ // 2
    a1, a3 = along_row(grad, 1, 0), along_row(grad, 3, 0)
    b1, b3 = along_row(gz, 0, 1), along_row(gz, 0, 3)
    a2 = jnp.concatenate(
        [along_row(a1[:ROWS // 2], 1, 0), along_row(a3[ROWS // 2:], 3, 0)], axis=0
    )
    b2 = jnp.concatenate([along_row(b1[:half], 0, 1), along_row(b3[half:], 0, 3)], axis=0)
    b13 = jnp.concatenate([b1, b3], axis=0)
    f1, f3 = along_row(b13, 1, 0), along_row(b13, 3, 0)
    xs = jnp.concatenate([gx, a1[NZ:], a3[NZ:], a2[NZ:]], axis=0)
    e1, e3 = along_row(xs, 0, 1), along_row(xs, 0, 3)
    p1 = along_row(jnp.concatenate([b2, f1[:NZ]], axis=0), 1, 0)
    p3 = along_row(jnp.concatenate([b2, f3[NZ:]], axis=0), 3, 0)
    p2 = along_row(b2, 2, 0)
    q1, q3 = along_row(e1[:2 * NX], 0, 1), along_row(e3[2 * NX:], 0, 3)

    pieces_z = [gz, a1[:NZ], a3[:NZ], a2[:NZ], b1, b3, b2, p2, f1, f3, p1, p3]
    pieces_x = [xs, e1, e3, q1, q3]

    ids_z, ids_x = block_ids(ORDER_Z, x, z), block_ids(ORDER_X, x, z)

    def place(ids):
        return (c - ids % 2 + 2) % 2 * 8 + (y - ids // 2 % 4 + 4) % 4 * 2 + (l - ids // 8 + 2) % 2

    def slot(ids):
        return jnp.where(ids % 2 == c, 8, 0) + ids // 2

    inputs_z, inputs_x = order_inputs(place(ids_z), place(ids_x), own, other)
    send_z, keep_z = input_grad_parts(slot(ids_z), pieces_z, weight, NZ)
    send_x, keep_x = input_grad_parts(slot(ids_x), pieces_x, weight, NX)
    weight_grad = weight_grad_of(inputs_z, inputs_x, pieces_z, pieces_x)
    input_grad = jnp.concatenate(
        [reduce_rows(send_z, keep_z, l, y), reduce_rows(send_x, keep_x, l, y)], axis=0
    )
    return (input_grad, weight_grad)


def solution(mesh):
    in_specs = (P("col", "row"), P("row", "col"), P("row", "col"), P("row", "col"))
    out_specs = (P("col", "row"), P("row", "col"))
    return jax.shard_map(local, mesh=mesh, in_specs=in_specs, out_specs=out_specs, check_vma=False)
```

time: 248 us -> 169 us (0.68); the launches traced: 243 us -> 168 us
  waiting for transfers between devices: 202 us -> 61.7 us
  starting transfers between devices: 0.12 us -> 56.5 us
  Pallas kernels: 0 us -> 28.1 us
  matrix products: 19.4 us -> 0 us
  between operations: 13.8 us -> 1.14 us
  local copies, waits for them, and re-layouts: 3.92 us -> 10.4 us
  other arithmetic: 4.49 us -> 9.72 us
    all_gather x2 -> x0, waiting for transfers between devices: 147 us -> none  [the longest x1 106 us: local(): all_grad = lax.all_gather(grad, 'row', axis=0, tiled=True)]
    ppermute x0 -> x32, waiting for transfers between devices: none -> 61.7 us  [the longest x17 54.3 us: along_row(): return lax.ppermute(a, 'row', perm)]
    ppermute x0 -> x32, starting transfers between devices: none -> 56.5 us  [the longest x17 35.5 us: along_row(): return lax.ppermute(a, 'row', perm)]
    reduce_scatter x1 -> x0, waiting for transfers between devices: 54.3 us -> none  [local(): lax.psum_scatter(times_weight(all_grad, weight), 'col', scatter_dimension...]
    pallas_call x0 -> x4, Pallas kernels: none -> 28.1 us  [the longest x2 15.9 us: input_grad_parts(): pl.pallas_call(kernel, out_shape=(jax.ShapeDtypeStruct((8, rows, d), jnp....]
    dot_general x2 -> x0, matrix products: 19.4 us -> none  [the longest x1 9.85 us: inner_rows(): lax.dot_general(left, right, (((0,), (0,)), ((), ())), preferred_element_...]
    slice x0 -> x15, local copies, waits for them, and re-layouts: none -> 5.89 us  [the longest x2 1.65 us: local(): pieces_z = [gz, a1[:NZ], a3[:NZ], a2[:NZ], b1, b3, b2, p2, f1, f3, p1, p3]]
    concatenate x0 -> x4, other arithmetic: none -> 3.56 us  [the longest x1 1.76 us: local(): jnp.concatenate([along_row(a1[:ROWS // 2], 1, 0), along_row(a3[ROWS // 2:...]
  transfers between devices with their start and end apart: 3 -> 32, of which waited for: 3 -> 9; matrix products, arithmetic and copies ran while one was open for 10% -> 9% of each run, Pallas kernels for 0% -> 17%
where the time goes in v1:
time: 169 us; the launch traced here: 168 us
  waiting for transfers between devices  61.7 us (37%)
  starting transfers between devices  56.5 us (33%)
  Pallas kernels  28.1 us (17%)
  local copies, waits for them, and re-layouts  10.4 us (6%)
  other arithmetic  9.72 us (6%)
    ppermute x17, waiting for transfers between devices, along_row(): return lax.ppermute(a, 'row', perm)  54.3 us
    ppermute x17, starting transfers between devices, along_row(): return lax.ppermute(a, 'row', perm)  35.5 us
    ppermute x15, starting transfers between devices, along_col(): return lax.ppermute(a, 'col', perm)  21.1 us
    pallas_call x2, Pallas kernels, input_grad_parts(): pl.pallas_call(kernel, out_shape=(jax.ShapeDtypeStruct((8, rows, d), jnp....  15.9 us
    pallas_call x1, Pallas kernels, weight_grad_of(): pl.pallas_call(kernel, grid=(hidden // tile,), out_shape=jax.ShapeDtypeSt...  8.83 us
    ppermute x15, waiting for transfers between devices, along_col(): return lax.ppermute(a, 'col', perm)  7.45 us
    pallas_call x1, Pallas kernels, order_inputs(): pl.pallas_call(kernel, out_shape=(jax.ShapeDtypeStruct((16 * NZ, d), own....  3.4 us
  transfers between devices with their start and end apart: 32, of which 9 were waited for; matrix products, arithmetic and copies ran while one was open for 9% of the time, Pallas kernels for 17%

profile of v1, /device:TPU:8, one launch (start us, length us, event | category | flops | bytes accessed | tf_op | source)
XLA Modules:
  0.0 167.6 jit_solution(2958453369081088798)
XLA Ops:
  0.6 2.0 %fusion.7 = bf16[128,2048]{1,0:T(8,128)(2,1)S(1)} fusion(bf16[128,2048]{1,0:T(8,128)(2,1)} %param.5, bf16[128,2048]{1,0:T(8,128)(2,1)} %param.6), kind=kLoop, calls=%fused_computation.15 | loop fusion | flops 5505024 | bytes 1572864 | tf_op jit(solution)/shard_map/convert_element_type | solution.py:177
  2.6 0.8 slice.64.refs_0_
  3.4 6.3 %collective-permute-start.5 = (bf16[96,2048]{1,0:T(8,128)(2,1)}, bf16[96,2048]{1,0:T(8,128)(2,1)S(1)}, u32[]{:S(2)}, u32[]{:S(2)}) collective-permute-start(bf16[96,2048]{1,0:T(8,128)(2,1)} %slice.64.refs_0_), channel_id=1, source_target_pairs={{0,48},{16,0},{32,16},{48,32},{64,112},{80,64},{96,80},{112,96},{1... | collective-permute-start | bytes 1179656 | tf_op jit(solution)/shard_map/ppermute | solution.py:29
  9.7 2.8 %collective-permute-start.1 = (bf16[128,2048]{1,0:T(8,128)(2,1)S(1)}, bf16[128,2048]{1,0:T(8,128)(2,1)S(1)}, u32[]{:S(2)}, u32[]{:S(2)}) collective-permute-start(bf16[128,2048]{1,0:T(8,128)(2,1)S(1)} %fusion.7), channel_id=1, source_target_pairs={{0,192},{16,208},{32,224},{48,240},{64,0},{80,16},{96,32},{112,48}... | collective-permute-start | bytes 1572872 | tf_op jit(solution)/shard_map/ppermute | solution.py:29
  12.5 1.0 collective-permute-start.27
  13.5 0.1 stack.96
  13.6 0.1 stack.95
  13.7 0.6 fusion.23
  14.3 0.5 fusion.26.slot_ref
  14.8 16.9 %collective-permute-done.4.refs_4_ = bf16[96,2048]{1,0:T(8,128)(2,1)S(1)} collective-permute-done((bf16[96,2048]{1,0:T(8,128)(2,1)}, bf16[96,2048]{1,0:T(8,128)(2,1)S(1)}, u32[]{:S(2)}, u32[]{:S(2)}) %collective-permute-start.4) | collective-permute-done | bytes 393248 | tf_op jit(solution)/shard_map/ppermute | solution.py:29
  31.7 0.8 constant_dynamic-update-slice_fusion.3
  32.6 0.8 constant_dynamic-update-slice_fusion.2
  33.4 2.8 %collective-permute-start.10 = (bf16[192,2048]{1,0:T(8,128)(2,1)}, bf16[192,2048]{1,0:T(8,128)(2,1)}, u32[]{:S(2)}, u32[]{:S(2)}) collective-permute-start(bf16[192,2048]{1,0:T(8,128)(2,1)} %constant_dynamic-update-slice_fusion.2), channel_id=1, source_target_pairs={{0,192},{16,208},{32,224},{48,240},{64,0},{80,16},{96,32},{112,48}... | collective-permute-start | bytes 2359304 | tf_op jit(solution)/shard_map/ppermute | solution.py:29
  36.2 0.7 slice.68
  36.9 0.8 collective-permute-start.3
  37.7 0.5 fusion.25.slot_ref
  38.3 0.7 slice.73
  38.9 1.2 collective-permute-start.9
  40.1 0.9 pad_maximum_fusion.5
  41.1 2.4 %collective-permute-start.29 = (bf16[2,128,512]{2,1,0:T(8,128)(2,1)S(1)}, bf16[2,128,512]{2,1,0:T(8,128)(2,1)S(1)}, u32[]{:S(2)}, u32[]{:S(2)}) collective-permute-start(bf16[2,128,512]{2,1,0:T(8,128)(2,1)S(1)} %pad_maximum_fusion.5), channel_id=1, source_target_pairs={{0,4},{1,5},{2,6},{3,7},{4,0},{5,1},{6,2},{7,3},{8,12},{9,13},{10,... | collective-permute-start | bytes 786440 | tf_op jit(solution)/shard_map/ppermute | solution.py:37
  43.6 6.9 %collective-permute-done.3 = bf16[64,2048]{1,0:T(8,128)(2,1)} collective-permute-done((bf16[64,2048]{1,0:T(8,128)(2,1)}, bf16[64,2048]{1,0:T(8,128)(2,1)}, u32[]{:S(2)}, u32[]{:S(2)}) %collective-permute-start.3) | collective-permute-done | bytes 262176 | tf_op jit(solution)/shard_map/ppermute | solution.py:29
  50.5 0.9 slice.76
  51.5 0.9 pad_maximum_fusion.3.refs_0_.refs_12_
  52.4 6.5 %collective-permute-start.19 = (bf16[128,2048]{1,0:T(8,128)(2,1)S(1)}, bf16[128,2048]{1,0:T(8,128)(2,1)S(1)}, u32[]{:S(2)}, u32[]{:S(2)}) collective-permute-start(bf16[128,2048]{1,0:T(8,128)(2,1)S(1)} %pad_maximum_fusion.3.refs_0_.refs_12_), channel_id=1, source_target_pairs={{0,48},{16,0},{32,16},{48,32},{64,112},{80,64},{96,80},{112,96},{1... | collective-permute-start | bytes 1572872 | tf_op jit(solution)/shard_map/ppermute | solution.py:29
  58.9 0.9 constant_dynamic-update-slice_fusion.7
  59.9 0.3 collective-permute-start.7
  60.2 2.7 %collective-permute-start.6 = (bf16[48,2048]{1,0:T(8,128)(2,1)S(1)}, bf16[48,2048]{1,0:T(8,128)(2,1)S(1)}, u32[]{:S(2)}, u32[]{:S(2)}) collective-permute-start(bf16[48,2048]{1,0:T(8,128)(2,1)S(1)} %slice.69), channel_id=1, source_target_pairs={{0,16},{16,32},{32,48},{48,0},{64,80},{80,96},{96,112},{112,64},{1... | collective-permute-start | bytes 589832 | tf_op jit(solution)/shard_map/ppermute | solution.py:29
  62.9 0.1 collective-permute-start.18
  63.1 1.0 slice.72
  64.2 0.7 collective-permute-start.30
  64.9 21.9 %collective-permute-done.7 = bf16[48,2048]{1,0:T(8,128)(2,1)S(1)} collective-permute-done((bf16[48,2048]{1,0:T(8,128)(2,1)S(1)}, bf16[48,2048]{1,0:T(8,128)(2,1)S(1)}, u32[]{:S(2)}, u32[]{:S(2)}) %collective-permute-start.7) | collective-permute-done | bytes 196640 | tf_op jit(solution)/shard_map/ppermute | solution.py:29
  86.8 1.2 collective-permute-start.2
  88.0 0.2 pad_maximum_fusion.2
  88.2 2.6 %collective-permute-start.12 = (bf16[192,2048]{1,0:T(8,128)(2,1)S(1)}, bf16[192,2048]{1,0:T(8,128)(2,1)}, u32[]{:S(2)}, u32[]{:S(2)}) collective-permute-start(bf16[192,2048]{1,0:T(8,128)(2,1)S(1)} %get-tuple-element.24), channel_id=1, source_target_pairs={{0,192},{16,208},{32,224},{48,240},{64,0},{80,16},{96,32},{112,48}... | collective-permute-start | bytes 2359304 | tf_op jit(solution)/shard_map/ppermute | solution.py:29
  90.9 4.7 %collective-permute-start.21 = (bf16[64,2048]{1,0:T(8,128)(2,1)S(1)}, bf16[64,2048]{1,0:T(8,128)(2,1)S(1)}, u32[]{:S(2)}, u32[]{:S(2)}) collective-permute-start(bf16[64,2048]{1,0:T(8,128)(2,1)S(1)} %slice.78), channel_id=1, source_target_pairs={{0,48},{16,0},{32,16},{48,32},{64,112},{80,64},{96,80},{112,96},{1... | collective-permute-start | bytes 786440 | tf_op jit(solution)/shard_map/ppermute | solution.py:29
  95.7 3.6 %collective-permute-start.8 = (bf16[96,2048]{1,0:T(8,128)(2,1)S(1)}, bf16[96,2048]{1,0:T(8,128)(2,1)S(1)}, u32[]{:S(2)}, u32[]{:S(2)}) collective-permute-start(bf16[96,2048]{1,0:T(8,128)(2,1)S(1)} %constant_dynamic-update-slice_fusion.refs_6_), channel_id=1, source_target_pairs={{0,128},{16,144},{32,160},{48,176},{64,192},{80,208},{96,224},{112... | collective-permute-start | bytes 1179656 | tf_op jit(solution)/shard_map/ppermute | solution.py:29
  99.3 0.9 slice.66.refs_2_
  100.1 0.8 slice.65.refs_1_
  100.9 3.9 %collective-permute-done.21.refs_4_.refs_16_ = bf16[64,2048]{1,0:T(8,128)(2,1)S(1)} collective-permute-done((bf16[64,2048]{1,0:T(8,128)(2,1)S(1)}, bf16[64,2048]{1,0:T(8,128)(2,1)S(1)}, u32[]{:S(2)}, u32[]{:S(2)}) %collective-permute-start.21) | collective-permute-done | bytes 262176 | tf_op jit(solution)/shard_map/ppermute | solution.py:29
  104.9 1.8 %pad_maximum_fusion.4.refs_3_ = bf16[96,2048]{1,0:T(8,128)(2,1)} fusion(bf16[64,2048]{1,0:T(8,128)(2,1)} %collective-permute-done.3, bf16[64,2048]{1,0:T(8,128)(2,1)S(1)} %collective-permute-done.2), kind=kLoop, calls=%fused_computation.22 | loop fusion | flops 786432 | bytes 917504 | tf_op jit(solution)/shard_map/concatenate | solution.py:182
  106.6 4.5 %collective-permute-done.20.refs_3_.refs_15_ = bf16[64,2048]{1,0:T(8,128)(2,1)S(1)} collective-permute-done((bf16[64,2048]{1,0:T(8,128)(2,1)S(1)}, bf16[64,2048]{1,0:T(8,128)(2,1)S(1)}, u32[]{:S(2)}, u32[]{:S(2)}) %collective-permute-start.20) | collective-permute-done | bytes 262176 | tf_op jit(solution)/shard_map/ppermute | solution.py:29
  111.1 0.7 copy-done.12
  111.9 6.6 %shard_map.60 = (bf16[8,32,512]{2,1,0:T(8,128)(2,1)}, f32[8,32,512]{2,1,0:T(8,128)}) custom-call(s32[16]{0:T(128)} %fusion.26.slot_ref, bf16[128,2048]{1,0:T(8,128)(2,1)} %copy-done, bf16[128,2048]{1,0:T(8,128)(2,1)} %copy-done.4, bf16[128,2048]{1,0:T(8,128)(2,1)} %copy-done.3, bf16[64,2048]{1,0:T(8,128)(2,1)} %copy-done.12, bf16[64,2048]{1,0:T(8,128)(2,1)} %copy-done.11, ...), custom_call_target="tpu_custom_call" | custom-call | flops 1073741824 | bytes 2097152 | tf_op jit(solution)/shard_map/pallas_call | solution.py:106
  118.5 0.1 collective-permute-start.22
  118.6 0.7 copy-done.15
  119.3 9.3 %shard_map.59 = (bf16[8,96,512]{2,1,0:T(8,128)(2,1)}, f32[8,96,512]{2,1,0:T(8,128)}) custom-call(s32[16]{0:T(128)} %fusion.25.slot_ref, bf16[96,2048]{1,0:T(8,128)(2,1)} %slice.64.refs_0_, bf16[96,2048]{1,0:T(8,128)(2,1)} %slice.65.refs_1_, bf16[96,2048]{1,0:T(8,128)(2,1)} %slice.66.refs_2_, bf16[96,2048]{1,0:T(8,128)(2,1)} %pad_maximum_fusion.4.refs_3_, ...), custom_call_target="tpu_custom_call" | custom-call | flops 3221225472 | bytes 6291456 | tf_op jit(solution)/shard_map/pallas_call | solution.py:106
  128.6 0.5 collective-permute-start.13
  129.2 1.7 collective-permute-start.23
  130.9 0.4 collective-permute-start.24
  131.3 2.3 %collective-permute-start.25 = (bf16[2,32,512]{2,1,0:T(8,128)(2,1)S(1)}, bf16[2,32,512]{2,1,0:T(8,128)(2,1)S(1)}, u32[]{:S(2)}, u32[]{:S(2)}) collective-permute-start(bf16[2,32,512]{2,1,0:T(8,128)(2,1)S(1)} %get-tuple-element.23), channel_id=1, source_target_pairs={{0,4},{1,5},{2,6},{3,7},{4,0},{5,1},{6,2},{7,3},{8,12},{9,13},{10,... | collective-permute-start | bytes 196616 | tf_op jit(solution)/shard_map/ppermute | solution.py:37
  133.6 3.4 %shard_map.61 = (bf16[1536,512]{1,0:T(8,128)(2,1)}, bf16[512,512]{1,0:T(8,128)(2,1)}) custom-call(s32[16]{0:T(128)} %get-tuple-element.16.pz, s32[16]{0:T(128)} %get-tuple-element.26.px, bf16[8,128,512]{2,1,0:T(8,128)(2,1)} %copy-done.2, bf16[8,128,512]{2,1,0:T(8,128)(2,1)} %collective-permute-done.31.other_ref), custom_call_target="tpu_custom_call" | custom-call | bytes 4194304 | tf_op jit(solution)/shard_map/pallas_call | solution.py:67
  137.1 7.3 %collective-permute-start.26 = (bf16[32,512]{1,0:T(8,128)(2,1)S(1)}, bf16[32,512]{1,0:T(8,128)(2,1)S(1)}, u32[]{:S(2)}, u32[]{:S(2)}) collective-permute-start(bf16[32,512]{1,0:T(8,128)(2,1)S(1)} %fusion.22), channel_id=1, source_target_pairs={{0,8},{1,9},{2,10},{3,11},{4,12},{5,13},{6,14},{7,15},{8,0},{9,1},... | collective-permute-start | bytes 98312 | tf_op jit(solution)/shard_map/ppermute | solution.py:37
  144.4 1.4 convert_add_fusion.1
  145.8 0.1 fusion.11
  145.9 1.5 collective-permute-start.14
  147.4 0.6 collective-permute-start.15
  148.0 2.1 %collective-permute-start.16 = (bf16[2,96,512]{2,1,0:T(8,128)(2,1)S(1)}, bf16[2,96,512]{2,1,0:T(8,128)(2,1)S(1)}, u32[]{:S(2)}, u32[]{:S(2)}) collective-permute-start(bf16[2,96,512]{2,1,0:T(8,128)(2,1)S(1)} %get-tuple-element.20), channel_id=1, source_target_pairs={{0,4},{1,5},{2,6},{3,7},{4,0},{5,1},{6,2},{7,3},{8,12},{9,13},{10,... | collective-permute-start | bytes 589832 | tf_op jit(solution)/shard_map/ppermute | solution.py:37
  150.2 3.7 %collective-permute-done.14 = bf16[2,96,512]{2,1,0:T(8,128)(2,1)S(1)} collective-permute-done((bf16[2,96,512]{2,1,0:T(8,128)(2,1)S(1)}, bf16[2,96,512]{2,1,0:T(8,128)(2,1)S(1)}, u32[]{:S(2)}, u32[]{:S(2)}) %collective-permute-start.14) | collective-permute-done | bytes 196640 | tf_op jit(solution)/shard_map/ppermute | solution.py:37
  153.8 1.3 collective-permute-done.15
  155.2 2.4 %collective-permute-done.16 = bf16[2,96,512]{2,1,0:T(8,128)(2,1)S(1)} collective-permute-done((bf16[2,96,512]{2,1,0:T(8,128)(2,1)S(1)}, bf16[2,96,512]{2,1,0:T(8,128)(2,1)S(1)}, u32[]{:S(2)}, u32[]{:S(2)}) %collective-permute-start.16) | collective-permute-done | bytes 196640 | tf_op jit(solution)/shard_map/ppermute | solution.py:37
  157.5 0.1 fusion.10
  157.7 0.4 collective-permute-start.17
  158.1 8.8 %shard_map.62 = bf16[512,2048]{1,0:T(8,128)(2,1)} custom-call(bf16[1536,512]{1,0:T(8,128)(2,1)} %get-tuple-element.12.iz_ref, bf16[512,512]{1,0:T(8,128)(2,1)} %get-tuple-element.13.ix_ref, bf16[96,2048]{1,0:T(8,128)(2,1)} %slice.64.refs_0_, bf16[96,2048]{1,0:T(8,128)(2,1)} %slice.65.refs_1_, bf16[96,2048]{1,0:T(8,128)(2,1)} %slice.66.refs_2_, ...), custom_call_target="tpu_custom_call" | custom-call | flops 4294967296 | bytes 12582912 | tf_op jit(solution)/shard_map/pallas_call | solution.py:135
  167.0 0.7 pad_maximum_fusion.6
  (81 shorter events, 0.7 us)
Async XLA Ops:
  0.6 11.8 %copy-start.10 = (bf16[128,512]{1,0:T(8,128)(2,1)S(1)}, bf16[128,512]{1,0:T(8,128)(2,1)}, u32[]{:S(2)}) copy-start(bf16[128,512]{1,0:T(8,128)(2,1)} %param.4) | copy-start | bytes 393220
  3.4 29.2 %collective-permute-start.5 = (bf16[96,2048]{1,0:T(8,128)(2,1)}, bf16[96,2048]{1,0:T(8,128)(2,1)S(1)}, u32[]{:S(2)}, u32[]{:S(2)}) collective-permute-start(bf16[96,2048]{1,0:T(8,128)(2,1)} %slice.64.refs_0_), channel_id=1, source_target_pairs={{0,48},{16,0},{32,16},{48,32},{64,112},{80,64},{96,80},{112,96},{1... | collective-permute-start | bytes 1179656 | tf_op jit(solution)/shard_map/ppermute | solution.py:29
  9.7 22.1 %collective-permute-start.4 = (bf16[96,2048]{1,0:T(8,128)(2,1)}, bf16[96,2048]{1,0:T(8,128)(2,1)S(1)}, u32[]{:S(2)}, u32[]{:S(2)}) collective-permute-start(bf16[96,2048]{1,0:T(8,128)(2,1)} %slice.64.refs_0_), channel_id=1, source_target_pairs={{0,16},{16,32},{32,48},{48,0},{64,80},{80,96},{96,112},{112,64},{1... | collective-permute-start | bytes 1179656 | tf_op jit(solution)/shard_map/ppermute | solution.py:29
  9.7 26.5 %collective-permute-start.1 = (bf16[128,2048]{1,0:T(8,128)(2,1)S(1)}, bf16[128,2048]{1,0:T(8,128)(2,1)S(1)}, u32[]{:S(2)}, u32[]{:S(2)}) collective-permute-start(bf16[128,2048]{1,0:T(8,128)(2,1)S(1)} %fusion.7), channel_id=1, source_target_pairs={{0,192},{16,208},{32,224},{48,240},{64,0},{80,16},{96,32},{112,48}... | collective-permute-start | bytes 1572872 | tf_op jit(solution)/shard_map/ppermute | solution.py:29
  12.4 31.0 %collective-permute-start = (bf16[128,2048]{1,0:T(8,128)(2,1)S(1)}, bf16[128,2048]{1,0:T(8,128)(2,1)S(1)}, u32[]{:S(2)}, u32[]{:S(2)}) collective-permute-start(bf16[128,2048]{1,0:T(8,128)(2,1)S(1)} %fusion.7), channel_id=1, source_target_pairs={{0,64},{16,80},{32,96},{48,112},{64,128},{80,144},{96,160},{112,17... | collective-permute-start | bytes 1572872 | tf_op jit(solution)/shard_map/ppermute | solution.py:29
  12.5 27.7 %collective-permute-start.27 = (bf16[128,512]{1,0:T(8,128)(2,1)S(1)}, bf16[128,512]{1,0:T(8,128)(2,1)}, u32[]{:S(2)}, u32[]{:S(2)}) collective-permute-start(bf16[128,512]{1,0:T(8,128)(2,1)S(1)} %copy-done.10), channel_id=1, source_target_pairs={{0,8},{1,9},{2,10},{3,11},{4,12},{5,13},{6,14},{7,15},{8,0},{9,1},... | collective-permute-start | bytes 393224 | tf_op jit(solution)/shard_map/ppermute | solution.py:37
  31.7 28.1 %copy-start.8 = (bf16[96,2048]{1,0:T(8,128)(2,1)}, bf16[96,2048]{1,0:T(8,128)(2,1)S(1)}, u32[]{:S(2)}) copy-start(bf16[96,2048]{1,0:T(8,128)(2,1)S(1)} %collective-permute-done.4.refs_4_) | copy-start | bytes 1179652
  32.6 27.2 %copy-start.7 = (bf16[96,2048]{1,0:T(8,128)(2,1)}, bf16[96,2048]{1,0:T(8,128)(2,1)S(1)}, u32[]{:S(2)}) copy-start(bf16[96,2048]{1,0:T(8,128)(2,1)S(1)} %collective-permute-done.5.refs_5_) | copy-start | bytes 1179652
  33.4 29.5 %collective-permute-start.10 = (bf16[192,2048]{1,0:T(8,128)(2,1)}, bf16[192,2048]{1,0:T(8,128)(2,1)}, u32[]{:S(2)}, u32[]{:S(2)}) collective-permute-start(bf16[192,2048]{1,0:T(8,128)(2,1)} %constant_dynamic-update-slice_fusion.2), channel_id=1, source_target_pairs={{0,192},{16,208},{32,224},{48,240},{64,0},{80,16},{96,32},{112,48}... | collective-permute-start | bytes 2359304 | tf_op jit(solution)/shard_map/ppermute | solution.py:29
  36.9 13.6 %collective-permute-start.3 = (bf16[64,2048]{1,0:T(8,128)(2,1)}, bf16[64,2048]{1,0:T(8,128)(2,1)}, u32[]{:S(2)}, u32[]{:S(2)}) collective-permute-start(bf16[64,2048]{1,0:T(8,128)(2,1)} %slice.68), channel_id=1, source_target_pairs={{0,192},{16,208},{32,224},{48,240},{64,0},{80,16},{96,32},{112,48}... | collective-permute-start | bytes 786440 | tf_op jit(solution)/shard_map/ppermute | solution.py:29
  38.9 25.2 %collective-permute-start.9 = (bf16[192,2048]{1,0:T(8,128)(2,1)}, bf16[192,2048]{1,0:T(8,128)(2,1)S(1)}, u32[]{:S(2)}, u32[]{:S(2)}) collective-permute-start(bf16[192,2048]{1,0:T(8,128)(2,1)} %constant_dynamic-update-slice_fusion.2), channel_id=1, source_target_pairs={{0,64},{16,80},{32,96},{48,112},{64,128},{80,144},{96,160},{112,17... | collective-permute-start | bytes 2359304 | tf_op jit(solution)/shard_map/ppermute | solution.py:29
  41.1 18.8 %collective-permute-start.29 = (bf16[2,128,512]{2,1,0:T(8,128)(2,1)S(1)}, bf16[2,128,512]{2,1,0:T(8,128)(2,1)S(1)}, u32[]{:S(2)}, u32[]{:S(2)}) collective-permute-start(bf16[2,128,512]{2,1,0:T(8,128)(2,1)S(1)} %pad_maximum_fusion.5), channel_id=1, source_target_pairs={{0,4},{1,5},{2,6},{3,7},{4,0},{5,1},{6,2},{7,3},{8,12},{9,13},{10,... | collective-permute-start | bytes 786440 | tf_op jit(solution)/shard_map/ppermute | solution.py:37
  43.5 8.0 %copy-start.5 = (bf16[128,2048]{1,0:T(8,128)(2,1)}, bf16[128,2048]{1,0:T(8,128)(2,1)S(1)}, u32[]{:S(2)}) copy-start(bf16[128,2048]{1,0:T(8,128)(2,1)S(1)} %collective-permute-done) | copy-start | bytes 1572868
  43.5 16.8 %collective-permute-start.28 = (bf16[2,128,512]{2,1,0:T(8,128)(2,1)S(1)}, bf16[2,128,512]{2,1,0:T(8,128)(2,1)S(1)}, u32[]{:S(2)}, u32[]{:S(2)}) collective-permute-start(bf16[2,128,512]{2,1,0:T(8,128)(2,1)S(1)} %pad_maximum_fusion.5), channel_id=1, source_target_pairs={{0,2},{1,3},{2,4},{3,5},{4,6},{5,7},{6,0},{7,1},{8,10},{9,11},{10,... | collective-permute-start | bytes 786440 | tf_op jit(solution)/shard_map/ppermute | solution.py:37
  52.4 11.7 %copy-start = (bf16[128,2048]{1,0:T(8,128)(2,1)}, bf16[128,2048]{1,0:T(8,128)(2,1)S(1)}, u32[]{:S(2)}) copy-start(bf16[128,2048]{1,0:T(8,128)(2,1)S(1)} %pad_maximum_fusion.3.refs_0_.refs_12_) | copy-start | bytes 1572868
  52.4 10.6 %copy-start.6 = (bf16[128,2048]{1,0:T(8,128)(2,1)S(1)}, bf16[128,2048]{1,0:T(8,128)(2,1)}, u32[]{:S(2)}) copy-start(bf16[128,2048]{1,0:T(8,128)(2,1)} %copy-done.5) | copy-start | bytes 1572868
  52.4 38.4 %collective-permute-start.19 = (bf16[128,2048]{1,0:T(8,128)(2,1)S(1)}, bf16[128,2048]{1,0:T(8,128)(2,1)S(1)}, u32[]{:S(2)}, u32[]{:S(2)}) collective-permute-start(bf16[128,2048]{1,0:T(8,128)(2,1)S(1)} %pad_maximum_fusion.3.refs_0_.refs_12_), channel_id=1, source_target_pairs={{0,48},{16,0},{32,16},{48,32},{64,112},{80,64},{96,80},{112,96},{1... | collective-permute-start | bytes 1572872 | tf_op jit(solution)/shard_map/ppermute | solution.py:29
  59.9 26.9 %collective-permute-start.7 = (bf16[48,2048]{1,0:T(8,128)(2,1)S(1)}, bf16[48,2048]{1,0:T(8,128)(2,1)S(1)}, u32[]{:S(2)}, u32[]{:S(2)}) collective-permute-start(bf16[48,2048]{1,0:T(8,128)(2,1)S(1)} %slice.70), channel_id=1, source_target_pairs={{0,48},{16,0},{32,16},{48,32},{64,112},{80,64},{96,80},{112,96},{1... | collective-permute-start | bytes 589832 | tf_op jit(solution)/shard_map/ppermute | solution.py:29
  60.2 27.8 %collective-permute-start.6 = (bf16[48,2048]{1,0:T(8,128)(2,1)S(1)}, bf16[48,2048]{1,0:T(8,128)(2,1)S(1)}, u32[]{:S(2)}, u32[]{:S(2)}) collective-permute-start(bf16[48,2048]{1,0:T(8,128)(2,1)S(1)} %slice.69), channel_id=1, source_target_pairs={{0,16},{16,32},{32,48},{48,0},{64,80},{80,96},{96,112},{112,64},{1... | collective-permute-start | bytes 589832 | tf_op jit(solution)/shard_map/ppermute | solution.py:29
  62.9 27.9 %collective-permute-start.18 = (bf16[128,2048]{1,0:T(8,128)(2,1)S(1)}, bf16[128,2048]{1,0:T(8,128)(2,1)S(1)}, u32[]{:S(2)}, u32[]{:S(2)}) collective-permute-start(bf16[128,2048]{1,0:T(8,128)(2,1)S(1)} %pad_maximum_fusion.3.refs_0_.refs_12_), channel_id=1, source_target_pairs={{0,16},{16,32},{32,48},{48,0},{64,80},{80,96},{96,112},{112,64},{1... | collective-permute-start | bytes 1572872 | tf_op jit(solution)/shard_map/ppermute | solution.py:29
  64.1 24.1 %copy-start.13 = (bf16[192,2048]{1,0:T(8,128)(2,1)}, bf16[192,2048]{1,0:T(8,128)(2,1)S(1)}, u32[]{:S(2)}) copy-start(bf16[192,2048]{1,0:T(8,128)(2,1)S(1)} %collective-permute-done.9.refs_8_) | copy-start | bytes 2359300
  64.2 31.5 %collective-permute-start.30 = (bf16[2,128,512]{2,1,0:T(8,128)(2,1)S(1)}, bf16[2,128,512]{2,1,0:T(8,128)(2,1)S(1)}, u32[]{:S(2)}, u32[]{:S(2)}) collective-permute-start(bf16[2,128,512]{2,1,0:T(8,128)(2,1)S(1)} %pad_maximum_fusion.5), channel_id=1, source_target_pairs={{0,6},{1,7},{2,0},{3,1},{4,2},{5,3},{6,4},{7,5},{8,14},{9,15},{10,... | collective-permute-start | bytes 786440 | tf_op jit(solution)/shard_map/ppermute | solution.py:37
  86.8 12.4 %collective-permute-start.2 = (bf16[64,2048]{1,0:T(8,128)(2,1)S(1)}, bf16[64,2048]{1,0:T(8,128)(2,1)S(1)}, u32[]{:S(2)}, u32[]{:S(2)}) collective-permute-start(bf16[64,2048]{1,0:T(8,128)(2,1)S(1)} %slice.67), channel_id=1, source_target_pairs={{0,64},{16,80},{32,96},{48,112},{64,128},{80,144},{96,160},{112,17... | collective-permute-start | bytes 786440 | tf_op jit(solution)/shard_map/ppermute | solution.py:29
  88.2 30.4 %collective-permute-start.12 = (bf16[192,2048]{1,0:T(8,128)(2,1)S(1)}, bf16[192,2048]{1,0:T(8,128)(2,1)}, u32[]{:S(2)}, u32[]{:S(2)}) collective-permute-start(bf16[192,2048]{1,0:T(8,128)(2,1)S(1)} %get-tuple-element.24), channel_id=1, source_target_pairs={{0,192},{16,208},{32,224},{48,240},{64,0},{80,16},{96,32},{112,48}... | collective-permute-start | bytes 2359304 | tf_op jit(solution)/shard_map/ppermute | solution.py:29
  90.8 9.3 %copy-start.3 = (bf16[128,2048]{1,0:T(8,128)(2,1)}, bf16[128,2048]{1,0:T(8,128)(2,1)S(1)}, u32[]{:S(2)}) copy-start(bf16[128,2048]{1,0:T(8,128)(2,1)S(1)} %collective-permute-done.19.refs_2_.refs_14_) | copy-start | bytes 1572868
  90.8 27.8 %collective-permute-start.11 = (bf16[192,2048]{1,0:T(8,128)(2,1)S(1)}, bf16[192,2048]{1,0:T(8,128)(2,1)}, u32[]{:S(2)}, u32[]{:S(2)}) collective-permute-start(bf16[192,2048]{1,0:T(8,128)(2,1)S(1)} %get-tuple-element.25), channel_id=1, source_target_pairs={{0,64},{16,80},{32,96},{48,112},{64,128},{80,144},{96,160},{112,17... | collective-permute-start | bytes 2359304 | tf_op jit(solution)/shard_map/ppermute | solution.py:29
  90.9 15.8 %copy-start.4 = (bf16[128,2048]{1,0:T(8,128)(2,1)}, bf16[128,2048]{1,0:T(8,128)(2,1)S(1)}, u32[]{:S(2)}) copy-start(bf16[128,2048]{1,0:T(8,128)(2,1)S(1)} %collective-permute-done.18.refs_1_.refs_13_) | copy-start | bytes 1572868
  90.9 14.0 %collective-permute-start.21 = (bf16[64,2048]{1,0:T(8,128)(2,1)S(1)}, bf16[64,2048]{1,0:T(8,128)(2,1)S(1)}, u32[]{:S(2)}, u32[]{:S(2)}) collective-permute-start(bf16[64,2048]{1,0:T(8,128)(2,1)S(1)} %slice.78), channel_id=1, source_target_pairs={{0,48},{16,0},{32,16},{48,32},{64,112},{80,64},{96,80},{112,96},{1... | collective-permute-start | bytes 786440 | tf_op jit(solution)/shard_map/ppermute | solution.py:29
  95.6 11.0 %copy-start.14 = (bf16[96,2048]{1,0:T(8,128)(2,1)}, bf16[96,2048]{1,0:T(8,128)(2,1)S(1)}, u32[]{:S(2)}) copy-start(bf16[96,2048]{1,0:T(8,128)(2,1)S(1)} %constant_dynamic-update-slice_fusion.refs_6_) | copy-start | bytes 1179652
  95.7 22.9 %collective-permute-start.8 = (bf16[96,2048]{1,0:T(8,128)(2,1)S(1)}, bf16[96,2048]{1,0:T(8,128)(2,1)S(1)}, u32[]{:S(2)}, u32[]{:S(2)}) collective-permute-start(bf16[96,2048]{1,0:T(8,128)(2,1)S(1)} %constant_dynamic-update-slice_fusion.refs_6_), channel_id=1, source_target_pairs={{0,128},{16,144},{32,160},{48,176},{64,192},{80,208},{96,224},{112... | collective-permute-start | bytes 1179656 | tf_op jit(solution)/shard_map/ppermute | solution.py:29
  99.2 11.9 %collective-permute-start.20 = (bf16[64,2048]{1,0:T(8,128)(2,1)S(1)}, bf16[64,2048]{1,0:T(8,128)(2,1)S(1)}, u32[]{:S(2)}, u32[]{:S(2)}) collective-permute-start(bf16[64,2048]{1,0:T(8,128)(2,1)S(1)} %slice.77), channel_id=1, source_target_pairs={{0,16},{16,32},{32,48},{48,0},{64,80},{80,96},{96,112},{112,64},{1... | collective-permute-start | bytes 786440 | tf_op jit(solution)/shard_map/ppermute | solution.py:29
  99.2 19.2 %copy-start.2 = (bf16[8,128,512]{2,1,0:T(8,128)(2,1)}, bf16[8,128,512]{2,1,0:T(8,128)(2,1)S(1)}, u32[]{:S(2)}) copy-start(bf16[8,128,512]{2,1,0:T(8,128)(2,1)S(1)} %constant_dynamic-update-slice_fusion.4.own_ref) | copy-start | bytes 3145732
  104.8 6.3 %copy-start.11 = (bf16[64,2048]{1,0:T(8,128)(2,1)}, bf16[64,2048]{1,0:T(8,128)(2,1)S(1)}, u32[]{:S(2)}) copy-start(bf16[64,2048]{1,0:T(8,128)(2,1)S(1)} %collective-permute-done.21.refs_4_.refs_16_) | copy-start | bytes 786436
  104.8 28.8 %collective-permute-start.31 = (bf16[8,128,512]{2,1,0:T(8,128)(2,1)S(1)}, bf16[8,128,512]{2,1,0:T(8,128)(2,1)}, u32[]{:S(2)}, u32[]{:S(2)}) collective-permute-start(bf16[8,128,512]{2,1,0:T(8,128)(2,1)S(1)} %constant_dynamic-update-slice_fusion.4.own_ref), channel_id=1, source_target_pairs={{0,1},{1,0},{2,3},{3,2},{4,5},{5,4},{6,7},{7,6},{8,9},{9,8},{10,11... | collective-permute-start | bytes 3145736 | tf_op jit(solution)/shard_map/ppermute | solution.py:37
  111.1 0.7 copy-start.12
  118.5 10.6 %copy-start.9 = (f32[8,32,512]{2,1,0:T(8,128)S(1)}, f32[8,32,512]{2,1,0:T(8,128)}, u32[]{:S(2)}) copy-start(f32[8,32,512]{2,1,0:T(8,128)} %get-tuple-element.10) | copy-start | bytes 1572868
  118.5 10.6 %collective-permute-start.22 = (bf16[8,32,512]{2,1,0:T(8,128)(2,1)}, bf16[8,32,512]{2,1,0:T(8,128)(2,1)S(1)}, u32[]{:S(2)}, u32[]{:S(2)}) collective-permute-start(bf16[8,32,512]{2,1,0:T(8,128)(2,1)} %get-tuple-element.11), channel_id=1, source_target_pairs={{0,1},{1,0},{2,3},{3,2},{4,5},{5,4},{6,7},{7,6},{8,9},{9,8},{10,11... | collective-permute-start | bytes 786440 | tf_op jit(solution)/shard_map/ppermute | solution.py:37
  118.6 0.7 copy-start.15
  128.6 15.9 %collective-permute-start.13 = (bf16[8,96,512]{2,1,0:T(8,128)(2,1)}, bf16[8,96,512]{2,1,0:T(8,128)(2,1)}, u32[]{:S(2)}, u32[]{:S(2)}) collective-permute-start(bf16[8,96,512]{2,1,0:T(8,128)(2,1)} %get-tuple-element.9), channel_id=1, source_target_pairs={{0,1},{1,0},{2,3},{3,2},{4,5},{5,4},{6,7},{7,6},{8,9},{9,8},{10,11... | collective-permute-start | bytes 2359304 | tf_op jit(solution)/shard_map/ppermute | solution.py:37
  129.2 15.3 %copy-start.1 = (f32[8,96,512]{2,1,0:T(8,128)S(1)}, f32[8,96,512]{2,1,0:T(8,128)}, u32[]{:S(2)}) copy-start(f32[8,96,512]{2,1,0:T(8,128)} %get-tuple-element.8) | copy-start | bytes 4718596
  129.2 7.8 %collective-permute-start.23 = (bf16[2,32,512]{2,1,0:T(8,128)(2,1)S(1)}, bf16[2,32,512]{2,1,0:T(8,128)(2,1)S(1)}, u32[]{:S(2)}, u32[]{:S(2)}) collective-permute-start(bf16[2,32,512]{2,1,0:T(8,128)(2,1)S(1)} %get-tuple-element.21), channel_id=1, source_target_pairs={{0,2},{1,3},{2,4},{3,5},{4,6},{5,7},{6,0},{7,1},{8,10},{9,11},{10,... | collective-permute-start | bytes 196616 | tf_op jit(solution)/shard_map/ppermute | solution.py:37
  130.9 6.2 %collective-permute-start.24 = (bf16[2,32,512]{2,1,0:T(8,128)(2,1)S(1)}, bf16[2,32,512]{2,1,0:T(8,128)(2,1)S(1)}, u32[]{:S(2)}, u32[]{:S(2)}) collective-permute-start(bf16[2,32,512]{2,1,0:T(8,128)(2,1)S(1)} %get-tuple-element.22), channel_id=1, source_target_pairs={{0,6},{1,7},{2,0},{3,1},{4,2},{5,3},{6,4},{7,5},{8,14},{9,15},{10,... | collective-permute-start | bytes 196616 | tf_op jit(solution)/shard_map/ppermute | solution.py:37
  131.3 5.8 %collective-permute-start.25 = (bf16[2,32,512]{2,1,0:T(8,128)(2,1)S(1)}, bf16[2,32,512]{2,1,0:T(8,128)(2,1)S(1)}, u32[]{:S(2)}, u32[]{:S(2)}) collective-permute-start(bf16[2,32,512]{2,1,0:T(8,128)(2,1)S(1)} %get-tuple-element.23), channel_id=1, source_target_pairs={{0,4},{1,5},{2,6},{3,7},{4,0},{5,1},{6,2},{7,3},{8,12},{9,13},{10,... | collective-permute-start | bytes 196616 | tf_op jit(solution)/shard_map/ppermute | solution.py:37
  137.1 13.0 %collective-permute-start.26 = (bf16[32,512]{1,0:T(8,128)(2,1)S(1)}, bf16[32,512]{1,0:T(8,128)(2,1)S(1)}, u32[]{:S(2)}, u32[]{:S(2)}) collective-permute-start(bf16[32,512]{1,0:T(8,128)(2,1)S(1)} %fusion.22), channel_id=1, source_target_pairs={{0,8},{1,9},{2,10},{3,11},{4,12},{5,13},{6,14},{7,15},{8,0},{9,1},... | collective-permute-start | bytes 98312 | tf_op jit(solution)/shard_map/ppermute | solution.py:37
  145.9 7.9 %collective-permute-start.14 = (bf16[2,96,512]{2,1,0:T(8,128)(2,1)S(1)}, bf16[2,96,512]{2,1,0:T(8,128)(2,1)S(1)}, u32[]{:S(2)}, u32[]{:S(2)}) collective-permute-start(bf16[2,96,512]{2,1,0:T(8,128)(2,1)S(1)} %get-tuple-element.18), channel_id=1, source_target_pairs={{0,2},{1,3},{2,4},{3,5},{4,6},{5,7},{6,0},{7,1},{8,10},{9,11},{10,... | collective-permute-start | bytes 589832 | tf_op jit(solution)/shard_map/ppermute | solution.py:37
  147.4 7.8 %collective-permute-start.15 = (bf16[2,96,512]{2,1,0:T(8,128)(2,1)S(1)}, bf16[2,96,512]{2,1,0:T(8,128)(2,1)S(1)}, u32[]{:S(2)}, u32[]{:S(2)}) collective-permute-start(bf16[2,96,512]{2,1,0:T(8,128)(2,1)S(1)} %get-tuple-element.19), channel_id=1, source_target_pairs={{0,6},{1,7},{2,0},{3,1},{4,2},{5,3},{6,4},{7,5},{8,14},{9,15},{10,... | collective-permute-start | bytes 589832 | tf_op jit(solution)/shard_map/ppermute | solution.py:37
  148.0 9.5 %collective-permute-start.16 = (bf16[2,96,512]{2,1,0:T(8,128)(2,1)S(1)}, bf16[2,96,512]{2,1,0:T(8,128)(2,1)S(1)}, u32[]{:S(2)}, u32[]{:S(2)}) collective-permute-start(bf16[2,96,512]{2,1,0:T(8,128)(2,1)S(1)} %get-tuple-element.20), channel_id=1, source_target_pairs={{0,4},{1,5},{2,6},{3,7},{4,0},{5,1},{6,2},{7,3},{8,12},{9,13},{10,... | collective-permute-start | bytes 589832 | tf_op jit(solution)/shard_map/ppermute | solution.py:37
  157.7 9.2 %collective-permute-start.17 = (bf16[96,512]{1,0:T(8,128)(2,1)S(1)}, bf16[96,512]{1,0:T(8,128)(2,1)S(1)}, u32[]{:S(2)}, u32[]{:S(2)}) collective-permute-start(bf16[96,512]{1,0:T(8,128)(2,1)S(1)} %fusion.17), channel_id=1, source_target_pairs={{0,8},{1,9},{2,10},{3,11},{4,12},{5,13},{6,14},{7,15},{8,0},{9,1},... | collective-permute-start | bytes 294920 | tf_op jit(solution)/shard_map/ppermute | solution.py:37

commit v2 on v0

v2 whole, which is shorter than its diff:
```python
import math

import jax
import jax.numpy as jnp
from jax import lax
from jax.experimental import pallas as pl
from jax.experimental.pallas import tpu as pltpu
from jax.sharding import PartitionSpec as P

ROWS = 128
NZ = 96
NX = ROWS - NZ
VMEM_LIMIT = 16 * 1024 * 1024

ORDER_Z = ((0, 0), (1, 0), (3, 0), (2, 0), (0, 1), (0, 3), (0, 2),
           (1, 1), (1, 3), (3, 1), (3, 3), (2, 2), (1, 2), (2, 1), (3, 2), (2, 3))
ORDER_X = tuple((dx, dz) for dz in (0, 1, 3, 2) for dx in (0, 1, 3, 2))


def gelu_slope(preact):
    h = preact.astype(jnp.float32)
    scale_c = math.sqrt(2.0 / math.pi)
    t = jnp.tanh(scale_c * (h + 0.044715 * h * h * h))
    return 0.5 * (1.0 + t) + 0.5 * h * (1.0 - t * t) * scale_c * (1.0 + 3.0 * 0.044715 * h * h)


def along_row(a, dx, dz, name):
    perm = [(x * 4 + z, (x + dx) % 4 * 4 + (z + dz) % 4) for x in range(4) for z in range(4)]
    with jax.named_scope("ff_" + name):
        return lax.ppermute(a, "row", perm)


def along_col(a, dl, dy, dc, name):
    perm = [
        (l * 8 + y * 2 + c, (l + dl) % 2 * 8 + (y + dy) % 4 * 2 + (c + dc) % 2)
        for l in range(2) for y in range(4) for c in range(2)
    ]
    with jax.named_scope("ff_" + name):
        return lax.ppermute(a, "col", perm)


def swap_y(a, dy, name):
    perm = [(l * 8 + y * 2 + c, l * 8 + (y ^ dy) * 2 + c) for l in range(2) for y in range(4) for c in range(2)]
    with jax.named_scope("ff_" + name):
        return lax.ppermute(a, "col", perm)


def vmem():
    return pl.BlockSpec(memory_space=pltpu.VMEM)


def smem():
    return pl.BlockSpec(memory_space=pltpu.SMEM)


def block_ids(order, x, z):
    return jnp.stack([(x - dx + 4) % 4 * 4 + (z - dz + 4) % 4 for dx, dz in order]).astype(jnp.int32)


def hbm():
    return pl.BlockSpec(memory_space=pl.ANY)


def tied(a, *before):
    return lax.optimization_barrier((a, *before))


def order_inputs(place_z, place_x, own, other):
    def kernel(pz, px, own_ref, other_ref, out_ref, rows_ref):
        low_x = 16 * NZ
        for i in range(16):
            for places, low, size, at in ((pz, 0, NZ, i * NZ), (px, NZ, NX, low_x + i * NX)):
                place = places[i]

                @pl.when(place < 8)
                def _():
                    rows_ref[at:at + size, :] = own_ref[place, low:low + size, :]

                @pl.when(place >= 8)
                def _():
                    rows_ref[at:at + size, :] = other_ref[place - 8, low:low + size, :]

        out_ref[...] = rows_ref[...].T

    d = own.shape[-1]
    return pl.pallas_call(
        kernel,
        out_shape=jax.ShapeDtypeStruct((d, 16 * ROWS), own.dtype),
        in_specs=[smem(), smem(), vmem(), vmem()],
        out_specs=vmem(),
        scratch_shapes=[pltpu.VMEM((16 * ROWS, d), own.dtype)],
        compiler_params=pltpu.CompilerParams(vmem_limit_bytes=VMEM_LIMIT),
        cost_estimate=pl.CostEstimate(flops=0, bytes_accessed=0, transcendentals=0),
    )(place_z, place_x, own, other)


def input_grad_parts(slots, groups, weight, into=None):
    d, hidden = weight.shape
    n = len(groups)
    blocks = [(i, k, per, at) for i, (_, _, size, per, at) in enumerate(groups) for k in range(size // per)]

    def kernel(slot_ref, *refs):
        w_ref = refs[n]
        send_ref, keep_ref = refs[-2:]
        panel = jnp.concatenate(
            [r[low:low + size, :] for r, (_, low, size, _, _) in zip(refs, groups)], axis=0
        )
        sums = lax.dot_general(
            panel, w_ref[...], (((1,), (1,)), ((), ())), preferred_element_type=jnp.float32
        )
        row = 0
        for number, (_, _, per, at) in enumerate(blocks):
            part = sums[row:row + per]
            slot = slot_ref[number]

            @pl.when(slot < 8)
            def _():
                send_ref[slot, at:at + per, :] = part.astype(jnp.bfloat16)

            @pl.when(slot >= 8)
            def _():
                keep_ref[slot - 8, at:at + per, :] = part

            row += per

    extra = [] if into is None else list(into)
    return pl.pallas_call(
        kernel,
        out_shape=(
            jax.ShapeDtypeStruct((8, ROWS, d), jnp.bfloat16),
            jax.ShapeDtypeStruct((8, ROWS, d), jnp.float32),
        ),
        in_specs=[smem()] + [vmem()] * (n + 1 + len(extra)),
        out_specs=(vmem(), vmem()),
        input_output_aliases={n + 2: 0, n + 3: 1} if extra else {},
        compiler_params=pltpu.CompilerParams(vmem_limit_bytes=VMEM_LIMIT),
        cost_estimate=pl.CostEstimate(flops=0, bytes_accessed=0, transcendentals=0),
    )(slots, *[g[0] for g in groups], weight, *extra)


def weight_grad_of(inputs, pieces, tile=512):
    d, rows = inputs.shape
    hidden = pieces[0][0].shape[1]
    n, tiles = len(pieces), pieces[0][0].shape[1] // tile

    def kernel(in_ref, *refs):
        out_ref, right, result, sem, out_sem = refs[n:]

        def copies(j):
            at, found = 0, []
            for i, (_, low, size) in enumerate(pieces):
                found.append(pltpu.make_async_copy(
                    refs[i].at[pl.ds(low, size), pl.ds(j * tile, tile)],
                    right.at[j % 2, pl.ds(at, size), :],
                    sem.at[j % 2, i],
                ))
                at += size
            return found

        def leave(j):
            return pltpu.make_async_copy(
                result.at[j], out_ref.at[:, pl.ds(j * tile, tile)], out_sem.at[j]
            )

        for copy in copies(0):
            copy.start()
        for j in range(tiles):
            if j + 1 < tiles:
                for copy in copies(j + 1):
                    copy.start()
            for copy in copies(j):
                copy.wait()
            result[j] = lax.dot_general(
                in_ref[...], right[j % 2], (((1,), (0,)), ((), ())), preferred_element_type=jnp.float32
            ).astype(jnp.bfloat16)
            leave(j).start()
        for j in range(tiles):
            leave(j).wait()

    return pl.pallas_call(
        kernel,
        out_shape=jax.ShapeDtypeStruct((d, hidden), jnp.bfloat16),
        in_specs=[vmem()] + [hbm()] * n,
        out_specs=hbm(),
        scratch_shapes=[
            pltpu.VMEM((2, rows, tile), jnp.bfloat16),
            pltpu.VMEM((tiles, d, tile), jnp.bfloat16),
            pltpu.SemaphoreType.DMA((2, n)),
            pltpu.SemaphoreType.DMA((tiles,)),
        ],
        compiler_params=pltpu.CompilerParams(vmem_limit_bytes=VMEM_LIMIT),
        cost_estimate=pl.CostEstimate(
            flops=2 * 2048 * d * hidden, bytes_accessed=12 * 1024 * 1024, transcendentals=0
        ),
    )(inputs, *[p for p, _, _ in pieces])


def over_cores(place, keep, got):
    _, rows, d = keep.shape

    def kernel(place_ref, keep_ref, got_ref, *outs):
        y = place_ref[1]
        for i, dy in enumerate((1, 3, 2, 0)):
            for q in range(2):
                slot = q * 4 + (y + dy) % 4
                outs[i][q] = (keep_ref[slot] + got_ref[slot].astype(jnp.float32)).astype(outs[i].dtype)

    return pl.pallas_call(
        kernel,
        out_shape=[jax.ShapeDtypeStruct((2, rows, d), jnp.bfloat16)] * 3
        + [jax.ShapeDtypeStruct((2, rows, d), jnp.float32)],
        in_specs=[smem(), vmem(), vmem()],
        out_specs=[vmem()] * 4,
        compiler_params=pltpu.CompilerParams(vmem_limit_bytes=VMEM_LIMIT),
        cost_estimate=pl.CostEstimate(flops=0, bytes_accessed=0, transcendentals=0),
    )(place, keep, got)


def over_y(place, own, terms):
    _, rows, d = own.shape

    def kernel(place_ref, own_ref, *refs):
        def total(i):
            found = own_ref[i]
            for ref in refs[:3]:
                found = found + ref[i].astype(jnp.float32)
            return found

        l = place_ref[0]
        refs[3][...] = total(1 - l).astype(jnp.bfloat16)
        refs[4][...] = total(l)

    return pl.pallas_call(
        kernel,
        out_shape=[jax.ShapeDtypeStruct((rows, d), t) for t in (jnp.bfloat16, jnp.float32)],
        in_specs=[smem()] + [vmem()] * 4,
        out_specs=[vmem()] * 2,
        compiler_params=pltpu.CompilerParams(vmem_limit_bytes=VMEM_LIMIT),
        cost_estimate=pl.CostEstimate(flops=0, bytes_accessed=0, transcendentals=0),
    )(place, own, *terms)


def local(inputs, preact, out_grad, weight):
    row, col = lax.axis_index("row"), lax.axis_index("col")
    x, z = row // 4, row % 4
    l, y, c = col // 8, col // 2 % 4, col % 2

    def grad_of(p, g):
        return (g.astype(jnp.float32) * gelu_slope(p)).astype(jnp.bfloat16)

    grad = grad_of(preact, out_grad)
    half = NZ // 32 * 16
    ids_z, ids_x = block_ids(ORDER_Z, x, z), block_ids(ORDER_X, x, z)

    def place(ids):
        return (c ^ ids % 2) * 8 + (y ^ ids // 2 % 4) * 2 + (l ^ ids // 8)

    def whole(*arrays):
        return [(a, 0, a.shape[0]) for a in arrays]

    slots_z = jnp.where(ids_z % 2 == c, 8, 0) + ids_z // 2
    slots_x = jnp.where(ids_x % 2 == c, 8, 0) + ids_x // 2

    def terms(into, z_blocks, z_pieces, x_blocks=None, x_pieces=()):
        groups = [(*p, min(NZ, p[2]), 0) for p in z_pieces] + [(*p, NX, NZ) for p in x_pieces]
        slots = slots_z[z_blocks] if z_pieces else slots_x[x_blocks]
        if z_pieces and x_pieces:
            slots = jnp.concatenate([slots, slots_x[x_blocks]])
        return input_grad_parts(slots, groups, weight, into)


    gz = grad[:NZ]
    a1, a3 = along_row(grad, 1, 0, "G1"), along_row(grad, 3, 0, "G3")
    pair = jnp.stack([inputs, along_col(inputs, 1, 0, 0, "Il")])
    gz, pair = tied(gz, pair)
    b1, b3 = along_row(gz, 0, 1, "Z1"), along_row(gz, 0, 3, "Z3")
    i1 = swap_y(pair, 1, "I1")
    u = along_row(a1[:ROWS // 2], 1, 0, "Gr1")
    v = along_row(a3[ROWS // 2:], 3, 0, "Gr3")
    b1, b3, a1, a3 = tied(b1, b3, a1, a3)
    s = along_row(b1[:half], 0, 1, "Zr1")
    t = along_row(b3[half:], 0, 3, "Zr3")
    b13 = jnp.concatenate([b1, b3], axis=0)
    b13, u, v = tied(b13, u, v)
    f1, f3 = along_row(b13, 1, 0, "F1"), along_row(b13, 3, 0, "F3")
    near = jnp.concatenate([pair, i1])
    own = jnp.concatenate([near, swap_y(near, 2, "I2")])
    a2 = jnp.concatenate([u, v[:NZ - ROWS // 2]], axis=0)
    into = terms(None, slice(0, 4), [(gz, 0, NZ), (a1, 0, NZ), (a3, 0, NZ), *whole(a2)])
    xs = jnp.concatenate([grad[NZ:], a1[NZ:], a3[NZ:], v[NZ - ROWS // 2:]], axis=0)
    xs, s, t, own, *into = tied(xs, s, t, own, *into)
    e1, e3 = along_row(xs, 0, 1, "X1"), along_row(xs, 0, 3, "X3")
    b2 = jnp.concatenate([s, t], axis=0)
    p2 = along_row(b2, 2, 0, "P2")
    p1 = along_row(jnp.concatenate([b2, f1[:NZ]], axis=0), 1, 0, "P1")
    p3 = along_row(jnp.concatenate([b2, f3[NZ:]], axis=0), 3, 0, "P3")
    into = terms(into, slice(4, 11), whole(b1, b3, b2, f1, f3))
    e1, e3, f1, f3, *into = tied(e1, e3, f1, f3, *into)
    q1 = along_row(e1[:2 * NX], 0, 1, "Xr1")
    q3 = along_row(e3[2 * NX:], 0, 3, "Xr3")
    own, p1, p3 = tied(own, p1, p3)
    other = along_col(own, 0, 0, 1, "Ic")
    into = terms(into, None, [], slice(0, 12), whole(xs, e1, e3))
    turned = order_inputs(place(ids_z), place(ids_x), own, other)
    p1, p3, *into = tied(p1, p3, *into)
    send, keep = terms(into, slice(11, 16), whole(p2, p1, p3), slice(12, 16), whole(q1, q3))

    at = jnp.stack([l, y]).astype(jnp.int32)
    got = along_col(send, 0, 0, 1, "Rc")
    got, turned = tied(got, turned)
    *parts, rest = over_cores(at, keep, got)
    got = [along_col(t, 0, dy, 0, f"Ry{dy}") for t, dy in zip(parts, (1, 3, 2))]
    turned, rest = tied(turned, rest)
    pieces = [(gz, 0, NZ), (a1, 0, NZ), (a3, 0, NZ), *whole(a2, b1, b3, b2, f1, f3, p2, p1, p3, xs, e1, e3, q1, q3)]
    weight_grad = weight_grad_of(turned, pieces)
    *got, weight_grad = tied(*got, weight_grad)
    leaving, staying = over_y(at, rest, got)
    last = along_col(leaving, 1, 0, 0, "Rl")
    input_grad = (staying + last.astype(jnp.float32)).astype(jnp.bfloat16)
    return (input_grad, weight_grad)


def solution(mesh):
    in_specs = (P("col", "row"), P("row", "col"), P("row", "col"), P("row", "col"))
    out_specs = (P("col", "row"), P("row", "col"))
    return jax.shard_map(local, mesh=mesh, in_specs=in_specs, out_specs=out_specs, check_vma=False)
```

time: 248 us -> 113 us (0.46); the launches traced: 243 us -> 112 us
  waiting for transfers between devices: 202 us -> 47.2 us
  starting transfers between devices: 0.12 us -> 41.8 us
  matrix products: 19.4 us -> 0 us
  Pallas kernels: 0 us -> 18.4 us
  between operations: 13.8 us -> 1.04 us
  local copies, waits for them, and re-layouts: 3.92 us -> 0.68 us
    all_gather x2 -> x0, waiting for transfers between devices: 147 us -> none  [the longest x1 106 us: local(): all_grad = lax.all_gather(grad, 'row', axis=0, tiled=True)]
    reduce_scatter x1 -> x0, waiting for transfers between devices: 54.3 us -> none  [local(): lax.psum_scatter(times_weight(all_grad, weight), 'col', scatter_dimension...]
    ppermute x0 -> x26, waiting for transfers between devices: none -> 47.2 us  [the longest x17 39.2 us: along_row(): return lax.ppermute(a, 'row', perm)]
    ppermute x0 -> x26, starting transfers between devices: none -> 41.8 us  [the longest x17 30.5 us: along_row(): return lax.ppermute(a, 'row', perm)]
    dot_general x2 -> x0, matrix products: 19.4 us -> none  [the longest x1 9.85 us: inner_rows(): lax.dot_general(left, right, (((0,), (0,)), ((), ())), preferred_element_...]
    pallas_call x0 -> x8, Pallas kernels: none -> 18.4 us  [the longest x4 7.82 us: input_grad_parts(): pl.pallas_call(kernel, out_shape=(jax.ShapeDtypeStruct((8, ROWS, d), jnp....]
    unnamed x3 -> x9, local copies, waits for them, and re-layouts: 3.92 us -> 0.03 us
  transfers between devices with their start and end apart: 3 -> 26, of which waited for: 3 -> 15; matrix products, arithmetic and copies ran while one was open for 10% -> 3% of each run, Pallas kernels for 0% -> 15%
where the time goes in v2:
time: 113 us; the launch traced here: 112 us
  waiting for transfers between devices  47.2 us (42%)
  starting transfers between devices  41.8 us (37%)
  Pallas kernels  18.4 us (16%)
  other arithmetic  3.3 us (3%)
    ppermute x17, waiting for transfers between devices, along_row(): return lax.ppermute(a, 'row', perm)  39.2 us
    ppermute x17, starting transfers between devices, along_row(): return lax.ppermute(a, 'row', perm)  30.5 us
    ppermute x7, starting transfers between devices, along_col(): return lax.ppermute(a, 'col', perm)  8.54 us
    ppermute x7, waiting for transfers between devices, along_col(): return lax.ppermute(a, 'col', perm)  8.04 us
    pallas_call x4, Pallas kernels, input_grad_parts(): pl.pallas_call(kernel, out_shape=(jax.ShapeDtypeStruct((8, ROWS, d), jnp....  7.82 us
    pallas_call x1, Pallas kernels, weight_grad_of(): pl.pallas_call(kernel, out_shape=jax.ShapeDtypeStruct((d, hidden), jnp.bf...  7.49 us
    ppermute x2, starting transfers between devices, swap_y(): return lax.ppermute(a, 'col', perm)  2.83 us
  transfers between devices with their start and end apart: 26, of which 15 were waited for; matrix products, arithmetic and copies ran while one was open for 3% of the time, Pallas kernels for 15%

profile of v2, /device:TPU:8, one launch (start us, length us, event | category | flops | bytes accessed | tf_op | source)
XLA Modules:
  0.0 112.4 jit_solution(2705071631977449720)
XLA Ops:
  0.6 2.0 %collective-permute-start = (bf16[128,512]{1,0:T(8,128)(2,1)}, bf16[128,512]{1,0:T(8,128)(2,1)S(1)}, u32[]{:S(2)}, u32[]{:S(2)}) collective-permute-start(bf16[128,512]{1,0:T(8,128)(2,1)} %param.4), channel_id=1, source_target_pairs={{0,8},{1,9},{2,10},{3,11},{4,12},{5,13},{6,14},{7,15},{8,0},{9,1},... | collective-permute-start | bytes 393224 | tf_op jit(solution)/shard_map/ff_Il/ppermute | solution.py:39
  2.6 1.9 %fusion.7 = bf16[128,2048]{1,0:T(8,128)(2,1)S(1)} fusion(bf16[128,2048]{1,0:T(8,128)(2,1)} %param.5, bf16[128,2048]{1,0:T(8,128)(2,1)} %param.6), kind=kLoop, calls=%fused_computation.14 | loop fusion | flops 5505024 | bytes 1572864 | tf_op jit(solution)/shard_map/convert_element_type | solution.py:249
  4.6 2.8 %collective-permute-start.4 = (bf16[128,2048]{1,0:T(8,128)(2,1)S(1)}, bf16[128,2048]{1,0:T(8,128)(2,1)S(1)}, u32[]{:S(2)}, u32[]{:S(2)}) collective-permute-start(bf16[128,2048]{1,0:T(8,128)(2,1)S(1)} %fusion.7), channel_id=1, source_target_pairs={{0,192},{16,208},{32,224},{48,240},{64,0},{80,16},{96,32},{112,48}... | collective-permute-start | bytes 1572872 | tf_op jit(solution)/shard_map/ff_G3/ppermute | solution.py:30
  7.5 0.1 stack.107
  7.6 5.5 %collective-permute-start.2 = (bf16[96,2048]{1,0:T(8,128)(2,1)S(1)}, bf16[96,2048]{1,0:T(8,128)(2,1)S(1)}, u32[]{:S(2)}, u32[]{:S(2)}) collective-permute-start(bf16[96,2048]{1,0:T(8,128)(2,1)S(1)} %slice.77.refs_0_), channel_id=1, source_target_pairs={{0,48},{16,0},{32,16},{48,32},{64,112},{80,64},{96,80},{112,96},{1... | collective-permute-start | bytes 1179656 | tf_op jit(solution)/shard_map/ff_Z3/ppermute | solution.py:30
  13.1 0.0 collective-permute-start.1
  13.1 0.4 collective-permute-start.9
  13.6 0.1 stack.108
  13.7 4.6 %collective-permute-done.4.refs_2_ = bf16[128,2048]{1,0:T(8,128)(2,1)S(1)} collective-permute-done((bf16[128,2048]{1,0:T(8,128)(2,1)S(1)}, bf16[128,2048]{1,0:T(8,128)(2,1)S(1)}, u32[]{:S(2)}, u32[]{:S(2)}) %collective-permute-start.4) | collective-permute-done | bytes 524320 | tf_op jit(solution)/shard_map/ff_G3/ppermute | solution.py:30
  18.3 3.8 %collective-permute-start.6 = (bf16[64,2048]{1,0:T(8,128)(2,1)S(1)}, bf16[64,2048]{1,0:T(8,128)(2,1)S(1)}, u32[]{:S(2)}, u32[]{:S(2)}) collective-permute-start(bf16[64,2048]{1,0:T(8,128)(2,1)S(1)} %slice.79), channel_id=1, source_target_pairs={{0,192},{16,208},{32,224},{48,240},{64,0},{80,16},{96,32},{112,48}... | collective-permute-start | bytes 786440 | tf_op jit(solution)/shard_map/ff_Gr3/ppermute | solution.py:30
  22.1 0.0 collective-permute-done.3.refs_1_
  22.1 0.1 collective-permute-start.5
  22.3 2.4 %collective-permute-start.10 = (bf16[4,128,512]{2,1,0:T(8,128)(2,1)S(1)}, bf16[4,128,512]{2,1,0:T(8,128)(2,1)S(1)}, u32[]{:S(2)}, u32[]{:S(2)}) collective-permute-start(bf16[4,128,512]{2,1,0:T(8,128)(2,1)S(1)} %pad_maximum_fusion.6), channel_id=1, source_target_pairs={{0,4},{1,5},{2,6},{3,7},{4,0},{5,1},{6,2},{7,3},{8,12},{9,13},{10,... | collective-permute-start | bytes 1572872 | tf_op jit(solution)/shard_map/ff_I2/ppermute | solution.py:45
  24.7 3.1 %collective-permute-done.2.refs_1_.refs_5_ = bf16[96,2048]{1,0:T(8,128)(2,1)S(1)} collective-permute-done((bf16[96,2048]{1,0:T(8,128)(2,1)S(1)}, bf16[96,2048]{1,0:T(8,128)(2,1)S(1)}, u32[]{:S(2)}, u32[]{:S(2)}) %collective-permute-start.2) | collective-permute-done | bytes 393248 | tf_op jit(solution)/shard_map/ff_Z3/ppermute | solution.py:30
  27.8 5.4 %collective-permute-done.1.refs_0_.refs_4_ = bf16[96,2048]{1,0:T(8,128)(2,1)S(1)} collective-permute-done((bf16[96,2048]{1,0:T(8,128)(2,1)S(1)}, bf16[96,2048]{1,0:T(8,128)(2,1)S(1)}, u32[]{:S(2)}, u32[]{:S(2)}) %collective-permute-start.1) | collective-permute-done | bytes 393248 | tf_op jit(solution)/shard_map/ff_Z1/ppermute | solution.py:30
  33.3 0.1 collective-permute-start.8
  33.4 0.0 slice-start
  33.4 2.9 %collective-permute-start.7 = (bf16[48,2048]{1,0:T(8,128)(2,1)S(1)}, bf16[48,2048]{1,0:T(8,128)(2,1)S(1)}, u32[]{:S(2)}, u32[]{:S(2)}) collective-permute-start(bf16[48,2048]{1,0:T(8,128)(2,1)S(1)} %slice.66), channel_id=1, source_target_pairs={{0,16},{16,32},{32,48},{48,0},{64,80},{80,96},{96,112},{112,64},{1... | collective-permute-start | bytes 589832 | tf_op jit(solution)/shard_map/ff_Zr1/ppermute | solution.py:30
  36.3 0.1 pad_maximum_fusion.1
  36.3 0.0 copy-start
  36.4 3.0 %collective-permute-start.14 = (bf16[192,2048]{1,0:T(8,128)(2,1)S(1)}, bf16[192,2048]{1,0:T(8,128)(2,1)S(1)}, u32[]{:S(2)}, u32[]{:S(2)}) collective-permute-start(bf16[192,2048]{1,0:T(8,128)(2,1)S(1)} %pad_maximum_fusion.1), channel_id=1, source_target_pairs={{0,192},{16,208},{32,224},{48,240},{64,0},{80,16},{96,32},{112,48}... | collective-permute-start | bytes 2359304 | tf_op jit(solution)/shard_map/ff_F3/ppermute | solution.py:30
  39.5 1.6 %shard_map.59 = (bf16[8,128,512]{2,1,0:T(8,128)(2,1)S(1)}, f32[8,128,512]{2,1,0:T(8,128)S(1)}) custom-call(s32[4]{0:T(128)S(1)} %bitcast.22, bf16[96,2048]{1,0:T(8,128)(2,1)S(1)} %slice.77.refs_0_, bf16[128,2048]{1,0:T(8,128)(2,1)S(1)} %collective-permute-done.3.refs_1_, bf16[128,2048]{1,0:T(8,128)(2,1)S(1)} %copy-done.2, ...), custom_call_target="tpu_custom_call" | custom-call | tf_op jit(solution)/shard_map/pallas_call | solution.py:127
  41.2 0.1 pad_maximum_fusion.own_ref
  41.3 2.7 %collective-permute-done.8 = bf16[48,2048]{1,0:T(8,128)(2,1)S(1)} collective-permute-done((bf16[48,2048]{1,0:T(8,128)(2,1)S(1)}, bf16[48,2048]{1,0:T(8,128)(2,1)S(1)}, u32[]{:S(2)}, u32[]{:S(2)}) %collective-permute-start.8) | collective-permute-done | bytes 196640 | tf_op jit(solution)/shard_map/ff_Zr3/ppermute | solution.py:30
  44.0 1.3 %collective-permute-done.7 = bf16[48,2048]{1,0:T(8,128)(2,1)S(1)} collective-permute-done((bf16[48,2048]{1,0:T(8,128)(2,1)S(1)}, bf16[48,2048]{1,0:T(8,128)(2,1)S(1)}, u32[]{:S(2)}, u32[]{:S(2)}) %collective-permute-start.7) | collective-permute-done | bytes 196640 | tf_op jit(solution)/shard_map/ff_Zr1/ppermute | solution.py:30
  45.3 0.0 collective-permute-start.17
  45.3 2.9 %collective-permute-start.16 = (bf16[128,2048]{1,0:T(8,128)(2,1)S(1)}, bf16[128,2048]{1,0:T(8,128)(2,1)S(1)}, u32[]{:S(2)}, u32[]{:S(2)}) collective-permute-start(bf16[128,2048]{1,0:T(8,128)(2,1)S(1)} %pad_maximum_fusion.5.refs_0_.refs_12_), channel_id=1, source_target_pairs={{0,16},{16,32},{32,48},{48,0},{64,80},{80,96},{96,112},{112,64},{1... | collective-permute-start | bytes 1572872 | tf_op jit(solution)/shard_map/ff_X1/ppermute | solution.py:30
  48.3 4.8 %collective-permute-done.14.refs_4_.refs_8_ = bf16[192,2048]{1,0:T(8,128)(2,1)S(1)} collective-permute-done((bf16[192,2048]{1,0:T(8,128)(2,1)S(1)}, bf16[192,2048]{1,0:T(8,128)(2,1)S(1)}, u32[]{:S(2)}, u32[]{:S(2)}) %collective-permute-start.14) | collective-permute-done | bytes 786464 | tf_op jit(solution)/shard_map/ff_F3/ppermute | solution.py:30
  53.1 3.4 %collective-permute-done.12.refs_3_.refs_7_ = bf16[192,2048]{1,0:T(8,128)(2,1)S(1)} collective-permute-done((bf16[192,2048]{1,0:T(8,128)(2,1)S(1)}, bf16[192,2048]{1,0:T(8,128)(2,1)S(1)}, u32[]{:S(2)}, u32[]{:S(2)}) %collective-permute-start.12) | collective-permute-done | bytes 786464 | tf_op jit(solution)/shard_map/ff_F1/ppermute | solution.py:30
  56.5 0.2 pad_maximum_fusion.4
  56.7 0.4 collective-permute-start.15
  57.1 1.7 %collective-permute-start.13 = (bf16[192,2048]{1,0:T(8,128)(2,1)S(1)}, bf16[192,2048]{1,0:T(8,128)(2,1)S(1)}, u32[]{:S(2)}, u32[]{:S(2)}) collective-permute-start(bf16[192,2048]{1,0:T(8,128)(2,1)S(1)} %get-tuple-element.107), channel_id=1, source_target_pairs={{0,64},{16,80},{32,96},{48,112},{64,128},{80,144},{96,160},{112,17... | collective-permute-start | bytes 2359304 | tf_op jit(solution)/shard_map/ff_P1/ppermute | solution.py:30
  58.8 0.1 collective-permute-start.11
  59.0 0.1 slice.73.slot_ref
  59.0 0.1 slice.57
  59.1 2.3 %shard_map.60 = (bf16[8,128,512]{2,1,0:T(8,128)(2,1)S(1)}, f32[8,128,512]{2,1,0:T(8,128)S(1)}) custom-call(s32[7]{0:T(128)S(1)} %slice.73.slot_ref, bf16[96,2048]{1,0:T(8,128)(2,1)S(1)} %collective-permute-done.1.refs_0_.refs_4_, bf16[96,2048]{1,0:T(8,128)(2,1)S(1)} %collective-permute-done.2.refs_1_.refs_5_, ...), custom_call_target="tpu_custom_call", output_to_operand_aliasing={{0}: (7, {}), {1}: (8, {})} | custom-call | tf_op jit(solution)/shard_map/pallas_call | solution.py:127
  61.4 3.1 %collective-permute-done.17.refs_2_.refs_14_ = bf16[128,2048]{1,0:T(8,128)(2,1)S(1)} collective-permute-done((bf16[128,2048]{1,0:T(8,128)(2,1)S(1)}, bf16[128,2048]{1,0:T(8,128)(2,1)S(1)}, u32[]{:S(2)}, u32[]{:S(2)}) %collective-permute-start.17) | collective-permute-done | bytes 524320 | tf_op jit(solution)/shard_map/ff_X3/ppermute | solution.py:30
  64.5 0.0 collective-permute-done.16.refs_1_.refs_13_
  64.5 6.7 %collective-permute-start.19 = (bf16[64,2048]{1,0:T(8,128)(2,1)S(1)}, bf16[64,2048]{1,0:T(8,128)(2,1)S(1)}, u32[]{:S(2)}, u32[]{:S(2)}) collective-permute-start(bf16[64,2048]{1,0:T(8,128)(2,1)S(1)} %slice.75), channel_id=1, source_target_pairs={{0,48},{16,0},{32,16},{48,32},{64,112},{80,64},{96,80},{112,96},{1... | collective-permute-start | bytes 786440 | tf_op jit(solution)/shard_map/ff_Xr3/ppermute | solution.py:30
  71.3 0.4 collective-permute-start.18
  71.7 0.1 slice.58
  71.8 0.1 pad_add_fusion.1.slot_ref
  71.9 1.7 %shard_map.61 = (bf16[8,128,512]{2,1,0:T(8,128)(2,1)S(1)}, f32[8,128,512]{2,1,0:T(8,128)S(1)}) custom-call(s32[12]{0:T(128)S(1)} %bitcast.23, bf16[128,2048]{1,0:T(8,128)(2,1)S(1)} %pad_maximum_fusion.5.refs_0_.refs_12_, bf16[128,2048]{1,0:T(8,128)(2,1)S(1)} %collective-permute-done.16.refs_1_.refs_13_, ...), custom_call_target="tpu_custom_call", output_to_operand_aliasing={{0}: (5, {}), {1}: (6, {})} | custom-call | tf_op jit(solution)/shard_map/pallas_call | solution.py:127
  73.6 3.4 %collective-permute-done.15.refs_2_.refs_11_ = bf16[192,2048]{1,0:T(8,128)(2,1)S(1)} collective-permute-done((bf16[192,2048]{1,0:T(8,128)(2,1)S(1)}, bf16[192,2048]{1,0:T(8,128)(2,1)S(1)}, u32[]{:S(2)}, u32[]{:S(2)}) %collective-permute-start.15) | collective-permute-done | bytes 786464 | tf_op jit(solution)/shard_map/ff_P3/ppermute | solution.py:30
  77.0 3.4 %collective-permute-done.13.refs_1_.refs_10_ = bf16[192,2048]{1,0:T(8,128)(2,1)S(1)} collective-permute-done((bf16[192,2048]{1,0:T(8,128)(2,1)S(1)}, bf16[192,2048]{1,0:T(8,128)(2,1)S(1)}, u32[]{:S(2)}, u32[]{:S(2)}) %collective-permute-start.13) | collective-permute-done | bytes 786464 | tf_op jit(solution)/shard_map/ff_P1/ppermute | solution.py:30
  80.4 0.0 collective-permute-start.21
  80.4 0.0 collective-permute-done.11.refs_0_.refs_9_
  80.4 1.2 %collective-permute-done.19.refs_4_.refs_16_ = bf16[64,2048]{1,0:T(8,128)(2,1)S(1)} collective-permute-done((bf16[64,2048]{1,0:T(8,128)(2,1)S(1)}, bf16[64,2048]{1,0:T(8,128)(2,1)S(1)}, u32[]{:S(2)}, u32[]{:S(2)}) %collective-permute-start.19) | collective-permute-done | bytes 262176 | tf_op jit(solution)/shard_map/ff_Xr3/ppermute | solution.py:30
  81.6 2.7 %collective-permute-done.18.refs_3_.refs_15_ = bf16[64,2048]{1,0:T(8,128)(2,1)S(1)} collective-permute-done((bf16[64,2048]{1,0:T(8,128)(2,1)S(1)}, bf16[64,2048]{1,0:T(8,128)(2,1)S(1)}, u32[]{:S(2)}, u32[]{:S(2)}) %collective-permute-start.18) | collective-permute-done | bytes 262176 | tf_op jit(solution)/shard_map/ff_Xr1/ppermute | solution.py:30
  84.3 2.2 %shard_map.62 = (bf16[8,128,512]{2,1,0:T(8,128)(2,1)S(1)}, f32[8,128,512]{2,1,0:T(8,128)S(1)}) custom-call(s32[9]{0:T(128)S(1)} %pad_add_fusion.1.slot_ref, bf16[96,2048]{1,0:T(8,128)(2,1)S(1)} %collective-permute-done.11.refs_0_.refs_9_, ...), custom_call_target="tpu_custom_call", output_to_operand_aliasing={{0}: (7, {}), {1}: (8, {})} | custom-call | tf_op jit(solution)/shard_map/pallas_call | solution.py:127
  86.5 0.1 collective-permute-start.20
  86.6 0.1 pad_add_fusion.place_ref
  86.7 1.7 %shard_map.63.in_ref = bf16[512,2048]{1,0:T(8,128)(2,1)S(1)} custom-call(s32[16]{0:T(128)S(1)} %get-tuple-element.104.pz, s32[16]{0:T(128)S(1)} %get-tuple-element.102.px, bf16[8,128,512]{2,1,0:T(8,128)(2,1)S(1)} %pad_maximum_fusion.own_ref, bf16[8,128,512]{2,1,0:T(8,128)(2,1)S(1)} %collective-permute-done.21.other_ref), custom_call_target="tpu_custom_call" | custom-call | tf_op jit(solution)/shard_map/pallas_call | solution.py:86
  88.4 0.9 collective-permute-done.20.got_ref
  89.3 0.7 shard_map.64
  90.0 1.6 %collective-permute-start.22 = (bf16[2,128,512]{2,1,0:T(8,128)(2,1)S(1)}, bf16[2,128,512]{2,1,0:T(8,128)(2,1)S(1)}, u32[]{:S(2)}, u32[]{:S(2)}) collective-permute-start(bf16[2,128,512]{2,1,0:T(8,128)(2,1)S(1)} %get-tuple-element.90), channel_id=1, source_target_pairs={{0,2},{1,3},{2,4},{3,5},{4,6},{5,7},{6,0},{7,1},{8,10},{9,11},{10,... | collective-permute-start | bytes 786440 | tf_op jit(solution)/shard_map/ff_Ry1/ppermute | solution.py:39
  91.6 0.5 collective-permute-start.23
  92.1 2.3 %collective-permute-start.24 = (bf16[2,128,512]{2,1,0:T(8,128)(2,1)S(1)}, bf16[2,128,512]{2,1,0:T(8,128)(2,1)S(1)}, u32[]{:S(2)}, u32[]{:S(2)}) collective-permute-start(bf16[2,128,512]{2,1,0:T(8,128)(2,1)S(1)} %get-tuple-element.92), channel_id=1, source_target_pairs={{0,4},{1,5},{2,6},{3,7},{4,0},{5,1},{6,2},{7,3},{8,12},{9,13},{10,... | collective-permute-start | bytes 786440 | tf_op jit(solution)/shard_map/ff_Ry2/ppermute | solution.py:39
  94.4 7.5 %shard_map.65 = bf16[512,2048]{1,0:T(8,128)(2,1)} custom-call(bf16[512,2048]{1,0:T(8,128)(2,1)S(1)} %shard_map.63.in_ref, bf16[96,2048]{1,0:T(8,128)(2,1)S(1)} %slice.77.refs_0_, bf16[128,2048]{1,0:T(8,128)(2,1)S(1)} %collective-permute-done.3.refs_1_, bf16[128,2048]{1,0:T(8,128)(2,1)S(1)} %copy-done.2, bf16[96,2048]{1,0:T(8,128)(2,1)S(1)} %pad_maximum_fusion.7.refs_3_, ...), custom_call_target="tpu_custom_call" | custom-call | flops 4294967296 | bytes 12582912 | tf_op jit(solution)/shard_map/pallas_call | solution.py:180
  101.9 4.1 %collective-permute-done.24.refs_2_ = bf16[2,128,512]{2,1,0:T(8,128)(2,1)S(1)} collective-permute-done((bf16[2,128,512]{2,1,0:T(8,128)(2,1)S(1)}, bf16[2,128,512]{2,1,0:T(8,128)(2,1)S(1)}, u32[]{:S(2)}, u32[]{:S(2)}) %collective-permute-start.24) | collective-permute-done | bytes 262176 | tf_op jit(solution)/shard_map/ff_Ry2/ppermute | solution.py:39
  106.0 0.7 shard_map.66
  106.7 2.0 %collective-permute-start.25 = (bf16[128,512]{1,0:T(8,128)(2,1)S(1)}, bf16[128,512]{1,0:T(8,128)(2,1)S(1)}, u32[]{:S(2)}, u32[]{:S(2)}) collective-permute-start(bf16[128,512]{1,0:T(8,128)(2,1)S(1)} %get-tuple-element.100), channel_id=1, source_target_pairs={{0,8},{1,9},{2,10},{3,11},{4,12},{5,13},{6,14},{7,15},{8,0},{9,1},... | collective-permute-start | bytes 393224 | tf_op jit(solution)/shard_map/ff_Rl/ppermute | solution.py:39
  108.7 3.0 %collective-permute-done.25 = bf16[128,512]{1,0:T(8,128)(2,1)S(1)} collective-permute-done((bf16[128,512]{1,0:T(8,128)(2,1)S(1)}, bf16[128,512]{1,0:T(8,128)(2,1)S(1)}, u32[]{:S(2)}, u32[]{:S(2)}) %collective-permute-start.25) | collective-permute-done | bytes 131104 | tf_op jit(solution)/shard_map/ff_Rl/ppermute | solution.py:39
  111.8 0.7 add_convert_fusion
  (40 shorter events, 0.5 us)
Async XLA Ops:
  0.6 7.0 %copy-start.3 = (bf16[128,512]{1,0:T(8,128)(2,1)S(1)}, bf16[128,512]{1,0:T(8,128)(2,1)}, u32[]{:S(2)}) copy-start(bf16[128,512]{1,0:T(8,128)(2,1)} %param.4) | copy-start | bytes 393220
  0.6 6.9 %collective-permute-start = (bf16[128,512]{1,0:T(8,128)(2,1)}, bf16[128,512]{1,0:T(8,128)(2,1)S(1)}, u32[]{:S(2)}, u32[]{:S(2)}) collective-permute-start(bf16[128,512]{1,0:T(8,128)(2,1)} %param.4), channel_id=1, source_target_pairs={{0,8},{1,9},{2,10},{3,11},{4,12},{5,13},{6,14},{7,15},{8,0},{9,1},... | collective-permute-start | bytes 393224 | tf_op jit(solution)/shard_map/ff_Il/ppermute | solution.py:39
  4.6 13.7 %collective-permute-start.4 = (bf16[128,2048]{1,0:T(8,128)(2,1)S(1)}, bf16[128,2048]{1,0:T(8,128)(2,1)S(1)}, u32[]{:S(2)}, u32[]{:S(2)}) collective-permute-start(bf16[128,2048]{1,0:T(8,128)(2,1)S(1)} %fusion.7), channel_id=1, source_target_pairs={{0,192},{16,208},{32,224},{48,240},{64,0},{80,16},{96,32},{112,48}... | collective-permute-start | bytes 1572872 | tf_op jit(solution)/shard_map/ff_G3/ppermute | solution.py:30
  7.4 14.7 %collective-permute-start.3 = (bf16[128,2048]{1,0:T(8,128)(2,1)S(1)}, bf16[128,2048]{1,0:T(8,128)(2,1)S(1)}, u32[]{:S(2)}, u32[]{:S(2)}) collective-permute-start(bf16[128,2048]{1,0:T(8,128)(2,1)S(1)} %fusion.7), channel_id=1, source_target_pairs={{0,64},{16,80},{32,96},{48,112},{64,128},{80,144},{96,160},{112,17... | collective-permute-start | bytes 1572872 | tf_op jit(solution)/shard_map/ff_G1/ppermute | solution.py:30
  7.6 20.2 %collective-permute-start.2 = (bf16[96,2048]{1,0:T(8,128)(2,1)S(1)}, bf16[96,2048]{1,0:T(8,128)(2,1)S(1)}, u32[]{:S(2)}, u32[]{:S(2)}) collective-permute-start(bf16[96,2048]{1,0:T(8,128)(2,1)S(1)} %slice.77.refs_0_), channel_id=1, source_target_pairs={{0,48},{16,0},{32,16},{48,32},{64,112},{80,64},{96,80},{112,96},{1... | collective-permute-start | bytes 1179656 | tf_op jit(solution)/shard_map/ff_Z3/ppermute | solution.py:30
  13.1 20.1 %collective-permute-start.1 = (bf16[96,2048]{1,0:T(8,128)(2,1)S(1)}, bf16[96,2048]{1,0:T(8,128)(2,1)S(1)}, u32[]{:S(2)}, u32[]{:S(2)}) collective-permute-start(bf16[96,2048]{1,0:T(8,128)(2,1)S(1)} %slice.77.refs_0_), channel_id=1, source_target_pairs={{0,16},{16,32},{32,48},{48,0},{64,80},{80,96},{96,112},{112,64},{1... | collective-permute-start | bytes 1179656 | tf_op jit(solution)/shard_map/ff_Z1/ppermute | solution.py:30
  13.1 9.1 %collective-permute-start.9 = (bf16[2,128,512]{2,1,0:T(8,128)(2,1)S(1)}, bf16[2,128,512]{2,1,0:T(8,128)(2,1)S(1)}, u32[]{:S(2)}, u32[]{:S(2)}) collective-permute-start(bf16[2,128,512]{2,1,0:T(8,128)(2,1)S(1)} %pad_maximum_fusion.8), channel_id=1, source_target_pairs={{0,2},{1,3},{2,0},{3,1},{4,6},{5,7},{6,4},{7,5},{8,10},{9,11},{10,... | collective-permute-start | bytes 786440 | tf_op jit(solution)/shard_map/ff_I1/ppermute | solution.py:45
  18.3 14.9 %copy-start.1 = (bf16[128,2048]{1,0:T(8,128)(2,1)}, bf16[128,2048]{1,0:T(8,128)(2,1)S(1)}, u32[]{:S(2)}) copy-start(bf16[128,2048]{1,0:T(8,128)(2,1)S(1)} %collective-permute-done.4.refs_2_) | copy-start | bytes 1572868
  18.3 18.0 %collective-permute-start.6 = (bf16[64,2048]{1,0:T(8,128)(2,1)S(1)}, bf16[64,2048]{1,0:T(8,128)(2,1)S(1)}, u32[]{:S(2)}, u32[]{:S(2)}) collective-permute-start(bf16[64,2048]{1,0:T(8,128)(2,1)S(1)} %slice.79), channel_id=1, source_target_pairs={{0,192},{16,208},{32,224},{48,240},{64,0},{80,16},{96,32},{112,48}... | collective-permute-start | bytes 786440 | tf_op jit(solution)/shard_map/ff_Gr3/ppermute | solution.py:30
  22.1 14.2 %collective-permute-start.5 = (bf16[64,2048]{1,0:T(8,128)(2,1)S(1)}, bf16[64,2048]{1,0:T(8,128)(2,1)S(1)}, u32[]{:S(2)}, u32[]{:S(2)}) collective-permute-start(bf16[64,2048]{1,0:T(8,128)(2,1)S(1)} %slice.78), channel_id=1, source_target_pairs={{0,64},{16,80},{32,96},{48,112},{64,128},{80,144},{96,160},{112,17... | collective-permute-start | bytes 786440 | tf_op jit(solution)/shard_map/ff_Gr1/ppermute | solution.py:30
  22.3 18.9 %collective-permute-start.10 = (bf16[4,128,512]{2,1,0:T(8,128)(2,1)S(1)}, bf16[4,128,512]{2,1,0:T(8,128)(2,1)S(1)}, u32[]{:S(2)}, u32[]{:S(2)}) collective-permute-start(bf16[4,128,512]{2,1,0:T(8,128)(2,1)S(1)} %pad_maximum_fusion.6), channel_id=1, source_target_pairs={{0,4},{1,5},{2,6},{3,7},{4,0},{5,1},{6,2},{7,3},{8,12},{9,13},{10,... | collective-permute-start | bytes 1572872 | tf_op jit(solution)/shard_map/ff_I2/ppermute | solution.py:45
  33.3 10.8 %collective-permute-start.8 = (bf16[48,2048]{1,0:T(8,128)(2,1)S(1)}, bf16[48,2048]{1,0:T(8,128)(2,1)S(1)}, u32[]{:S(2)}, u32[]{:S(2)}) collective-permute-start(bf16[48,2048]{1,0:T(8,128)(2,1)S(1)} %slice.67), channel_id=1, source_target_pairs={{0,48},{16,0},{32,16},{48,32},{64,112},{80,64},{96,80},{112,96},{1... | collective-permute-start | bytes 589832 | tf_op jit(solution)/shard_map/ff_Zr3/ppermute | solution.py:30
  33.4 6.1 %slice-start = ((bf16[128,2048]{1,0:T(8,128)(2,1)}), bf16[32,2048]{1,0:T(8,128)(2,1)S(1)}, s32[]{:S(2)}) async-start(bf16[128,2048]{1,0:T(8,128)(2,1)} %copy-done.1), calls=%async_computation | async-start | bytes 262144 | tf_op jit(solution)/shard_map/slice | solution.py:290
  33.4 12.0 %collective-permute-start.7 = (bf16[48,2048]{1,0:T(8,128)(2,1)S(1)}, bf16[48,2048]{1,0:T(8,128)(2,1)S(1)}, u32[]{:S(2)}, u32[]{:S(2)}) collective-permute-start(bf16[48,2048]{1,0:T(8,128)(2,1)S(1)} %slice.66), channel_id=1, source_target_pairs={{0,16},{16,32},{32,48},{48,0},{64,80},{80,96},{96,112},{112,64},{1... | collective-permute-start | bytes 589832 | tf_op jit(solution)/shard_map/ff_Zr1/ppermute | solution.py:30
  36.3 3.2 %copy-start.2 = (bf16[128,2048]{1,0:T(8,128)(2,1)S(1)}, bf16[128,2048]{1,0:T(8,128)(2,1)}, u32[]{:S(2)}) copy-start(bf16[128,2048]{1,0:T(8,128)(2,1)} %copy-done.1) | copy-start | bytes 1572868
  36.3 3.2 %copy-start = (bf16[512,2048]{1,0:T(8,128)(2,1)S(1)}, bf16[512,2048]{1,0:T(8,128)(2,1)}, u32[]{:S(2)}) copy-start(bf16[512,2048]{1,0:T(8,128)(2,1)} %refs_5_.3) | copy-start | bytes 6291460
  36.4 16.7 %collective-permute-start.14 = (bf16[192,2048]{1,0:T(8,128)(2,1)S(1)}, bf16[192,2048]{1,0:T(8,128)(2,1)S(1)}, u32[]{:S(2)}, u32[]{:S(2)}) collective-permute-start(bf16[192,2048]{1,0:T(8,128)(2,1)S(1)} %pad_maximum_fusion.1), channel_id=1, source_target_pairs={{0,192},{16,208},{32,224},{48,240},{64,0},{80,16},{96,32},{112,48}... | collective-permute-start | bytes 2359304 | tf_op jit(solution)/shard_map/ff_F3/ppermute | solution.py:30
  39.4 17.1 %collective-permute-start.12 = (bf16[192,2048]{1,0:T(8,128)(2,1)S(1)}, bf16[192,2048]{1,0:T(8,128)(2,1)S(1)}, u32[]{:S(2)}, u32[]{:S(2)}) collective-permute-start(bf16[192,2048]{1,0:T(8,128)(2,1)S(1)} %pad_maximum_fusion.1), channel_id=1, source_target_pairs={{0,64},{16,80},{32,96},{48,112},{64,128},{80,144},{96,160},{112,17... | collective-permute-start | bytes 2359304 | tf_op jit(solution)/shard_map/ff_F1/ppermute | solution.py:30
  45.3 19.1 %collective-permute-start.17 = (bf16[128,2048]{1,0:T(8,128)(2,1)S(1)}, bf16[128,2048]{1,0:T(8,128)(2,1)S(1)}, u32[]{:S(2)}, u32[]{:S(2)}) collective-permute-start(bf16[128,2048]{1,0:T(8,128)(2,1)S(1)} %pad_maximum_fusion.5.refs_0_.refs_12_), channel_id=1, source_target_pairs={{0,48},{16,0},{32,16},{48,32},{64,112},{80,64},{96,80},{112,96},{1... | collective-permute-start | bytes 1572872 | tf_op jit(solution)/shard_map/ff_X3/ppermute | solution.py:30
  45.3 19.1 %collective-permute-start.16 = (bf16[128,2048]{1,0:T(8,128)(2,1)S(1)}, bf16[128,2048]{1,0:T(8,128)(2,1)S(1)}, u32[]{:S(2)}, u32[]{:S(2)}) collective-permute-start(bf16[128,2048]{1,0:T(8,128)(2,1)S(1)} %pad_maximum_fusion.5.refs_0_.refs_12_), channel_id=1, source_target_pairs={{0,16},{16,32},{32,48},{48,0},{64,80},{80,96},{96,112},{112,64},{1... | collective-permute-start | bytes 1572872 | tf_op jit(solution)/shard_map/ff_X1/ppermute | solution.py:30
  56.7 20.3 %collective-permute-start.15 = (bf16[192,2048]{1,0:T(8,128)(2,1)S(1)}, bf16[192,2048]{1,0:T(8,128)(2,1)S(1)}, u32[]{:S(2)}, u32[]{:S(2)}) collective-permute-start(bf16[192,2048]{1,0:T(8,128)(2,1)S(1)} %get-tuple-element.106), channel_id=1, source_target_pairs={{0,192},{16,208},{32,224},{48,240},{64,0},{80,16},{96,32},{112,48}... | collective-permute-start | bytes 2359304 | tf_op jit(solution)/shard_map/ff_P3/ppermute | solution.py:30
  57.1 23.3 %collective-permute-start.13 = (bf16[192,2048]{1,0:T(8,128)(2,1)S(1)}, bf16[192,2048]{1,0:T(8,128)(2,1)S(1)}, u32[]{:S(2)}, u32[]{:S(2)}) collective-permute-start(bf16[192,2048]{1,0:T(8,128)(2,1)S(1)} %get-tuple-element.107), channel_id=1, source_target_pairs={{0,64},{16,80},{32,96},{48,112},{64,128},{80,144},{96,160},{112,17... | collective-permute-start | bytes 2359304 | tf_op jit(solution)/shard_map/ff_P1/ppermute | solution.py:30
  58.8 21.6 %collective-permute-start.11 = (bf16[96,2048]{1,0:T(8,128)(2,1)S(1)}, bf16[96,2048]{1,0:T(8,128)(2,1)S(1)}, u32[]{:S(2)}, u32[]{:S(2)}) collective-permute-start(bf16[96,2048]{1,0:T(8,128)(2,1)S(1)} %constant_dynamic-update-slice_fusion.refs_2_.refs_6_), channel_id=1, source_target_pairs={{0,128},{16,144},{32,160},{48,176},{64,192},{80,208},{96,224},{112... | collective-permute-start | bytes 1179656 | tf_op jit(solution)/shard_map/ff_P2/ppermute | solution.py:30
  64.5 17.1 %collective-permute-start.19 = (bf16[64,2048]{1,0:T(8,128)(2,1)S(1)}, bf16[64,2048]{1,0:T(8,128)(2,1)S(1)}, u32[]{:S(2)}, u32[]{:S(2)}) collective-permute-start(bf16[64,2048]{1,0:T(8,128)(2,1)S(1)} %slice.75), channel_id=1, source_target_pairs={{0,48},{16,0},{32,16},{48,32},{64,112},{80,64},{96,80},{112,96},{1... | collective-permute-start | bytes 786440 | tf_op jit(solution)/shard_map/ff_Xr3/ppermute | solution.py:30
  71.3 13.0 %collective-permute-start.18 = (bf16[64,2048]{1,0:T(8,128)(2,1)S(1)}, bf16[64,2048]{1,0:T(8,128)(2,1)S(1)}, u32[]{:S(2)}, u32[]{:S(2)}) collective-permute-start(bf16[64,2048]{1,0:T(8,128)(2,1)S(1)} %slice.74), channel_id=1, source_target_pairs={{0,16},{16,32},{32,48},{48,0},{64,80},{80,96},{96,112},{112,64},{1... | collective-permute-start | bytes 786440 | tf_op jit(solution)/shard_map/ff_Xr1/ppermute | solution.py:30
  80.4 6.3 %collective-permute-start.21 = (bf16[8,128,512]{2,1,0:T(8,128)(2,1)S(1)}, bf16[8,128,512]{2,1,0:T(8,128)(2,1)S(1)}, u32[]{:S(2)}, u32[]{:S(2)}) collective-permute-start(bf16[8,128,512]{2,1,0:T(8,128)(2,1)S(1)} %pad_maximum_fusion.own_ref), channel_id=1, source_target_pairs={{0,1},{1,0},{2,3},{3,2},{4,5},{5,4},{6,7},{7,6},{8,9},{9,8},{10,11... | collective-permute-start | bytes 3145736 | tf_op jit(solution)/shard_map/ff_Ic/ppermute | solution.py:39
  86.5 2.7 %collective-permute-start.20 = (bf16[8,128,512]{2,1,0:T(8,128)(2,1)S(1)}, bf16[8,128,512]{2,1,0:T(8,128)(2,1)S(1)}, u32[]{:S(2)}, u32[]{:S(2)}) collective-permute-start(bf16[8,128,512]{2,1,0:T(8,128)(2,1)S(1)} %get-tuple-element.83), channel_id=1, source_target_pairs={{0,1},{1,0},{2,3},{3,2},{4,5},{5,4},{6,7},{7,6},{8,9},{9,8},{10,11... | collective-permute-start | bytes 3145736 | tf_op jit(solution)/shard_map/ff_Rc/ppermute | solution.py:39
  90.0 11.9 %collective-permute-start.22 = (bf16[2,128,512]{2,1,0:T(8,128)(2,1)S(1)}, bf16[2,128,512]{2,1,0:T(8,128)(2,1)S(1)}, u32[]{:S(2)}, u32[]{:S(2)}) collective-permute-start(bf16[2,128,512]{2,1,0:T(8,128)(2,1)S(1)} %get-tuple-element.90), channel_id=1, source_target_pairs={{0,2},{1,3},{2,4},{3,5},{4,6},{5,7},{6,0},{7,1},{8,10},{9,11},{10,... | collective-permute-start | bytes 786440 | tf_op jit(solution)/shard_map/ff_Ry1/ppermute | solution.py:39
  91.6 10.3 %collective-permute-start.23 = (bf16[2,128,512]{2,1,0:T(8,128)(2,1)S(1)}, bf16[2,128,512]{2,1,0:T(8,128)(2,1)S(1)}, u32[]{:S(2)}, u32[]{:S(2)}) collective-permute-start(bf16[2,128,512]{2,1,0:T(8,128)(2,1)S(1)} %get-tuple-element.91), channel_id=1, source_target_pairs={{0,6},{1,7},{2,0},{3,1},{4,2},{5,3},{6,4},{7,5},{8,14},{9,15},{10,... | collective-permute-start | bytes 786440 | tf_op jit(solution)/shard_map/ff_Ry3/ppermute | solution.py:39
  92.1 13.9 %collective-permute-start.24 = (bf16[2,128,512]{2,1,0:T(8,128)(2,1)S(1)}, bf16[2,128,512]{2,1,0:T(8,128)(2,1)S(1)}, u32[]{:S(2)}, u32[]{:S(2)}) collective-permute-start(bf16[2,128,512]{2,1,0:T(8,128)(2,1)S(1)} %get-tuple-element.92), channel_id=1, source_target_pairs={{0,4},{1,5},{2,6},{3,7},{4,0},{5,1},{6,2},{7,3},{8,12},{9,13},{10,... | collective-permute-start | bytes 786440 | tf_op jit(solution)/shard_map/ff_Ry2/ppermute | solution.py:39
  106.7 5.1 %collective-permute-start.25 = (bf16[128,512]{1,0:T(8,128)(2,1)S(1)}, bf16[128,512]{1,0:T(8,128)(2,1)S(1)}, u32[]{:S(2)}, u32[]{:S(2)}) collective-permute-start(bf16[128,512]{1,0:T(8,128)(2,1)S(1)} %get-tuple-element.100), channel_id=1, source_target_pairs={{0,8},{1,9},{2,10},{3,11},{4,12},{5,13},{6,14},{7,15},{8,0},{9,1},... | collective-permute-start | bytes 393224 | tf_op jit(solution)/shard_map/ff_Rl/ppermute | solution.py:39

commit v3 on v2

--- a/solution.py
+++ b/solution.py
@@ -272,11 +272,11 @@
     gz = grad[:NZ]
     a1, a3 = along_row(grad, 1, 0, "G1"), along_row(grad, 3, 0, "G3")
     pair = jnp.stack([inputs, along_col(inputs, 1, 0, 0, "Il")])
-    gz, pair = tied(gz, pair)
     b1, b3 = along_row(gz, 0, 1, "Z1"), along_row(gz, 0, 3, "Z3")
-    i1 = swap_y(pair, 1, "I1")
     u = along_row(a1[:ROWS // 2], 1, 0, "Gr1")
     v = along_row(a3[ROWS // 2:], 3, 0, "Gr3")
+    pair, a1 = tied(pair, a1)
+    i1 = swap_y(pair, 1, "I1")
     b1, b3, a1, a3 = tied(b1, b3, a1, a3)
     s = along_row(b1[:half], 0, 1, "Zr1")
     t = along_row(b3[half:], 0, 3, "Zr3")
@@ -288,7 +288,7 @@
     a2 = jnp.concatenate([u, v[:NZ - ROWS // 2]], axis=0)
     into = terms(None, slice(0, 4), [(gz, 0, NZ), (a1, 0, NZ), (a3, 0, NZ), *whole(a2)])
     xs = jnp.concatenate([grad[NZ:], a1[NZ:], a3[NZ:], v[NZ - ROWS // 2:]], axis=0)
-    xs, s, t, own, *into = tied(xs, s, t, own, *into)
+    xs, s, t, *into = tied(xs, s, t, *into)
     e1, e3 = along_row(xs, 0, 1, "X1"), along_row(xs, 0, 3, "X3")
     b2 = jnp.concatenate([s, t], axis=0)
     p2 = along_row(b2, 2, 0, "P2")

time: 113 us -> 113 us (level)
  waiting for transfers between devices: 47.2 us -> 49 us
  starting transfers between devices: 41.8 us -> 40.1 us
    ppermute x7, waiting for transfers between devices: 8.04 us -> 11.4 us  [along_col(): return lax.ppermute(a, 'col', perm)]
    ppermute x7, starting transfers between devices: 8.54 us -> 6.12 us  [along_col(): return lax.ppermute(a, 'col', perm)]
    ppermute x17, waiting for transfers between devices: 39.2 us -> 37.7 us  [along_row(): return lax.ppermute(a, 'row', perm)]
  transfers between devices with their start and end apart: 26 -> 26, of which waited for: 15 -> 14; matrix products, arithmetic and copies ran while one was open for 3% -> 1% of each run, Pallas kernels for 15% -> 15%
where the time goes in v3:
time: 113 us; the launch traced here: 112 us
  waiting for transfers between devices  49 us (43%)
  starting transfers between devices  40.1 us (35%)
  Pallas kernels  18.4 us (16%)
  other arithmetic  3.36 us (3%)
    ppermute x17, waiting for transfers between devices, along_row(): return lax.ppermute(a, 'row', perm)  37.7 us
    ppermute x17, starting transfers between devices, along_row(): return lax.ppermute(a, 'row', perm)  31.2 us
    ppermute x7, waiting for transfers between devices, along_col(): return lax.ppermute(a, 'col', perm)  11.4 us
    pallas_call x4, Pallas kernels, input_grad_parts(): pl.pallas_call(kernel, out_shape=(jax.ShapeDtypeStruct((8, ROWS, d), jnp....  7.84 us
    pallas_call x1, Pallas kernels, weight_grad_of(): pl.pallas_call(kernel, out_shape=jax.ShapeDtypeStruct((d, hidden), jnp.bf...  7.49 us
    ppermute x7, starting transfers between devices, along_col(): return lax.ppermute(a, 'col', perm)  6.12 us
    ppermute x2, starting transfers between devices, swap_y(): return lax.ppermute(a, 'col', perm)  2.71 us
  transfers between devices with their start and end apart: 26, of which 14 were waited for; matrix products, arithmetic and copies ran while one was open for 1% of the time, Pallas kernels for 15%

profile of v3, /device:TPU:8, one launch (start us, length us, event | category | flops | bytes accessed | tf_op | source)
XLA Modules:
  0.0 112.5 jit_solution(9261565364394401274)
XLA Ops:
  0.6 2.0 %fusion.7 = bf16[128,2048]{1,0:T(8,128)(2,1)S(1)} fusion(bf16[128,2048]{1,0:T(8,128)(2,1)} %param.5, bf16[128,2048]{1,0:T(8,128)(2,1)} %param.6), kind=kLoop, calls=%fused_computation.14 | loop fusion | flops 5505024 | bytes 1572864 | tf_op jit(solution)/shard_map/convert_element_type | solution.py:249
  2.6 6.4 %collective-permute-start.1 = (bf16[96,2048]{1,0:T(8,128)(2,1)S(1)}, bf16[96,2048]{1,0:T(8,128)(2,1)S(1)}, u32[]{:S(2)}, u32[]{:S(2)}) collective-permute-start(bf16[96,2048]{1,0:T(8,128)(2,1)S(1)} %slice.77.refs_0_), channel_id=1, source_target_pairs={{0,48},{16,0},{32,16},{48,32},{64,112},{80,64},{96,80},{112,96},{1... | collective-permute-start | bytes 1179656 | tf_op jit(solution)/shard_map/ff_Z3/ppermute | solution.py:30
  9.0 0.0 collective-permute-start
  9.0 2.8 %collective-permute-start.4 = (bf16[128,2048]{1,0:T(8,128)(2,1)S(1)}, bf16[128,2048]{1,0:T(8,128)(2,1)S(1)}, u32[]{:S(2)}, u32[]{:S(2)}) collective-permute-start(bf16[128,2048]{1,0:T(8,128)(2,1)S(1)} %fusion.7), channel_id=1, source_target_pairs={{0,192},{16,208},{32,224},{48,240},{64,0},{80,16},{96,32},{112,48}... | collective-permute-start | bytes 1572872 | tf_op jit(solution)/shard_map/ff_G3/ppermute | solution.py:30
  11.8 0.0 collective-permute-start.3
  11.8 1.0 collective-permute-start.2
  12.8 0.1 stack.107
  12.9 0.1 stack.108
  13.1 0.1 slice.73.slot_ref
  13.2 9.5 %collective-permute-done.4.refs_2_ = bf16[128,2048]{1,0:T(8,128)(2,1)S(1)} collective-permute-done((bf16[128,2048]{1,0:T(8,128)(2,1)S(1)}, bf16[128,2048]{1,0:T(8,128)(2,1)S(1)}, u32[]{:S(2)}, u32[]{:S(2)}) %collective-permute-start.4) | collective-permute-done | bytes 524320 | tf_op jit(solution)/shard_map/ff_G3/ppermute | solution.py:30
  22.7 3.8 %collective-permute-start.6 = (bf16[64,2048]{1,0:T(8,128)(2,1)S(1)}, bf16[64,2048]{1,0:T(8,128)(2,1)S(1)}, u32[]{:S(2)}, u32[]{:S(2)}) collective-permute-start(bf16[64,2048]{1,0:T(8,128)(2,1)S(1)} %slice.79), channel_id=1, source_target_pairs={{0,192},{16,208},{32,224},{48,240},{64,0},{80,16},{96,32},{112,48}... | collective-permute-start | bytes 786440 | tf_op jit(solution)/shard_map/ff_Gr3/ppermute | solution.py:30
  26.5 0.1 collective-permute-start.5
  26.6 2.1 %collective-permute-done.2 = bf16[128,512]{1,0:T(8,128)(2,1)S(1)} collective-permute-done((bf16[128,512]{1,0:T(8,128)(2,1)S(1)}, bf16[128,512]{1,0:T(8,128)(2,1)S(1)}, u32[]{:S(2)}, u32[]{:S(2)}) %collective-permute-start.2) | collective-permute-done | bytes 131104 | tf_op jit(solution)/shard_map/ff_Il/ppermute | solution.py:39
  28.7 0.0 collective-permute-done.1.refs_1_.refs_5_
  28.7 1.9 %collective-permute-done.refs_0_.refs_4_ = bf16[96,2048]{1,0:T(8,128)(2,1)S(1)} collective-permute-done((bf16[96,2048]{1,0:T(8,128)(2,1)S(1)}, bf16[96,2048]{1,0:T(8,128)(2,1)S(1)}, u32[]{:S(2)}, u32[]{:S(2)}) %collective-permute-start) | collective-permute-done | bytes 393248 | tf_op jit(solution)/shard_map/ff_Z1/ppermute | solution.py:30
  30.7 0.0 copy-start
  30.7 1.4 %collective-permute-start.8 = (bf16[48,2048]{1,0:T(8,128)(2,1)S(1)}, bf16[48,2048]{1,0:T(8,128)(2,1)S(1)}, u32[]{:S(2)}, u32[]{:S(2)}) collective-permute-start(bf16[48,2048]{1,0:T(8,128)(2,1)S(1)} %slice.67), channel_id=1, source_target_pairs={{0,48},{16,0},{32,16},{48,32},{64,112},{80,64},{96,80},{112,96},{1... | collective-permute-start | bytes 589832 | tf_op jit(solution)/shard_map/ff_Zr3/ppermute | solution.py:30
  32.2 1.6 %collective-permute-start.7 = (bf16[48,2048]{1,0:T(8,128)(2,1)S(1)}, bf16[48,2048]{1,0:T(8,128)(2,1)S(1)}, u32[]{:S(2)}, u32[]{:S(2)}) collective-permute-start(bf16[48,2048]{1,0:T(8,128)(2,1)S(1)} %slice.66), channel_id=1, source_target_pairs={{0,16},{16,32},{32,48},{48,0},{64,80},{80,96},{96,112},{112,64},{1... | collective-permute-start | bytes 589832 | tf_op jit(solution)/shard_map/ff_Zr1/ppermute | solution.py:30
  33.7 0.4 collective-permute-start.10
  34.2 0.1 pad_maximum_fusion.1
  34.3 0.1 collective-permute-done.5
  34.4 2.7 %collective-permute-start.14 = (bf16[192,2048]{1,0:T(8,128)(2,1)S(1)}, bf16[192,2048]{1,0:T(8,128)(2,1)S(1)}, u32[]{:S(2)}, u32[]{:S(2)}) collective-permute-start(bf16[192,2048]{1,0:T(8,128)(2,1)S(1)} %pad_maximum_fusion.1), channel_id=1, source_target_pairs={{0,192},{16,208},{32,224},{48,240},{64,0},{80,16},{96,32},{112,48}... | collective-permute-start | bytes 2359304 | tf_op jit(solution)/shard_map/ff_F3/ppermute | solution.py:30
  37.1 0.0 collective-permute-start.12
  37.2 1.6 %shard_map.59 = (bf16[8,128,512]{2,1,0:T(8,128)(2,1)S(1)}, f32[8,128,512]{2,1,0:T(8,128)S(1)}) custom-call(s32[4]{0:T(128)S(1)} %bitcast.22, bf16[96,2048]{1,0:T(8,128)(2,1)S(1)} %slice.77.refs_0_, bf16[128,2048]{1,0:T(8,128)(2,1)S(1)} %collective-permute-done.3.refs_1_, bf16[128,2048]{1,0:T(8,128)(2,1)S(1)} %collective-permute-done.4.refs_2_, ...), custom_call_target="tpu_custom_call" | custom-call | tf_op jit(solution)/shard_map/pallas_call | solution.py:127
  38.9 0.0 collective-permute-done.8
  38.9 5.4 %collective-permute-done.7 = bf16[48,2048]{1,0:T(8,128)(2,1)S(1)} collective-permute-done((bf16[48,2048]{1,0:T(8,128)(2,1)S(1)}, bf16[48,2048]{1,0:T(8,128)(2,1)S(1)}, u32[]{:S(2)}, u32[]{:S(2)}) %collective-permute-start.7) | collective-permute-done | bytes 196640 | tf_op jit(solution)/shard_map/ff_Zr1/ppermute | solution.py:30
  44.3 2.9 %collective-permute-start.16 = (bf16[128,2048]{1,0:T(8,128)(2,1)S(1)}, bf16[128,2048]{1,0:T(8,128)(2,1)S(1)}, u32[]{:S(2)}, u32[]{:S(2)}) collective-permute-start(bf16[128,2048]{1,0:T(8,128)(2,1)S(1)} %pad_maximum_fusion.5.refs_0_.refs_12_), channel_id=1, source_target_pairs={{0,16},{16,32},{32,48},{48,0},{64,80},{80,96},{96,112},{112,64},{1... | collective-permute-start | bytes 1572872 | tf_op jit(solution)/shard_map/ff_X1/ppermute | solution.py:30
  47.2 2.3 %collective-permute-start.11 = (bf16[4,128,512]{2,1,0:T(8,128)(2,1)S(1)}, bf16[4,128,512]{2,1,0:T(8,128)(2,1)S(1)}, u32[]{:S(2)}, u32[]{:S(2)}) collective-permute-start(bf16[4,128,512]{2,1,0:T(8,128)(2,1)S(1)} %pad_maximum_fusion.6), channel_id=1, source_target_pairs={{0,4},{1,5},{2,6},{3,7},{4,0},{5,1},{6,2},{7,3},{8,12},{9,13},{10,... | collective-permute-start | bytes 1572872 | tf_op jit(solution)/shard_map/ff_I2/ppermute | solution.py:45
  49.5 1.7 %collective-permute-done.14.refs_4_.refs_8_ = bf16[192,2048]{1,0:T(8,128)(2,1)S(1)} collective-permute-done((bf16[192,2048]{1,0:T(8,128)(2,1)S(1)}, bf16[192,2048]{1,0:T(8,128)(2,1)S(1)}, u32[]{:S(2)}, u32[]{:S(2)}) %collective-permute-start.14) | collective-permute-done | bytes 786464 | tf_op jit(solution)/shard_map/ff_F3/ppermute | solution.py:30
  51.3 3.1 %collective-permute-done.12.refs_3_.refs_7_ = bf16[192,2048]{1,0:T(8,128)(2,1)S(1)} collective-permute-done((bf16[192,2048]{1,0:T(8,128)(2,1)S(1)}, bf16[192,2048]{1,0:T(8,128)(2,1)S(1)}, u32[]{:S(2)}, u32[]{:S(2)}) %collective-permute-start.12) | collective-permute-done | bytes 786464 | tf_op jit(solution)/shard_map/ff_F1/ppermute | solution.py:30
  54.5 0.2 pad_maximum_fusion.4
  54.7 0.4 collective-permute-start.15
  55.1 1.7 %collective-permute-start.13 = (bf16[192,2048]{1,0:T(8,128)(2,1)S(1)}, bf16[192,2048]{1,0:T(8,128)(2,1)S(1)}, u32[]{:S(2)}, u32[]{:S(2)}) collective-permute-start(bf16[192,2048]{1,0:T(8,128)(2,1)S(1)} %get-tuple-element.105), channel_id=1, source_target_pairs={{0,64},{16,80},{32,96},{48,112},{64,128},{80,144},{96,160},{112,17... | collective-permute-start | bytes 2359304 | tf_op jit(solution)/shard_map/ff_P1/ppermute | solution.py:30
  56.8 2.3 %shard_map.60 = (bf16[8,128,512]{2,1,0:T(8,128)(2,1)S(1)}, f32[8,128,512]{2,1,0:T(8,128)S(1)}) custom-call(s32[7]{0:T(128)S(1)} %slice.73.slot_ref, bf16[96,2048]{1,0:T(8,128)(2,1)S(1)} %collective-permute-done.refs_0_.refs_4_, bf16[96,2048]{1,0:T(8,128)(2,1)S(1)} %collective-permute-done.1.refs_1_.refs_5_, ...), custom_call_target="tpu_custom_call", output_to_operand_aliasing={{0}: (7, {}), {1}: (8, {})} | custom-call | tf_op jit(solution)/shard_map/pallas_call | solution.py:127
  59.1 6.6 %collective-permute-done.17.refs_2_.refs_14_ = bf16[128,2048]{1,0:T(8,128)(2,1)S(1)} collective-permute-done((bf16[128,2048]{1,0:T(8,128)(2,1)S(1)}, bf16[128,2048]{1,0:T(8,128)(2,1)S(1)}, u32[]{:S(2)}, u32[]{:S(2)}) %collective-permute-start.17) | collective-permute-done | bytes 524320 | tf_op jit(solution)/shard_map/ff_X3/ppermute | solution.py:30
  65.7 4.5 %collective-permute-start.9 = (bf16[96,2048]{1,0:T(8,128)(2,1)S(1)}, bf16[96,2048]{1,0:T(8,128)(2,1)S(1)}, u32[]{:S(2)}, u32[]{:S(2)}) collective-permute-start(bf16[96,2048]{1,0:T(8,128)(2,1)S(1)} %constant_dynamic-update-slice_fusion.refs_2_.refs_6_), channel_id=1, source_target_pairs={{0,128},{16,144},{32,160},{48,176},{64,192},{80,208},{96,224},{112... | collective-permute-start | bytes 1179656 | tf_op jit(solution)/shard_map/ff_P2/ppermute | solution.py:30
  70.2 0.0 collective-permute-done.16.refs_1_.refs_13_
  70.2 0.1 collective-permute-start.19
  70.3 0.0 collective-permute-done.11
  70.3 2.9 %collective-permute-start.18 = (bf16[64,2048]{1,0:T(8,128)(2,1)S(1)}, bf16[64,2048]{1,0:T(8,128)(2,1)S(1)}, u32[]{:S(2)}, u32[]{:S(2)}) collective-permute-start(bf16[64,2048]{1,0:T(8,128)(2,1)S(1)} %slice.74), channel_id=1, source_target_pairs={{0,16},{16,32},{32,48},{48,0},{64,80},{80,96},{96,112},{112,64},{1... | collective-permute-start | bytes 786440 | tf_op jit(solution)/shard_map/ff_Xr1/ppermute | solution.py:30
  73.3 0.1 slice.57
  73.3 0.1 slice.58
  73.4 0.1 pad_add_fusion.1.slot_ref
  73.5 0.1 pad_maximum_fusion.own_ref
  73.6 1.7 %shard_map.61 = (bf16[8,128,512]{2,1,0:T(8,128)(2,1)S(1)}, f32[8,128,512]{2,1,0:T(8,128)S(1)}) custom-call(s32[12]{0:T(128)S(1)} %bitcast.23, bf16[128,2048]{1,0:T(8,128)(2,1)S(1)} %pad_maximum_fusion.5.refs_0_.refs_12_, bf16[128,2048]{1,0:T(8,128)(2,1)S(1)} %collective-permute-done.16.refs_1_.refs_13_, ...), custom_call_target="tpu_custom_call", output_to_operand_aliasing={{0}: (5, {}), {1}: (6, {})} | custom-call | tf_op jit(solution)/shard_map/pallas_call | solution.py:127
  75.3 0.0 collective-permute-done.15.refs_2_.refs_11_
  75.3 4.6 %collective-permute-done.13.refs_1_.refs_10_ = bf16[192,2048]{1,0:T(8,128)(2,1)S(1)} collective-permute-done((bf16[192,2048]{1,0:T(8,128)(2,1)S(1)}, bf16[192,2048]{1,0:T(8,128)(2,1)S(1)}, u32[]{:S(2)}, u32[]{:S(2)}) %collective-permute-start.13) | collective-permute-done | bytes 786464 | tf_op jit(solution)/shard_map/ff_P1/ppermute | solution.py:30
  79.9 0.4 collective-permute-done.19.refs_4_.refs_16_
  80.3 4.3 %collective-permute-done.18.refs_3_.refs_15_ = bf16[64,2048]{1,0:T(8,128)(2,1)S(1)} collective-permute-done((bf16[64,2048]{1,0:T(8,128)(2,1)S(1)}, bf16[64,2048]{1,0:T(8,128)(2,1)S(1)}, u32[]{:S(2)}, u32[]{:S(2)}) %collective-permute-start.18) | collective-permute-done | bytes 262176 | tf_op jit(solution)/shard_map/ff_Xr1/ppermute | solution.py:30
  84.6 2.2 %shard_map.62 = (bf16[8,128,512]{2,1,0:T(8,128)(2,1)S(1)}, f32[8,128,512]{2,1,0:T(8,128)S(1)}) custom-call(s32[9]{0:T(128)S(1)} %pad_add_fusion.1.slot_ref, bf16[96,2048]{1,0:T(8,128)(2,1)S(1)} %collective-permute-done.9.refs_0_.refs_9_, ...), custom_call_target="tpu_custom_call", output_to_operand_aliasing={{0}: (7, {}), {1}: (8, {})} | custom-call | tf_op jit(solution)/shard_map/pallas_call | solution.py:127
  86.8 0.1 collective-permute-start.20
  86.9 0.1 pad_add_fusion.place_ref
  87.0 1.7 %shard_map.63.in_ref = bf16[512,2048]{1,0:T(8,128)(2,1)S(1)} custom-call(s32[16]{0:T(128)S(1)} %get-tuple-element.102.pz, s32[16]{0:T(128)S(1)} %get-tuple-element.100.px, bf16[8,128,512]{2,1,0:T(8,128)(2,1)S(1)} %pad_maximum_fusion.own_ref, bf16[8,128,512]{2,1,0:T(8,128)(2,1)S(1)} %collective-permute-done.21.other_ref), custom_call_target="tpu_custom_call" | custom-call | tf_op jit(solution)/shard_map/pallas_call | solution.py:86
  88.6 0.9 collective-permute-done.20.got_ref
  89.5 0.7 shard_map.64
  90.2 0.6 collective-permute-start.22
  90.8 1.5 %collective-permute-start.23 = (bf16[2,128,512]{2,1,0:T(8,128)(2,1)S(1)}, bf16[2,128,512]{2,1,0:T(8,128)(2,1)S(1)}, u32[]{:S(2)}, u32[]{:S(2)}) collective-permute-start(bf16[2,128,512]{2,1,0:T(8,128)(2,1)S(1)} %get-tuple-element.89), channel_id=1, source_target_pairs={{0,6},{1,7},{2,0},{3,1},{4,2},{5,3},{6,4},{7,5},{8,14},{9,15},{10,... | collective-permute-start | bytes 786440 | tf_op jit(solution)/shard_map/ff_Ry3/ppermute | solution.py:39
  92.3 2.1 %collective-permute-start.24 = (bf16[2,128,512]{2,1,0:T(8,128)(2,1)S(1)}, bf16[2,128,512]{2,1,0:T(8,128)(2,1)S(1)}, u32[]{:S(2)}, u32[]{:S(2)}) collective-permute-start(bf16[2,128,512]{2,1,0:T(8,128)(2,1)S(1)} %get-tuple-element.90), channel_id=1, source_target_pairs={{0,4},{1,5},{2,6},{3,7},{4,0},{5,1},{6,2},{7,3},{8,12},{9,13},{10,... | collective-permute-start | bytes 786440 | tf_op jit(solution)/shard_map/ff_Ry2/ppermute | solution.py:39
  94.4 7.5 %shard_map.65 = bf16[512,2048]{1,0:T(8,128)(2,1)} custom-call(bf16[512,2048]{1,0:T(8,128)(2,1)S(1)} %shard_map.63.in_ref, bf16[96,2048]{1,0:T(8,128)(2,1)S(1)} %slice.77.refs_0_, bf16[128,2048]{1,0:T(8,128)(2,1)S(1)} %collective-permute-done.3.refs_1_, bf16[128,2048]{1,0:T(8,128)(2,1)S(1)} %collective-permute-done.4.refs_2_, ...), custom_call_target="tpu_custom_call" | custom-call | flops 4294967296 | bytes 12582912 | tf_op jit(solution)/shard_map/pallas_call | solution.py:180
  102.0 4.1 %collective-permute-done.24.refs_2_ = bf16[2,128,512]{2,1,0:T(8,128)(2,1)S(1)} collective-permute-done((bf16[2,128,512]{2,1,0:T(8,128)(2,1)S(1)}, bf16[2,128,512]{2,1,0:T(8,128)(2,1)S(1)}, u32[]{:S(2)}, u32[]{:S(2)}) %collective-permute-start.24) | collective-permute-done | bytes 262176 | tf_op jit(solution)/shard_map/ff_Ry2/ppermute | solution.py:39
  106.1 0.7 shard_map.66
  106.8 0.8 collective-permute-start.25
  107.6 4.2 %collective-permute-done.25 = bf16[128,512]{1,0:T(8,128)(2,1)S(1)} collective-permute-done((bf16[128,512]{1,0:T(8,128)(2,1)S(1)}, bf16[128,512]{1,0:T(8,128)(2,1)S(1)}, u32[]{:S(2)}, u32[]{:S(2)}) %collective-permute-start.25) | collective-permute-done | bytes 131104 | tf_op jit(solution)/shard_map/ff_Rl/ppermute | solution.py:39
  111.8 0.7 add_convert_fusion
  (35 shorter events, 0.5 us)
Async XLA Ops:
  0.6 11.2 %copy-start.1 = (bf16[128,512]{1,0:T(8,128)(2,1)S(1)}, bf16[128,512]{1,0:T(8,128)(2,1)}, u32[]{:S(2)}) copy-start(bf16[128,512]{1,0:T(8,128)(2,1)} %param.4) | copy-start | bytes 393220
  2.6 26.1 %collective-permute-start.1 = (bf16[96,2048]{1,0:T(8,128)(2,1)S(1)}, bf16[96,2048]{1,0:T(8,128)(2,1)S(1)}, u32[]{:S(2)}, u32[]{:S(2)}) collective-permute-start(bf16[96,2048]{1,0:T(8,128)(2,1)S(1)} %slice.77.refs_0_), channel_id=1, source_target_pairs={{0,48},{16,0},{32,16},{48,32},{64,112},{80,64},{96,80},{112,96},{1... | collective-permute-start | bytes 1179656 | tf_op jit(solution)/shard_map/ff_Z3/ppermute | solution.py:30
  9.0 21.6 %collective-permute-start = (bf16[96,2048]{1,0:T(8,128)(2,1)S(1)}, bf16[96,2048]{1,0:T(8,128)(2,1)S(1)}, u32[]{:S(2)}, u32[]{:S(2)}) collective-permute-start(bf16[96,2048]{1,0:T(8,128)(2,1)S(1)} %slice.77.refs_0_), channel_id=1, source_target_pairs={{0,16},{16,32},{32,48},{48,0},{64,80},{80,96},{96,112},{112,64},{1... | collective-permute-start | bytes 1179656 | tf_op jit(solution)/shard_map/ff_Z1/ppermute | solution.py:30
  9.0 13.7 %collective-permute-start.4 = (bf16[128,2048]{1,0:T(8,128)(2,1)S(1)}, bf16[128,2048]{1,0:T(8,128)(2,1)S(1)}, u32[]{:S(2)}, u32[]{:S(2)}) collective-permute-start(bf16[128,2048]{1,0:T(8,128)(2,1)S(1)} %fusion.7), channel_id=1, source_target_pairs={{0,192},{16,208},{32,224},{48,240},{64,0},{80,16},{96,32},{112,48}... | collective-permute-start | bytes 1572872 | tf_op jit(solution)/shard_map/ff_G3/ppermute | solution.py:30
  11.8 14.7 %collective-permute-start.3 = (bf16[128,2048]{1,0:T(8,128)(2,1)S(1)}, bf16[128,2048]{1,0:T(8,128)(2,1)S(1)}, u32[]{:S(2)}, u32[]{:S(2)}) collective-permute-start(bf16[128,2048]{1,0:T(8,128)(2,1)S(1)} %fusion.7), channel_id=1, source_target_pairs={{0,64},{16,80},{32,96},{48,112},{64,128},{80,144},{96,160},{112,17... | collective-permute-start | bytes 1572872 | tf_op jit(solution)/shard_map/ff_G1/ppermute | solution.py:30
  11.8 16.9 %collective-permute-start.2 = (bf16[128,512]{1,0:T(8,128)(2,1)S(1)}, bf16[128,512]{1,0:T(8,128)(2,1)S(1)}, u32[]{:S(2)}, u32[]{:S(2)}) collective-permute-start(bf16[128,512]{1,0:T(8,128)(2,1)S(1)} %copy-done.1), channel_id=1, source_target_pairs={{0,8},{1,9},{2,10},{3,11},{4,12},{5,13},{6,14},{7,15},{8,0},{9,1},... | collective-permute-start | bytes 393224 | tf_op jit(solution)/shard_map/ff_Il/ppermute | solution.py:39
  22.7 11.5 %collective-permute-start.6 = (bf16[64,2048]{1,0:T(8,128)(2,1)S(1)}, bf16[64,2048]{1,0:T(8,128)(2,1)S(1)}, u32[]{:S(2)}, u32[]{:S(2)}) collective-permute-start(bf16[64,2048]{1,0:T(8,128)(2,1)S(1)} %slice.79), channel_id=1, source_target_pairs={{0,192},{16,208},{32,224},{48,240},{64,0},{80,16},{96,32},{112,48}... | collective-permute-start | bytes 786440 | tf_op jit(solution)/shard_map/ff_Gr3/ppermute | solution.py:30
  26.5 7.9 %collective-permute-start.5 = (bf16[64,2048]{1,0:T(8,128)(2,1)S(1)}, bf16[64,2048]{1,0:T(8,128)(2,1)S(1)}, u32[]{:S(2)}, u32[]{:S(2)}) collective-permute-start(bf16[64,2048]{1,0:T(8,128)(2,1)S(1)} %slice.78), channel_id=1, source_target_pairs={{0,64},{16,80},{32,96},{48,112},{64,128},{80,144},{96,160},{112,17... | collective-permute-start | bytes 786440 | tf_op jit(solution)/shard_map/ff_Gr1/ppermute | solution.py:30
  30.7 6.5 %copy-start = (bf16[512,2048]{1,0:T(8,128)(2,1)S(1)}, bf16[512,2048]{1,0:T(8,128)(2,1)}, u32[]{:S(2)}) copy-start(bf16[512,2048]{1,0:T(8,128)(2,1)} %refs_5_.3) | copy-start | bytes 6291460
  30.7 8.1 %collective-permute-start.8 = (bf16[48,2048]{1,0:T(8,128)(2,1)S(1)}, bf16[48,2048]{1,0:T(8,128)(2,1)S(1)}, u32[]{:S(2)}, u32[]{:S(2)}) collective-permute-start(bf16[48,2048]{1,0:T(8,128)(2,1)S(1)} %slice.67), channel_id=1, source_target_pairs={{0,48},{16,0},{32,16},{48,32},{64,112},{80,64},{96,80},{112,96},{1... | collective-permute-start | bytes 589832 | tf_op jit(solution)/shard_map/ff_Zr3/ppermute | solution.py:30
  32.2 12.1 %collective-permute-start.7 = (bf16[48,2048]{1,0:T(8,128)(2,1)S(1)}, bf16[48,2048]{1,0:T(8,128)(2,1)S(1)}, u32[]{:S(2)}, u32[]{:S(2)}) collective-permute-start(bf16[48,2048]{1,0:T(8,128)(2,1)S(1)} %slice.66), channel_id=1, source_target_pairs={{0,16},{16,32},{32,48},{48,0},{64,80},{80,96},{96,112},{112,64},{1... | collective-permute-start | bytes 589832 | tf_op jit(solution)/shard_map/ff_Zr1/ppermute | solution.py:30
  33.7 13.4 %collective-permute-start.10 = (bf16[2,128,512]{2,1,0:T(8,128)(2,1)S(1)}, bf16[2,128,512]{2,1,0:T(8,128)(2,1)S(1)}, u32[]{:S(2)}, u32[]{:S(2)}) collective-permute-start(bf16[2,128,512]{2,1,0:T(8,128)(2,1)S(1)} %pad_maximum_fusion.8), channel_id=1, source_target_pairs={{0,2},{1,3},{2,0},{3,1},{4,6},{5,7},{6,4},{7,5},{8,10},{9,11},{10,... | collective-permute-start | bytes 786440 | tf_op jit(solution)/shard_map/ff_I1/ppermute | solution.py:45
  34.4 16.9 %collective-permute-start.14 = (bf16[192,2048]{1,0:T(8,128)(2,1)S(1)}, bf16[192,2048]{1,0:T(8,128)(2,1)S(1)}, u32[]{:S(2)}, u32[]{:S(2)}) collective-permute-start(bf16[192,2048]{1,0:T(8,128)(2,1)S(1)} %pad_maximum_fusion.1), channel_id=1, source_target_pairs={{0,192},{16,208},{32,224},{48,240},{64,0},{80,16},{96,32},{112,48}... | collective-permute-start | bytes 2359304 | tf_op jit(solution)/shard_map/ff_F3/ppermute | solution.py:30
  37.1 17.3 %collective-permute-start.12 = (bf16[192,2048]{1,0:T(8,128)(2,1)S(1)}, bf16[192,2048]{1,0:T(8,128)(2,1)S(1)}, u32[]{:S(2)}, u32[]{:S(2)}) collective-permute-start(bf16[192,2048]{1,0:T(8,128)(2,1)S(1)} %pad_maximum_fusion.1), channel_id=1, source_target_pairs={{0,64},{16,80},{32,96},{48,112},{64,128},{80,144},{96,160},{112,17... | collective-permute-start | bytes 2359304 | tf_op jit(solution)/shard_map/ff_F1/ppermute | solution.py:30
  44.3 21.4 %collective-permute-start.17 = (bf16[128,2048]{1,0:T(8,128)(2,1)S(1)}, bf16[128,2048]{1,0:T(8,128)(2,1)S(1)}, u32[]{:S(2)}, u32[]{:S(2)}) collective-permute-start(bf16[128,2048]{1,0:T(8,128)(2,1)S(1)} %pad_maximum_fusion.5.refs_0_.refs_12_), channel_id=1, source_target_pairs={{0,48},{16,0},{32,16},{48,32},{64,112},{80,64},{96,80},{112,96},{1... | collective-permute-start | bytes 1572872 | tf_op jit(solution)/shard_map/ff_X3/ppermute | solution.py:30
  44.3 25.9 %collective-permute-start.16 = (bf16[128,2048]{1,0:T(8,128)(2,1)S(1)}, bf16[128,2048]{1,0:T(8,128)(2,1)S(1)}, u32[]{:S(2)}, u32[]{:S(2)}) collective-permute-start(bf16[128,2048]{1,0:T(8,128)(2,1)S(1)} %pad_maximum_fusion.5.refs_0_.refs_12_), channel_id=1, source_target_pairs={{0,16},{16,32},{32,48},{48,0},{64,80},{80,96},{96,112},{112,64},{1... | collective-permute-start | bytes 1572872 | tf_op jit(solution)/shard_map/ff_X1/ppermute | solution.py:30
  47.2 23.1 %collective-permute-start.11 = (bf16[4,128,512]{2,1,0:T(8,128)(2,1)S(1)}, bf16[4,128,512]{2,1,0:T(8,128)(2,1)S(1)}, u32[]{:S(2)}, u32[]{:S(2)}) collective-permute-start(bf16[4,128,512]{2,1,0:T(8,128)(2,1)S(1)} %pad_maximum_fusion.6), channel_id=1, source_target_pairs={{0,4},{1,5},{2,6},{3,7},{4,0},{5,1},{6,2},{7,3},{8,12},{9,13},{10,... | collective-permute-start | bytes 1572872 | tf_op jit(solution)/shard_map/ff_I2/ppermute | solution.py:45
  54.7 20.7 %collective-permute-start.15 = (bf16[192,2048]{1,0:T(8,128)(2,1)S(1)}, bf16[192,2048]{1,0:T(8,128)(2,1)S(1)}, u32[]{:S(2)}, u32[]{:S(2)}) collective-permute-start(bf16[192,2048]{1,0:T(8,128)(2,1)S(1)} %get-tuple-element.104), channel_id=1, source_target_pairs={{0,192},{16,208},{32,224},{48,240},{64,0},{80,16},{96,32},{112,48}... | collective-permute-start | bytes 2359304 | tf_op jit(solution)/shard_map/ff_P3/ppermute | solution.py:30
  55.1 24.8 %collective-permute-start.13 = (bf16[192,2048]{1,0:T(8,128)(2,1)S(1)}, bf16[192,2048]{1,0:T(8,128)(2,1)S(1)}, u32[]{:S(2)}, u32[]{:S(2)}) collective-permute-start(bf16[192,2048]{1,0:T(8,128)(2,1)S(1)} %get-tuple-element.105), channel_id=1, source_target_pairs={{0,64},{16,80},{32,96},{48,112},{64,128},{80,144},{96,160},{112,17... | collective-permute-start | bytes 2359304 | tf_op jit(solution)/shard_map/ff_P1/ppermute | solution.py:30
  65.7 14.2 %collective-permute-start.9 = (bf16[96,2048]{1,0:T(8,128)(2,1)S(1)}, bf16[96,2048]{1,0:T(8,128)(2,1)S(1)}, u32[]{:S(2)}, u32[]{:S(2)}) collective-permute-start(bf16[96,2048]{1,0:T(8,128)(2,1)S(1)} %constant_dynamic-update-slice_fusion.refs_2_.refs_6_), channel_id=1, source_target_pairs={{0,128},{16,144},{32,160},{48,176},{64,192},{80,208},{96,224},{112... | collective-permute-start | bytes 1179656 | tf_op jit(solution)/shard_map/ff_P2/ppermute | solution.py:30
  70.2 10.1 %collective-permute-start.19 = (bf16[64,2048]{1,0:T(8,128)(2,1)S(1)}, bf16[64,2048]{1,0:T(8,128)(2,1)S(1)}, u32[]{:S(2)}, u32[]{:S(2)}) collective-permute-start(bf16[64,2048]{1,0:T(8,128)(2,1)S(1)} %slice.75), channel_id=1, source_target_pairs={{0,48},{16,0},{32,16},{48,32},{64,112},{80,64},{96,80},{112,96},{1... | collective-permute-start | bytes 786440 | tf_op jit(solution)/shard_map/ff_Xr3/ppermute | solution.py:30
  70.3 14.2 %collective-permute-start.18 = (bf16[64,2048]{1,0:T(8,128)(2,1)S(1)}, bf16[64,2048]{1,0:T(8,128)(2,1)S(1)}, u32[]{:S(2)}, u32[]{:S(2)}) collective-permute-start(bf16[64,2048]{1,0:T(8,128)(2,1)S(1)} %slice.74), channel_id=1, source_target_pairs={{0,16},{16,32},{32,48},{48,0},{64,80},{80,96},{96,112},{112,64},{1... | collective-permute-start | bytes 786440 | tf_op jit(solution)/shard_map/ff_Xr1/ppermute | solution.py:30
  79.9 7.1 %collective-permute-start.21 = (bf16[8,128,512]{2,1,0:T(8,128)(2,1)S(1)}, bf16[8,128,512]{2,1,0:T(8,128)(2,1)S(1)}, u32[]{:S(2)}, u32[]{:S(2)}) collective-permute-start(bf16[8,128,512]{2,1,0:T(8,128)(2,1)S(1)} %pad_maximum_fusion.own_ref), channel_id=1, source_target_pairs={{0,1},{1,0},{2,3},{3,2},{4,5},{5,4},{6,7},{7,6},{8,9},{9,8},{10,11... | collective-permute-start | bytes 3145736 | tf_op jit(solution)/shard_map/ff_Ic/ppermute | solution.py:39
  86.8 2.7 %collective-permute-start.20 = (bf16[8,128,512]{2,1,0:T(8,128)(2,1)S(1)}, bf16[8,128,512]{2,1,0:T(8,128)(2,1)S(1)}, u32[]{:S(2)}, u32[]{:S(2)}) collective-permute-start(bf16[8,128,512]{2,1,0:T(8,128)(2,1)S(1)} %get-tuple-element.81), channel_id=1, source_target_pairs={{0,1},{1,0},{2,3},{3,2},{4,5},{5,4},{6,7},{7,6},{8,9},{9,8},{10,11... | collective-permute-start | bytes 3145736 | tf_op jit(solution)/shard_map/ff_Rc/ppermute | solution.py:39
  90.2 11.7 %collective-permute-start.22 = (bf16[2,128,512]{2,1,0:T(8,128)(2,1)S(1)}, bf16[2,128,512]{2,1,0:T(8,128)(2,1)S(1)}, u32[]{:S(2)}, u32[]{:S(2)}) collective-permute-start(bf16[2,128,512]{2,1,0:T(8,128)(2,1)S(1)} %get-tuple-element.88), channel_id=1, source_target_pairs={{0,2},{1,3},{2,4},{3,5},{4,6},{5,7},{6,0},{7,1},{8,10},{9,11},{10,... | collective-permute-start | bytes 786440 | tf_op jit(solution)/shard_map/ff_Ry1/ppermute | solution.py:39
  90.8 11.1 %collective-permute-start.23 = (bf16[2,128,512]{2,1,0:T(8,128)(2,1)S(1)}, bf16[2,128,512]{2,1,0:T(8,128)(2,1)S(1)}, u32[]{:S(2)}, u32[]{:S(2)}) collective-permute-start(bf16[2,128,512]{2,1,0:T(8,128)(2,1)S(1)} %get-tuple-element.89), channel_id=1, source_target_pairs={{0,6},{1,7},{2,0},{3,1},{4,2},{5,3},{6,4},{7,5},{8,14},{9,15},{10,... | collective-permute-start | bytes 786440 | tf_op jit(solution)/shard_map/ff_Ry3/ppermute | solution.py:39
  92.3 13.7 %collective-permute-start.24 = (bf16[2,128,512]{2,1,0:T(8,128)(2,1)S(1)}, bf16[2,128,512]{2,1,0:T(8,128)(2,1)S(1)}, u32[]{:S(2)}, u32[]{:S(2)}) collective-permute-start(bf16[2,128,512]{2,1,0:T(8,128)(2,1)S(1)} %get-tuple-element.90), channel_id=1, source_target_pairs={{0,4},{1,5},{2,6},{3,7},{4,0},{5,1},{6,2},{7,3},{8,12},{9,13},{10,... | collective-permute-start | bytes 786440 | tf_op jit(solution)/shard_map/ff_Ry2/ppermute | solution.py:39
  106.8 5.1 %collective-permute-start.25 = (bf16[128,512]{1,0:T(8,128)(2,1)S(1)}, bf16[128,512]{1,0:T(8,128)(2,1)S(1)}, u32[]{:S(2)}, u32[]{:S(2)}) collective-permute-start(bf16[128,512]{1,0:T(8,128)(2,1)S(1)} %get-tuple-element.98), channel_id=1, source_target_pairs={{0,8},{1,9},{2,10},{3,11},{4,12},{5,13},{6,14},{7,15},{8,0},{9,1},... | collective-permute-start | bytes 393224 | tf_op jit(solution)/shard_map/ff_Rl/ppermute | solution.py:39

commit v4 on v3

--- a/solution.py
+++ b/solution.py
@@ -295,7 +295,7 @@
     p1 = along_row(jnp.concatenate([b2, f1[:NZ]], axis=0), 1, 0, "P1")
     p3 = along_row(jnp.concatenate([b2, f3[NZ:]], axis=0), 3, 0, "P3")
     into = terms(into, slice(4, 11), whole(b1, b3, b2, f1, f3))
-    e1, e3, f1, f3, *into = tied(e1, e3, f1, f3, *into)
+    e1, e3, f1, f3 = tied(e1, e3, f1, f3)
     q1 = along_row(e1[:2 * NX], 0, 1, "Xr1")
     q3 = along_row(e3[2 * NX:], 0, 3, "Xr3")
     own, p1, p3 = tied(own, p1, p3)

time: 113 us -> 113 us (level)
  no operation moved by 1% of the time
where the time goes in v4:
time: 113 us; the launch traced here: 112 us
  waiting for transfers between devices  48.7 us (43%)
  starting transfers between devices  40.4 us (36%)
  Pallas kernels  18.4 us (16%)
  other arithmetic  3.36 us (3%)
    ppermute x17, waiting for transfers between devices, along_row(): return lax.ppermute(a, 'row', perm)  37.7 us
    ppermute x17, starting transfers between devices, along_row(): return lax.ppermute(a, 'row', perm)  31.2 us
    ppermute x7, waiting for transfers between devices, along_col(): return lax.ppermute(a, 'col', perm)  11.1 us
    pallas_call x4, Pallas kernels, input_grad_parts(): pl.pallas_call(kernel, out_shape=(jax.ShapeDtypeStruct((8, ROWS, d), jnp....  7.84 us
    pallas_call x1, Pallas kernels, weight_grad_of(): pl.pallas_call(kernel, out_shape=jax.ShapeDtypeStruct((d, hidden), jnp.bf...  7.49 us
    ppermute x7, starting transfers between devices, along_col(): return lax.ppermute(a, 'col', perm)  6.41 us
    ppermute x2, starting transfers between devices, swap_y(): return lax.ppermute(a, 'col', perm)  2.71 us
  transfers between devices with their start and end apart: 26, of which 14 were waited for; matrix products, arithmetic and copies ran while one was open for 1% of the time, Pallas kernels for 15%

profile of v4, /device:TPU:8, one launch (start us, length us, event | category | flops | bytes accessed | tf_op | source)
XLA Modules:
  0.0 112.5 jit_solution(838850744897913282)
XLA Ops:
  0.6 2.0 %fusion.7 = bf16[128,2048]{1,0:T(8,128)(2,1)S(1)} fusion(bf16[128,2048]{1,0:T(8,128)(2,1)} %param.5, bf16[128,2048]{1,0:T(8,128)(2,1)} %param.6), kind=kLoop, calls=%fused_computation.14 | loop fusion | flops 5505024 | bytes 1572864 | tf_op jit(solution)/shard_map/convert_element_type | solution.py:249
  2.6 6.4 %collective-permute-start.1 = (bf16[96,2048]{1,0:T(8,128)(2,1)S(1)}, bf16[96,2048]{1,0:T(8,128)(2,1)S(1)}, u32[]{:S(2)}, u32[]{:S(2)}) collective-permute-start(bf16[96,2048]{1,0:T(8,128)(2,1)S(1)} %slice.77.refs_0_), channel_id=1, source_target_pairs={{0,48},{16,0},{32,16},{48,32},{64,112},{80,64},{96,80},{112,96},{1... | collective-permute-start | bytes 1179656 | tf_op jit(solution)/shard_map/ff_Z3/ppermute | solution.py:30
  9.0 0.0 collective-permute-start
  9.0 2.8 %collective-permute-start.4 = (bf16[128,2048]{1,0:T(8,128)(2,1)S(1)}, bf16[128,2048]{1,0:T(8,128)(2,1)S(1)}, u32[]{:S(2)}, u32[]{:S(2)}) collective-permute-start(bf16[128,2048]{1,0:T(8,128)(2,1)S(1)} %fusion.7), channel_id=1, source_target_pairs={{0,192},{16,208},{32,224},{48,240},{64,0},{80,16},{96,32},{112,48}... | collective-permute-start | bytes 1572872 | tf_op jit(solution)/shard_map/ff_G3/ppermute | solution.py:30
  11.8 1.0 collective-permute-start.2
  12.8 0.1 stack.107
  12.9 0.1 stack.108
  13.1 9.6 %collective-permute-done.4.refs_2_ = bf16[128,2048]{1,0:T(8,128)(2,1)S(1)} collective-permute-done((bf16[128,2048]{1,0:T(8,128)(2,1)S(1)}, bf16[128,2048]{1,0:T(8,128)(2,1)S(1)}, u32[]{:S(2)}, u32[]{:S(2)}) %collective-permute-start.4) | collective-permute-done | bytes 524320 | tf_op jit(solution)/shard_map/ff_G3/ppermute | solution.py:30
  22.7 3.8 %collective-permute-start.6 = (bf16[64,2048]{1,0:T(8,128)(2,1)S(1)}, bf16[64,2048]{1,0:T(8,128)(2,1)S(1)}, u32[]{:S(2)}, u32[]{:S(2)}) collective-permute-start(bf16[64,2048]{1,0:T(8,128)(2,1)S(1)} %slice.79), channel_id=1, source_target_pairs={{0,192},{16,208},{32,224},{48,240},{64,0},{80,16},{96,32},{112,48}... | collective-permute-start | bytes 786440 | tf_op jit(solution)/shard_map/ff_Gr3/ppermute | solution.py:30
  26.5 0.0 collective-permute-done.3.refs_1_
  26.5 0.1 collective-permute-start.5
  26.6 2.1 %collective-permute-done.2 = bf16[128,512]{1,0:T(8,128)(2,1)S(1)} collective-permute-done((bf16[128,512]{1,0:T(8,128)(2,1)S(1)}, bf16[128,512]{1,0:T(8,128)(2,1)S(1)}, u32[]{:S(2)}, u32[]{:S(2)}) %collective-permute-start.2) | collective-permute-done | bytes 131104 | tf_op jit(solution)/shard_map/ff_Il/ppermute | solution.py:39
  28.7 1.9 %collective-permute-done.refs_0_.refs_4_ = bf16[96,2048]{1,0:T(8,128)(2,1)S(1)} collective-permute-done((bf16[96,2048]{1,0:T(8,128)(2,1)S(1)}, bf16[96,2048]{1,0:T(8,128)(2,1)S(1)}, u32[]{:S(2)}, u32[]{:S(2)}) %collective-permute-start) | collective-permute-done | bytes 393248 | tf_op jit(solution)/shard_map/ff_Z1/ppermute | solution.py:30
  30.7 0.0 copy-start
  30.7 1.4 %collective-permute-start.8 = (bf16[48,2048]{1,0:T(8,128)(2,1)S(1)}, bf16[48,2048]{1,0:T(8,128)(2,1)S(1)}, u32[]{:S(2)}, u32[]{:S(2)}) collective-permute-start(bf16[48,2048]{1,0:T(8,128)(2,1)S(1)} %slice.67), channel_id=1, source_target_pairs={{0,48},{16,0},{32,16},{48,32},{64,112},{80,64},{96,80},{112,96},{1... | collective-permute-start | bytes 589832 | tf_op jit(solution)/shard_map/ff_Zr3/ppermute | solution.py:30
  32.2 1.6 %collective-permute-start.7 = (bf16[48,2048]{1,0:T(8,128)(2,1)S(1)}, bf16[48,2048]{1,0:T(8,128)(2,1)S(1)}, u32[]{:S(2)}, u32[]{:S(2)}) collective-permute-start(bf16[48,2048]{1,0:T(8,128)(2,1)S(1)} %slice.66), channel_id=1, source_target_pairs={{0,16},{16,32},{32,48},{48,0},{64,80},{80,96},{96,112},{112,64},{1... | collective-permute-start | bytes 589832 | tf_op jit(solution)/shard_map/ff_Zr1/ppermute | solution.py:30
  33.7 0.4 collective-permute-start.10
  34.2 0.1 pad_maximum_fusion.1
  34.3 0.0 collective-permute-done.6
  34.3 0.1 collective-permute-done.5
  34.4 2.7 %collective-permute-start.14 = (bf16[192,2048]{1,0:T(8,128)(2,1)S(1)}, bf16[192,2048]{1,0:T(8,128)(2,1)S(1)}, u32[]{:S(2)}, u32[]{:S(2)}) collective-permute-start(bf16[192,2048]{1,0:T(8,128)(2,1)S(1)} %pad_maximum_fusion.1), channel_id=1, source_target_pairs={{0,192},{16,208},{32,224},{48,240},{64,0},{80,16},{96,32},{112,48}... | collective-permute-start | bytes 2359304 | tf_op jit(solution)/shard_map/ff_F3/ppermute | solution.py:30
  37.2 1.6 %shard_map.59 = (bf16[8,128,512]{2,1,0:T(8,128)(2,1)S(1)}, f32[8,128,512]{2,1,0:T(8,128)S(1)}) custom-call(s32[4]{0:T(128)S(1)} %bitcast.22, bf16[96,2048]{1,0:T(8,128)(2,1)S(1)} %slice.77.refs_0_, bf16[128,2048]{1,0:T(8,128)(2,1)S(1)} %collective-permute-done.3.refs_1_, bf16[128,2048]{1,0:T(8,128)(2,1)S(1)} %collective-permute-done.4.refs_2_, ...), custom_call_target="tpu_custom_call" | custom-call | tf_op jit(solution)/shard_map/pallas_call | solution.py:127
  38.9 0.0 collective-permute-done.8
  38.9 5.4 %collective-permute-done.7 = bf16[48,2048]{1,0:T(8,128)(2,1)S(1)} collective-permute-done((bf16[48,2048]{1,0:T(8,128)(2,1)S(1)}, bf16[48,2048]{1,0:T(8,128)(2,1)S(1)}, u32[]{:S(2)}, u32[]{:S(2)}) %collective-permute-start.7) | collective-permute-done | bytes 196640 | tf_op jit(solution)/shard_map/ff_Zr1/ppermute | solution.py:30
  44.3 0.0 collective-permute-start.17
  44.3 2.9 %collective-permute-start.16 = (bf16[128,2048]{1,0:T(8,128)(2,1)S(1)}, bf16[128,2048]{1,0:T(8,128)(2,1)S(1)}, u32[]{:S(2)}, u32[]{:S(2)}) collective-permute-start(bf16[128,2048]{1,0:T(8,128)(2,1)S(1)} %pad_maximum_fusion.5.refs_0_.refs_12_), channel_id=1, source_target_pairs={{0,16},{16,32},{32,48},{48,0},{64,80},{80,96},{96,112},{112,64},{1... | collective-permute-start | bytes 1572872 | tf_op jit(solution)/shard_map/ff_X1/ppermute | solution.py:30
  47.2 2.3 %collective-permute-start.11 = (bf16[4,128,512]{2,1,0:T(8,128)(2,1)S(1)}, bf16[4,128,512]{2,1,0:T(8,128)(2,1)S(1)}, u32[]{:S(2)}, u32[]{:S(2)}) collective-permute-start(bf16[4,128,512]{2,1,0:T(8,128)(2,1)S(1)} %pad_maximum_fusion.6), channel_id=1, source_target_pairs={{0,4},{1,5},{2,6},{3,7},{4,0},{5,1},{6,2},{7,3},{8,12},{9,13},{10,... | collective-permute-start | bytes 1572872 | tf_op jit(solution)/shard_map/ff_I2/ppermute | solution.py:45
  49.5 1.7 %collective-permute-done.14.refs_4_.refs_8_ = bf16[192,2048]{1,0:T(8,128)(2,1)S(1)} collective-permute-done((bf16[192,2048]{1,0:T(8,128)(2,1)S(1)}, bf16[192,2048]{1,0:T(8,128)(2,1)S(1)}, u32[]{:S(2)}, u32[]{:S(2)}) %collective-permute-start.14) | collective-permute-done | bytes 786464 | tf_op jit(solution)/shard_map/ff_F3/ppermute | solution.py:30
  51.3 3.1 %collective-permute-done.12.refs_3_.refs_7_ = bf16[192,2048]{1,0:T(8,128)(2,1)S(1)} collective-permute-done((bf16[192,2048]{1,0:T(8,128)(2,1)S(1)}, bf16[192,2048]{1,0:T(8,128)(2,1)S(1)}, u32[]{:S(2)}, u32[]{:S(2)}) %collective-permute-start.12) | collective-permute-done | bytes 786464 | tf_op jit(solution)/shard_map/ff_F1/ppermute | solution.py:30
  54.5 0.2 pad_maximum_fusion.4
  54.7 0.4 collective-permute-start.15
  55.1 1.7 %collective-permute-start.13 = (bf16[192,2048]{1,0:T(8,128)(2,1)S(1)}, bf16[192,2048]{1,0:T(8,128)(2,1)S(1)}, u32[]{:S(2)}, u32[]{:S(2)}) collective-permute-start(bf16[192,2048]{1,0:T(8,128)(2,1)S(1)} %get-tuple-element.101), channel_id=1, source_target_pairs={{0,64},{16,80},{32,96},{48,112},{64,128},{80,144},{96,160},{112,17... | collective-permute-start | bytes 2359304 | tf_op jit(solution)/shard_map/ff_P1/ppermute | solution.py:30
  56.8 8.9 %collective-permute-done.17.refs_2_.refs_14_ = bf16[128,2048]{1,0:T(8,128)(2,1)S(1)} collective-permute-done((bf16[128,2048]{1,0:T(8,128)(2,1)S(1)}, bf16[128,2048]{1,0:T(8,128)(2,1)S(1)}, u32[]{:S(2)}, u32[]{:S(2)}) %collective-permute-start.17) | collective-permute-done | bytes 524320 | tf_op jit(solution)/shard_map/ff_X3/ppermute | solution.py:30
  65.7 4.5 %collective-permute-start.9 = (bf16[96,2048]{1,0:T(8,128)(2,1)S(1)}, bf16[96,2048]{1,0:T(8,128)(2,1)S(1)}, u32[]{:S(2)}, u32[]{:S(2)}) collective-permute-start(bf16[96,2048]{1,0:T(8,128)(2,1)S(1)} %constant_dynamic-update-slice_fusion.refs_2_.refs_6_), channel_id=1, source_target_pairs={{0,128},{16,144},{32,160},{48,176},{64,192},{80,208},{96,224},{112... | collective-permute-start | bytes 1179656 | tf_op jit(solution)/shard_map/ff_P2/ppermute | solution.py:30
  70.2 0.0 collective-permute-done.16.refs_1_.refs_13_
  70.2 0.1 collective-permute-start.19
  70.3 2.9 %collective-permute-start.18 = (bf16[64,2048]{1,0:T(8,128)(2,1)S(1)}, bf16[64,2048]{1,0:T(8,128)(2,1)S(1)}, u32[]{:S(2)}, u32[]{:S(2)}) collective-permute-start(bf16[64,2048]{1,0:T(8,128)(2,1)S(1)} %slice.74), channel_id=1, source_target_pairs={{0,16},{16,32},{32,48},{48,0},{64,80},{80,96},{96,112},{112,64},{1... | collective-permute-start | bytes 786440 | tf_op jit(solution)/shard_map/ff_Xr1/ppermute | solution.py:30
  73.3 0.1 slice.73.slot_ref
  73.3 0.1 slice.57
  73.4 0.1 slice.58
  73.5 0.1 pad_add_fusion.1.slot_ref
  73.6 0.1 pad_maximum_fusion.own_ref
  73.7 2.3 %shard_map.60 = (bf16[8,128,512]{2,1,0:T(8,128)(2,1)S(1)}, f32[8,128,512]{2,1,0:T(8,128)S(1)}) custom-call(s32[7]{0:T(128)S(1)} %slice.73.slot_ref, bf16[96,2048]{1,0:T(8,128)(2,1)S(1)} %collective-permute-done.refs_0_.refs_4_, bf16[96,2048]{1,0:T(8,128)(2,1)S(1)} %collective-permute-done.1.refs_1_.refs_5_, ...), custom_call_target="tpu_custom_call", output_to_operand_aliasing={{0}: (7, {}), {1}: (8, {})} | custom-call | tf_op jit(solution)/shard_map/pallas_call | solution.py:127
  76.0 1.7 %shard_map.61 = (bf16[8,128,512]{2,1,0:T(8,128)(2,1)S(1)}, f32[8,128,512]{2,1,0:T(8,128)S(1)}) custom-call(s32[12]{0:T(128)S(1)} %bitcast.23, bf16[128,2048]{1,0:T(8,128)(2,1)S(1)} %pad_maximum_fusion.5.refs_0_.refs_12_, bf16[128,2048]{1,0:T(8,128)(2,1)S(1)} %collective-permute-done.16.refs_1_.refs_13_, ...), custom_call_target="tpu_custom_call", output_to_operand_aliasing={{0}: (5, {}), {1}: (6, {})} | custom-call | tf_op jit(solution)/shard_map/pallas_call | solution.py:127
  77.7 0.0 collective-permute-done.15.refs_2_.refs_11_
  77.7 2.2 %collective-permute-done.13.refs_1_.refs_10_ = bf16[192,2048]{1,0:T(8,128)(2,1)S(1)} collective-permute-done((bf16[192,2048]{1,0:T(8,128)(2,1)S(1)}, bf16[192,2048]{1,0:T(8,128)(2,1)S(1)}, u32[]{:S(2)}, u32[]{:S(2)}) %collective-permute-start.13) | collective-permute-done | bytes 786464 | tf_op jit(solution)/shard_map/ff_P1/ppermute | solution.py:30
  79.9 0.0 collective-permute-start.21
  79.9 0.4 collective-permute-done.19.refs_4_.refs_16_
  80.3 4.3 %collective-permute-done.18.refs_3_.refs_15_ = bf16[64,2048]{1,0:T(8,128)(2,1)S(1)} collective-permute-done((bf16[64,2048]{1,0:T(8,128)(2,1)S(1)}, bf16[64,2048]{1,0:T(8,128)(2,1)S(1)}, u32[]{:S(2)}, u32[]{:S(2)}) %collective-permute-start.18) | collective-permute-done | bytes 262176 | tf_op jit(solution)/shard_map/ff_Xr1/ppermute | solution.py:30
  84.6 2.2 %shard_map.62 = (bf16[8,128,512]{2,1,0:T(8,128)(2,1)S(1)}, f32[8,128,512]{2,1,0:T(8,128)S(1)}) custom-call(s32[9]{0:T(128)S(1)} %pad_add_fusion.1.slot_ref, bf16[96,2048]{1,0:T(8,128)(2,1)S(1)} %collective-permute-done.9.refs_0_.refs_9_, ...), custom_call_target="tpu_custom_call", output_to_operand_aliasing={{0}: (7, {}), {1}: (8, {})} | custom-call | tf_op jit(solution)/shard_map/pallas_call | solution.py:127
  86.8 0.1 collective-permute-start.20
  86.9 0.1 pad_add_fusion.place_ref
  87.0 1.7 %shard_map.63.in_ref = bf16[512,2048]{1,0:T(8,128)(2,1)S(1)} custom-call(s32[16]{0:T(128)S(1)} %get-tuple-element.98.pz, s32[16]{0:T(128)S(1)} %get-tuple-element.96.px, bf16[8,128,512]{2,1,0:T(8,128)(2,1)S(1)} %pad_maximum_fusion.own_ref, bf16[8,128,512]{2,1,0:T(8,128)(2,1)S(1)} %collective-permute-done.21.other_ref), custom_call_target="tpu_custom_call" | custom-call | tf_op jit(solution)/shard_map/pallas_call | solution.py:86
  88.6 0.9 collective-permute-done.20.got_ref
  89.5 0.7 shard_map.64
  90.2 0.6 collective-permute-start.22
  90.8 1.5 %collective-permute-start.23 = (bf16[2,128,512]{2,1,0:T(8,128)(2,1)S(1)}, bf16[2,128,512]{2,1,0:T(8,128)(2,1)S(1)}, u32[]{:S(2)}, u32[]{:S(2)}) collective-permute-start(bf16[2,128,512]{2,1,0:T(8,128)(2,1)S(1)} %get-tuple-element.85), channel_id=1, source_target_pairs={{0,6},{1,7},{2,0},{3,1},{4,2},{5,3},{6,4},{7,5},{8,14},{9,15},{10,... | collective-permute-start | bytes 786440 | tf_op jit(solution)/shard_map/ff_Ry3/ppermute | solution.py:39
  92.3 2.1 %collective-permute-start.24 = (bf16[2,128,512]{2,1,0:T(8,128)(2,1)S(1)}, bf16[2,128,512]{2,1,0:T(8,128)(2,1)S(1)}, u32[]{:S(2)}, u32[]{:S(2)}) collective-permute-start(bf16[2,128,512]{2,1,0:T(8,128)(2,1)S(1)} %get-tuple-element.86), channel_id=1, source_target_pairs={{0,4},{1,5},{2,6},{3,7},{4,0},{5,1},{6,2},{7,3},{8,12},{9,13},{10,... | collective-permute-start | bytes 786440 | tf_op jit(solution)/shard_map/ff_Ry2/ppermute | solution.py:39
  94.4 7.5 %shard_map.65 = bf16[512,2048]{1,0:T(8,128)(2,1)} custom-call(bf16[512,2048]{1,0:T(8,128)(2,1)S(1)} %shard_map.63.in_ref, bf16[96,2048]{1,0:T(8,128)(2,1)S(1)} %slice.77.refs_0_, bf16[128,2048]{1,0:T(8,128)(2,1)S(1)} %collective-permute-done.3.refs_1_, bf16[128,2048]{1,0:T(8,128)(2,1)S(1)} %collective-permute-done.4.refs_2_, ...), custom_call_target="tpu_custom_call" | custom-call | flops 4294967296 | bytes 12582912 | tf_op jit(solution)/shard_map/pallas_call | solution.py:180
  102.0 4.1 %collective-permute-done.24.refs_2_ = bf16[2,128,512]{2,1,0:T(8,128)(2,1)S(1)} collective-permute-done((bf16[2,128,512]{2,1,0:T(8,128)(2,1)S(1)}, bf16[2,128,512]{2,1,0:T(8,128)(2,1)S(1)}, u32[]{:S(2)}, u32[]{:S(2)}) %collective-permute-start.24) | collective-permute-done | bytes 262176 | tf_op jit(solution)/shard_map/ff_Ry2/ppermute | solution.py:39
  106.1 0.7 shard_map.66
  106.8 1.1 collective-permute-start.25
  107.9 3.9 %collective-permute-done.25 = bf16[128,512]{1,0:T(8,128)(2,1)S(1)} collective-permute-done((bf16[128,512]{1,0:T(8,128)(2,1)S(1)}, bf16[128,512]{1,0:T(8,128)(2,1)S(1)}, u32[]{:S(2)}, u32[]{:S(2)}) %collective-permute-start.25) | collective-permute-done | bytes 131104 | tf_op jit(solution)/shard_map/ff_Rl/ppermute | solution.py:39
  111.8 0.7 add_convert_fusion
  (35 shorter events, 0.5 us)
Async XLA Ops:
  0.6 11.2 %copy-start.1 = (bf16[128,512]{1,0:T(8,128)(2,1)S(1)}, bf16[128,512]{1,0:T(8,128)(2,1)}, u32[]{:S(2)}) copy-start(bf16[128,512]{1,0:T(8,128)(2,1)} %param.4) | copy-start | bytes 393220
  2.6 26.1 %collective-permute-start.1 = (bf16[96,2048]{1,0:T(8,128)(2,1)S(1)}, bf16[96,2048]{1,0:T(8,128)(2,1)S(1)}, u32[]{:S(2)}, u32[]{:S(2)}) collective-permute-start(bf16[96,2048]{1,0:T(8,128)(2,1)S(1)} %slice.77.refs_0_), channel_id=1, source_target_pairs={{0,48},{16,0},{32,16},{48,32},{64,112},{80,64},{96,80},{112,96},{1... | collective-permute-start | bytes 1179656 | tf_op jit(solution)/shard_map/ff_Z3/ppermute | solution.py:30
  9.0 21.6 %collective-permute-start = (bf16[96,2048]{1,0:T(8,128)(2,1)S(1)}, bf16[96,2048]{1,0:T(8,128)(2,1)S(1)}, u32[]{:S(2)}, u32[]{:S(2)}) collective-permute-start(bf16[96,2048]{1,0:T(8,128)(2,1)S(1)} %slice.77.refs_0_), channel_id=1, source_target_pairs={{0,16},{16,32},{32,48},{48,0},{64,80},{80,96},{96,112},{112,64},{1... | collective-permute-start | bytes 1179656 | tf_op jit(solution)/shard_map/ff_Z1/ppermute | solution.py:30
  9.0 13.7 %collective-permute-start.4 = (bf16[128,2048]{1,0:T(8,128)(2,1)S(1)}, bf16[128,2048]{1,0:T(8,128)(2,1)S(1)}, u32[]{:S(2)}, u32[]{:S(2)}) collective-permute-start(bf16[128,2048]{1,0:T(8,128)(2,1)S(1)} %fusion.7), channel_id=1, source_target_pairs={{0,192},{16,208},{32,224},{48,240},{64,0},{80,16},{96,32},{112,48}... | collective-permute-start | bytes 1572872 | tf_op jit(solution)/shard_map/ff_G3/ppermute | solution.py:30
  11.8 14.7 %collective-permute-start.3 = (bf16[128,2048]{1,0:T(8,128)(2,1)S(1)}, bf16[128,2048]{1,0:T(8,128)(2,1)S(1)}, u32[]{:S(2)}, u32[]{:S(2)}) collective-permute-start(bf16[128,2048]{1,0:T(8,128)(2,1)S(1)} %fusion.7), channel_id=1, source_target_pairs={{0,64},{16,80},{32,96},{48,112},{64,128},{80,144},{96,160},{112,17... | collective-permute-start | bytes 1572872 | tf_op jit(solution)/shard_map/ff_G1/ppermute | solution.py:30
  11.8 16.9 %collective-permute-start.2 = (bf16[128,512]{1,0:T(8,128)(2,1)S(1)}, bf16[128,512]{1,0:T(8,128)(2,1)S(1)}, u32[]{:S(2)}, u32[]{:S(2)}) collective-permute-start(bf16[128,512]{1,0:T(8,128)(2,1)S(1)} %copy-done.1), channel_id=1, source_target_pairs={{0,8},{1,9},{2,10},{3,11},{4,12},{5,13},{6,14},{7,15},{8,0},{9,1},... | collective-permute-start | bytes 393224 | tf_op jit(solution)/shard_map/ff_Il/ppermute | solution.py:39
  22.7 11.5 %collective-permute-start.6 = (bf16[64,2048]{1,0:T(8,128)(2,1)S(1)}, bf16[64,2048]{1,0:T(8,128)(2,1)S(1)}, u32[]{:S(2)}, u32[]{:S(2)}) collective-permute-start(bf16[64,2048]{1,0:T(8,128)(2,1)S(1)} %slice.79), channel_id=1, source_target_pairs={{0,192},{16,208},{32,224},{48,240},{64,0},{80,16},{96,32},{112,48}... | collective-permute-start | bytes 786440 | tf_op jit(solution)/shard_map/ff_Gr3/ppermute | solution.py:30
  26.5 7.9 %collective-permute-start.5 = (bf16[64,2048]{1,0:T(8,128)(2,1)S(1)}, bf16[64,2048]{1,0:T(8,128)(2,1)S(1)}, u32[]{:S(2)}, u32[]{:S(2)}) collective-permute-start(bf16[64,2048]{1,0:T(8,128)(2,1)S(1)} %slice.78), channel_id=1, source_target_pairs={{0,64},{16,80},{32,96},{48,112},{64,128},{80,144},{96,160},{112,17... | collective-permute-start | bytes 786440 | tf_op jit(solution)/shard_map/ff_Gr1/ppermute | solution.py:30
  30.7 6.5 %copy-start = (bf16[512,2048]{1,0:T(8,128)(2,1)S(1)}, bf16[512,2048]{1,0:T(8,128)(2,1)}, u32[]{:S(2)}) copy-start(bf16[512,2048]{1,0:T(8,128)(2,1)} %refs_5_.3) | copy-start | bytes 6291460
  30.7 8.1 %collective-permute-start.8 = (bf16[48,2048]{1,0:T(8,128)(2,1)S(1)}, bf16[48,2048]{1,0:T(8,128)(2,1)S(1)}, u32[]{:S(2)}, u32[]{:S(2)}) collective-permute-start(bf16[48,2048]{1,0:T(8,128)(2,1)S(1)} %slice.67), channel_id=1, source_target_pairs={{0,48},{16,0},{32,16},{48,32},{64,112},{80,64},{96,80},{112,96},{1... | collective-permute-start | bytes 589832 | tf_op jit(solution)/shard_map/ff_Zr3/ppermute | solution.py:30
  32.2 12.1 %collective-permute-start.7 = (bf16[48,2048]{1,0:T(8,128)(2,1)S(1)}, bf16[48,2048]{1,0:T(8,128)(2,1)S(1)}, u32[]{:S(2)}, u32[]{:S(2)}) collective-permute-start(bf16[48,2048]{1,0:T(8,128)(2,1)S(1)} %slice.66), channel_id=1, source_target_pairs={{0,16},{16,32},{32,48},{48,0},{64,80},{80,96},{96,112},{112,64},{1... | collective-permute-start | bytes 589832 | tf_op jit(solution)/shard_map/ff_Zr1/ppermute | solution.py:30
  33.7 13.4 %collective-permute-start.10 = (bf16[2,128,512]{2,1,0:T(8,128)(2,1)S(1)}, bf16[2,128,512]{2,1,0:T(8,128)(2,1)S(1)}, u32[]{:S(2)}, u32[]{:S(2)}) collective-permute-start(bf16[2,128,512]{2,1,0:T(8,128)(2,1)S(1)} %pad_maximum_fusion.8), channel_id=1, source_target_pairs={{0,2},{1,3},{2,0},{3,1},{4,6},{5,7},{6,4},{7,5},{8,10},{9,11},{10,... | collective-permute-start | bytes 786440 | tf_op jit(solution)/shard_map/ff_I1/ppermute | solution.py:45
  34.4 16.9 %collective-permute-start.14 = (bf16[192,2048]{1,0:T(8,128)(2,1)S(1)}, bf16[192,2048]{1,0:T(8,128)(2,1)S(1)}, u32[]{:S(2)}, u32[]{:S(2)}) collective-permute-start(bf16[192,2048]{1,0:T(8,128)(2,1)S(1)} %pad_maximum_fusion.1), channel_id=1, source_target_pairs={{0,192},{16,208},{32,224},{48,240},{64,0},{80,16},{96,32},{112,48}... | collective-permute-start | bytes 2359304 | tf_op jit(solution)/shard_map/ff_F3/ppermute | solution.py:30
  37.1 17.3 %collective-permute-start.12 = (bf16[192,2048]{1,0:T(8,128)(2,1)S(1)}, bf16[192,2048]{1,0:T(8,128)(2,1)S(1)}, u32[]{:S(2)}, u32[]{:S(2)}) collective-permute-start(bf16[192,2048]{1,0:T(8,128)(2,1)S(1)} %pad_maximum_fusion.1), channel_id=1, source_target_pairs={{0,64},{16,80},{32,96},{48,112},{64,128},{80,144},{96,160},{112,17... | collective-permute-start | bytes 2359304 | tf_op jit(solution)/shard_map/ff_F1/ppermute | solution.py:30
  44.3 21.4 %collective-permute-start.17 = (bf16[128,2048]{1,0:T(8,128)(2,1)S(1)}, bf16[128,2048]{1,0:T(8,128)(2,1)S(1)}, u32[]{:S(2)}, u32[]{:S(2)}) collective-permute-start(bf16[128,2048]{1,0:T(8,128)(2,1)S(1)} %pad_maximum_fusion.5.refs_0_.refs_12_), channel_id=1, source_target_pairs={{0,48},{16,0},{32,16},{48,32},{64,112},{80,64},{96,80},{112,96},{1... | collective-permute-start | bytes 1572872 | tf_op jit(solution)/shard_map/ff_X3/ppermute | solution.py:30
  44.3 25.9 %collective-permute-start.16 = (bf16[128,2048]{1,0:T(8,128)(2,1)S(1)}, bf16[128,2048]{1,0:T(8,128)(2,1)S(1)}, u32[]{:S(2)}, u32[]{:S(2)}) collective-permute-start(bf16[128,2048]{1,0:T(8,128)(2,1)S(1)} %pad_maximum_fusion.5.refs_0_.refs_12_), channel_id=1, source_target_pairs={{0,16},{16,32},{32,48},{48,0},{64,80},{80,96},{96,112},{112,64},{1... | collective-permute-start | bytes 1572872 | tf_op jit(solution)/shard_map/ff_X1/ppermute | solution.py:30
  47.2 23.1 %collective-permute-start.11 = (bf16[4,128,512]{2,1,0:T(8,128)(2,1)S(1)}, bf16[4,128,512]{2,1,0:T(8,128)(2,1)S(1)}, u32[]{:S(2)}, u32[]{:S(2)}) collective-permute-start(bf16[4,128,512]{2,1,0:T(8,128)(2,1)S(1)} %pad_maximum_fusion.6), channel_id=1, source_target_pairs={{0,4},{1,5},{2,6},{3,7},{4,0},{5,1},{6,2},{7,3},{8,12},{9,13},{10,... | collective-permute-start | bytes 1572872 | tf_op jit(solution)/shard_map/ff_I2/ppermute | solution.py:45
  54.7 23.0 %collective-permute-start.15 = (bf16[192,2048]{1,0:T(8,128)(2,1)S(1)}, bf16[192,2048]{1,0:T(8,128)(2,1)S(1)}, u32[]{:S(2)}, u32[]{:S(2)}) collective-permute-start(bf16[192,2048]{1,0:T(8,128)(2,1)S(1)} %get-tuple-element.100), channel_id=1, source_target_pairs={{0,192},{16,208},{32,224},{48,240},{64,0},{80,16},{96,32},{112,48}... | collective-permute-start | bytes 2359304 | tf_op jit(solution)/shard_map/ff_P3/ppermute | solution.py:30
  55.1 24.8 %collective-permute-start.13 = (bf16[192,2048]{1,0:T(8,128)(2,1)S(1)}, bf16[192,2048]{1,0:T(8,128)(2,1)S(1)}, u32[]{:S(2)}, u32[]{:S(2)}) collective-permute-start(bf16[192,2048]{1,0:T(8,128)(2,1)S(1)} %get-tuple-element.101), channel_id=1, source_target_pairs={{0,64},{16,80},{32,96},{48,112},{64,128},{80,144},{96,160},{112,17... | collective-permute-start | bytes 2359304 | tf_op jit(solution)/shard_map/ff_P1/ppermute | solution.py:30
  65.7 14.2 %collective-permute-start.9 = (bf16[96,2048]{1,0:T(8,128)(2,1)S(1)}, bf16[96,2048]{1,0:T(8,128)(2,1)S(1)}, u32[]{:S(2)}, u32[]{:S(2)}) collective-permute-start(bf16[96,2048]{1,0:T(8,128)(2,1)S(1)} %constant_dynamic-update-slice_fusion.refs_2_.refs_6_), channel_id=1, source_target_pairs={{0,128},{16,144},{32,160},{48,176},{64,192},{80,208},{96,224},{112... | collective-permute-start | bytes 1179656 | tf_op jit(solution)/shard_map/ff_P2/ppermute | solution.py:30
  70.2 10.1 %collective-permute-start.19 = (bf16[64,2048]{1,0:T(8,128)(2,1)S(1)}, bf16[64,2048]{1,0:T(8,128)(2,1)S(1)}, u32[]{:S(2)}, u32[]{:S(2)}) collective-permute-start(bf16[64,2048]{1,0:T(8,128)(2,1)S(1)} %slice.75), channel_id=1, source_target_pairs={{0,48},{16,0},{32,16},{48,32},{64,112},{80,64},{96,80},{112,96},{1... | collective-permute-start | bytes 786440 | tf_op jit(solution)/shard_map/ff_Xr3/ppermute | solution.py:30
  70.3 14.2 %collective-permute-start.18 = (bf16[64,2048]{1,0:T(8,128)(2,1)S(1)}, bf16[64,2048]{1,0:T(8,128)(2,1)S(1)}, u32[]{:S(2)}, u32[]{:S(2)}) collective-permute-start(bf16[64,2048]{1,0:T(8,128)(2,1)S(1)} %slice.74), channel_id=1, source_target_pairs={{0,16},{16,32},{32,48},{48,0},{64,80},{80,96},{96,112},{112,64},{1... | collective-permute-start | bytes 786440 | tf_op jit(solution)/shard_map/ff_Xr1/ppermute | solution.py:30
  79.9 7.1 %collective-permute-start.21 = (bf16[8,128,512]{2,1,0:T(8,128)(2,1)S(1)}, bf16[8,128,512]{2,1,0:T(8,128)(2,1)S(1)}, u32[]{:S(2)}, u32[]{:S(2)}) collective-permute-start(bf16[8,128,512]{2,1,0:T(8,128)(2,1)S(1)} %pad_maximum_fusion.own_ref), channel_id=1, source_target_pairs={{0,1},{1,0},{2,3},{3,2},{4,5},{5,4},{6,7},{7,6},{8,9},{9,8},{10,11... | collective-permute-start | bytes 3145736 | tf_op jit(solution)/shard_map/ff_Ic/ppermute | solution.py:39
  86.8 2.7 %collective-permute-start.20 = (bf16[8,128,512]{2,1,0:T(8,128)(2,1)S(1)}, bf16[8,128,512]{2,1,0:T(8,128)(2,1)S(1)}, u32[]{:S(2)}, u32[]{:S(2)}) collective-permute-start(bf16[8,128,512]{2,1,0:T(8,128)(2,1)S(1)} %get-tuple-element.77), channel_id=1, source_target_pairs={{0,1},{1,0},{2,3},{3,2},{4,5},{5,4},{6,7},{7,6},{8,9},{9,8},{10,11... | collective-permute-start | bytes 3145736 | tf_op jit(solution)/shard_map/ff_Rc/ppermute | solution.py:39
  90.2 11.7 %collective-permute-start.22 = (bf16[2,128,512]{2,1,0:T(8,128)(2,1)S(1)}, bf16[2,128,512]{2,1,0:T(8,128)(2,1)S(1)}, u32[]{:S(2)}, u32[]{:S(2)}) collective-permute-start(bf16[2,128,512]{2,1,0:T(8,128)(2,1)S(1)} %get-tuple-element.84), channel_id=1, source_target_pairs={{0,2},{1,3},{2,4},{3,5},{4,6},{5,7},{6,0},{7,1},{8,10},{9,11},{10,... | collective-permute-start | bytes 786440 | tf_op jit(solution)/shard_map/ff_Ry1/ppermute | solution.py:39
  90.8 11.1 %collective-permute-start.23 = (bf16[2,128,512]{2,1,0:T(8,128)(2,1)S(1)}, bf16[2,128,512]{2,1,0:T(8,128)(2,1)S(1)}, u32[]{:S(2)}, u32[]{:S(2)}) collective-permute-start(bf16[2,128,512]{2,1,0:T(8,128)(2,1)S(1)} %get-tuple-element.85), channel_id=1, source_target_pairs={{0,6},{1,7},{2,0},{3,1},{4,2},{5,3},{6,4},{7,5},{8,14},{9,15},{10,... | collective-permute-start | bytes 786440 | tf_op jit(solution)/shard_map/ff_Ry3/ppermute | solution.py:39
  92.3 13.7 %collective-permute-start.24 = (bf16[2,128,512]{2,1,0:T(8,128)(2,1)S(1)}, bf16[2,128,512]{2,1,0:T(8,128)(2,1)S(1)}, u32[]{:S(2)}, u32[]{:S(2)}) collective-permute-start(bf16[2,128,512]{2,1,0:T(8,128)(2,1)S(1)} %get-tuple-element.86), channel_id=1, source_target_pairs={{0,4},{1,5},{2,6},{3,7},{4,0},{5,1},{6,2},{7,3},{8,12},{9,13},{10,... | collective-permute-start | bytes 786440 | tf_op jit(solution)/shard_map/ff_Ry2/ppermute | solution.py:39
  106.8 5.1 %collective-permute-start.25 = (bf16[128,512]{1,0:T(8,128)(2,1)S(1)}, bf16[128,512]{1,0:T(8,128)(2,1)S(1)}, u32[]{:S(2)}, u32[]{:S(2)}) collective-permute-start(bf16[128,512]{1,0:T(8,128)(2,1)S(1)} %get-tuple-element.94), channel_id=1, source_target_pairs={{0,8},{1,9},{2,10},{3,11},{4,12},{5,13},{6,14},{7,15},{8,0},{9,1},... | collective-permute-start | bytes 393224 | tf_op jit(solution)/shard_map/ff_Rl/ppermute | solution.py:39
